TPU v7x, 32 devices: a whole 2x2x4 slice. The times are simulated.
32 devices in a mesh: seq: 8 (over z, core), fsdp: 4 (over y, x).
Axes of the slice: x: 2, y: 2, z: 4, core: 2. Of those that a mesh axis runs over, the one named last changes fastest.
Arguments:
- tokens: bfloat16 [4, 1024, 1536], P('fsdp', 'seq'), may hold values from -6 to 6
- cotangent: bfloat16 [4, 1024, 1536], P('fsdp', 'seq'), may hold values from -6 to 6
- norm_gain: bfloat16 [2, 1536], P(None, ('seq', 'fsdp')), may hold values from 0.5 to 1.5
- in_weight: bfloat16 [2, 1536, 6448], P(None, ('seq', 'fsdp')), may hold values from -0.15625 to 0.15625
- conv_kernel: bfloat16 [2, 4, 3328], P(None, None, ('seq', 'fsdp')), may hold values from -3 to 3
- conv_shift: bfloat16 [2, 3328], P(None, ('seq', 'fsdp')), may hold values from -0.5 to 0.5
- dt_bias: float32 [2, 48], P(None, 'seq'), may hold values from -8 to -2.5
- a_log: float32 [2, 48], P(None, 'seq'), may hold values from 0 to 2.5
- skip_gain: float32 [2, 48], P(None, 'seq'), may hold values from 0.5 to 1.5
- gate_gain: bfloat16 [2, 3072], P(None, ('seq', 'fsdp')), may hold values from 0.5 to 1.5
- out_weight: bfloat16 [2, 3072, 1536], P(None, ('seq', 'fsdp')), may hold values from -0.109375 to 0.109375
Outputs:
- out: bfloat16 [4, 1024, 1536], P('fsdp', 'seq')
- grad_tokens: float32 [4, 1024, 1536], P('fsdp', 'seq')
- grad_norm_gain: float32 [2, 1536], P(None, ('seq', 'fsdp'))
- grad_in_weight: float32 [2, 1536, 6448], P(None, ('seq', 'fsdp'))
- grad_conv_kernel: float32 [2, 4, 3328], P(None, None, ('seq', 'fsdp'))
- grad_conv_shift: float32 [2, 3328], P(None, ('seq', 'fsdp'))
- grad_dt_bias: float32 [2, 48], P(None, 'seq')
- grad_a_log: float32 [2, 48], P(None, 'seq')
- grad_skip_gain: float32 [2, 48], P(None, 'seq')
- grad_gate_gain: float32 [2, 3072], P(None, ('seq', 'fsdp'))
- grad_out_weight: float32 [2, 3072, 1536], P(None, ('seq', 'fsdp'))
All inputs are finite; a program needn't handle non-finite values.
Results may differ from a plain program's by a relative error of at most 0.02.
Values may be sent and summed in bfloat16 or wider, within the bound.
No kernel may reach another device: no remote copies, remote signals or barrier semaphores. Data moves between devices by JAX's collectives and lax.ppermute only.
A program may use at most 384 MiB of HBM per device.

v0:
```python
import jax
import jax.numpy as jnp
from jax import lax
from jax.sharding import PartitionSpec as P

HD = 64
NSTATE = 128
STRETCH = 256
DI = 3072


eps = 1e-05


def rms_scale(values, gain_row):
    return values * lax.rsqrt(jnp.mean(values * values, axis=-1, keepdims=True) + eps) * gain_row


def causal_conv(values, kernel, offset):
    width_conv = kernel.shape[0]
    padded = jnp.concatenate(
        [jnp.zeros((width_conv - 1, values.shape[1]), jnp.float32), values], axis=0
    )
    result = offset
    for lag_at in range(width_conv):
        result = result + kernel[lag_at] * padded[lag_at : lag_at + values.shape[0]]
    return result


def exact_product(form, left, right):
    return jnp.einsum(
        form, left, right, precision=lax.Precision.HIGHEST, preferred_element_type=jnp.float32
    )


def order_mask(extent, strict):
    row_ids = lax.broadcasted_iota(jnp.int32, (extent, extent), 0)
    col_ids = lax.broadcasted_iota(jnp.int32, (extent, extent), 1)
    if strict:
        return (row_ids > col_ids).astype(jnp.float32)
    return (row_ids >= col_ids).astype(jnp.float32)


def state_space(head_in, step_sizes, log_decay, b_in, c_in):
    length, head_count, head_dim = head_in.shape
    stretch_count = length // STRETCH
    lower_mask = order_mask(STRETCH, False)
    logs_t = log_decay.reshape(stretch_count, STRETCH, head_count).transpose(0, 2, 1)
    cumulative = exact_product("chj,ij->chi", logs_t, lower_mask)
    gap_log = cumulative[:, :, :, None] - cumulative[:, :, None, :]
    keep_mask = lower_mask[None, None] > 0
    weights = jnp.where(keep_mask, jnp.exp(jnp.where(keep_mask, gap_log, 0.0)), 0.0)
    b_stretches = b_in.reshape(stretch_count, STRETCH, b_in.shape[1])
    c_stretches = c_in.reshape(stretch_count, STRETCH, c_in.shape[1])
    scores = exact_product("cin,cjn->cij", c_stretches, b_stretches)
    steps_t = step_sizes.reshape(stretch_count, STRETCH, head_count).transpose(0, 2, 1)
    inputs_t = head_in.reshape(stretch_count, STRETCH, head_count, head_dim).transpose(0, 2, 1, 3)
    weighted = inputs_t * steps_t[..., None]
    within = exact_product("chij,chjp->chip", scores[:, None] * weights, weighted)
    to_end = jnp.exp(cumulative[..., -1:] - cumulative)
    stretch_states = exact_product("chjp,cjn->chpn", weighted * to_end[..., None], b_stretches)
    totals = cumulative[..., -1]
    prefix = exact_product("ab,bh->ah", order_mask(stretch_count, False), totals)
    span_log = (prefix - totals).T[:, :, None] - prefix.T[:, None, :]
    strict = order_mask(stretch_count, True)[None] > 0
    carry_weights = jnp.where(strict, jnp.exp(jnp.where(strict, span_log, 0.0)), 0.0)
    entering = exact_product("hab,bhpn->ahpn", carry_weights, stretch_states)
    carried = jnp.exp(cumulative)[..., None] * exact_product(
        "cin,chpn->chip", c_stretches, entering
    )
    return (within + carried).transpose(0, 2, 1, 3).reshape(length, head_count, head_dim)


def mixer(inputs):
    (
        gate_part,
        input_part,
        step_part,
        shared_part,
        kernel_x,
        offset_x,
        kernel_bc,
        offset_bc,
        bias_row,
        decay_row,
        skip_row,
    ) = inputs
    length = input_part.shape[0]
    head_count = step_part.shape[1]
    state_width = shared_part.shape[1] // 2
    convolved = jax.nn.silu(causal_conv(input_part, kernel_x, offset_x))
    shared_out = jax.nn.silu(causal_conv(shared_part, kernel_bc, offset_bc))
    step_sizes = jax.nn.softplus(step_part + bias_row)
    log_decay = -step_sizes * jnp.exp(decay_row)
    head_in = convolved.reshape(length, head_count, convolved.shape[1] // head_count)
    result = state_space(
        head_in, step_sizes, log_decay, shared_out[:, :state_width], shared_out[:, state_width:]
    )
    result = result + skip_row[:, None] * head_in
    return result.reshape(length, convolved.shape[1]) * jax.nn.silu(gate_part)


def layer_forward(residual, weights, head_params, start_at):
    normed, norm_pull = jax.vjp(rms_scale, residual, weights[0].astype(jnp.float32))
    normed_low = normed.astype(jnp.bfloat16)
    projected = jnp.dot(normed_low, weights[1], preferred_element_type=jnp.float32).astype(
        jnp.bfloat16
    )
    received = (
        lax.all_to_all(projected[None, :, :DI], "seq", split_axis=2, concat_axis=1, tiled=True),
        lax.all_to_all(
            projected[None, :, DI : 2 * DI], "seq", split_axis=2, concat_axis=1, tiled=True
        ),
        lax.all_to_all(
            projected[None, :, 2 * DI + 2 * NSTATE :],
            "seq",
            split_axis=2,
            concat_axis=1,
            tiled=True,
        ),
    )
    shared_all = lax.all_gather(
        projected[None, :, 2 * DI : 2 * DI + 2 * NSTATE], "seq", axis=1, tiled=True
    )
    kernel_full = weights[2].astype(jnp.float32)
    shift_full = weights[3].astype(jnp.float32)
    local_width = received[1].shape[2]
    inputs = (
        received[0][0].astype(jnp.float32),
        received[1][0].astype(jnp.float32),
        received[2][0].astype(jnp.float32),
        shared_all[0].astype(jnp.float32),
        lax.dynamic_slice_in_dim(kernel_full, start_at, local_width, 1),
        lax.dynamic_slice_in_dim(shift_full, start_at, local_width, 0),
        kernel_full[:, DI:],
        shift_full[DI:],
        head_params[0],
        head_params[1],
        head_params[2],
    )
    gated_out = mixer(inputs).astype(jnp.bfloat16)
    gathered_back = lax.all_to_all(gated_out[None], "seq", split_axis=1, concat_axis=2, tiled=True)[
        0
    ]
    scaled, gate_pull = jax.vjp(
        rms_scale, gathered_back.astype(jnp.float32), weights[4].astype(jnp.float32)
    )
    scaled_low = scaled.astype(jnp.bfloat16)
    branch = jnp.dot(scaled_low, weights[5], preferred_element_type=jnp.float32)
    return (residual + branch, (norm_pull, normed_low, inputs, gate_pull, scaled_low))


def layer_backward(grad_residual, weights, record, start_at):
    norm_pull, normed_low, inputs, gate_pull, scaled_low = record
    grad_low = grad_residual.astype(jnp.bfloat16)
    grad_out = lax.dot_general(
        scaled_low, grad_low, (((0,), (0,)), ((), ())), preferred_element_type=jnp.float32
    )
    grad_scaled = lax.dot_general(
        grad_low, weights[5], (((1,), (1,)), ((), ())), preferred_element_type=jnp.float32
    )
    grad_gated, grad_gate_gain = gate_pull(grad_scaled)
    grad_heads = lax.all_to_all(
        grad_gated.astype(jnp.bfloat16)[None], "seq", split_axis=2, concat_axis=1, tiled=True
    )[0]
    _, mixer_pull = jax.vjp(mixer, inputs)
    (grad_inputs,) = mixer_pull(grad_heads.astype(jnp.float32))
    (
        grad_gate_in,
        grad_input,
        grad_step,
        grad_shared,
        grad_kernel_x,
        grad_offset_x,
        grad_kernel_bc,
        grad_offset_bc,
        grad_bias,
        grad_decay,
        grad_skip,
    ) = grad_inputs
    sent_back = (
        lax.all_to_all(
            grad_gate_in.astype(jnp.bfloat16)[None], "seq", split_axis=1, concat_axis=2, tiled=True
        ),
        lax.all_to_all(
            grad_input.astype(jnp.bfloat16)[None], "seq", split_axis=1, concat_axis=2, tiled=True
        ),
        lax.all_to_all(
            grad_step.astype(jnp.bfloat16)[None], "seq", split_axis=1, concat_axis=2, tiled=True
        ),
    )
    shared_sum = (
        lax.psum_scatter(
            grad_shared[None].astype(jnp.bfloat16), "seq", scatter_dimension=1, tiled=True
        )
        .astype(jnp.float32)[0]
        .astype(jnp.bfloat16)
    )
    grad_proj = jnp.concatenate(
        [sent_back[0][0], sent_back[1][0], shared_sum, sent_back[2][0]], axis=1
    )
    grad_in = lax.dot_general(
        normed_low, grad_proj, (((0,), (0,)), ((), ())), preferred_element_type=jnp.float32
    )
    grad_normed = lax.dot_general(
        grad_proj, weights[1], (((1,), (1,)), ((), ())), preferred_element_type=jnp.float32
    )
    grad_before, grad_norm_gain = norm_pull(grad_normed)
    kernel_grad = jnp.concatenate(
        [jnp.zeros((grad_kernel_bc.shape[0], DI), jnp.float32), grad_kernel_bc], axis=1
    )
    kernel_grad = kernel_grad + lax.dynamic_update_slice_in_dim(
        jnp.zeros_like(kernel_grad), grad_kernel_x, start_at, 1
    )
    shift_grad = jnp.concatenate([jnp.zeros((DI,), jnp.float32), grad_offset_bc], axis=0)
    shift_grad = shift_grad + lax.dynamic_update_slice_in_dim(
        jnp.zeros_like(shift_grad), grad_offset_x, start_at, 0
    )
    partial_grads = (grad_norm_gain, grad_in, kernel_grad, shift_grad, grad_gate_gain, grad_out)
    head_sums = lax.psum((grad_bias, grad_decay, grad_skip), "fsdp")
    return (grad_residual + grad_before, partial_grads, head_sums)


def local(
    tokens,
    cotangent,
    norm_gain,
    in_weight,
    conv_kernel,
    conv_shift,
    dt_bias,
    a_log,
    skip_gain,
    gate_gain,
    out_weight,
):
    layer_count = in_weight.shape[0]
    local_width = dt_bias.shape[1] * HD
    start_at = lax.axis_index("seq") * local_width
    residual = tokens[0].astype(jnp.float32)
    records = []
    for current in range(layer_count):
        weights = (
            lax.all_gather(norm_gain[current], ("seq", "fsdp"), axis=0, tiled=True),
            lax.all_gather(in_weight[current], ("seq", "fsdp"), axis=0, tiled=True),
            lax.all_gather(conv_kernel[current], ("seq", "fsdp"), axis=1, tiled=True),
            lax.all_gather(conv_shift[current], ("seq", "fsdp"), axis=0, tiled=True),
            lax.all_gather(gate_gain[current], ("seq", "fsdp"), axis=0, tiled=True),
            lax.all_gather(out_weight[current], ("seq", "fsdp"), axis=0, tiled=True),
        )
        residual, record = layer_forward(
            residual, weights, (dt_bias[current], a_log[current], skip_gain[current]), start_at
        )
        kept_weights = None
        records.append((record, kept_weights))
    grad_residual = cotangent[0].astype(jnp.float32)
    reduced_all = []
    head_all = []
    for current in reversed(range(layer_count)):
        record, kept_weights = records[current]
        weights = (
            lax.all_gather(norm_gain[current], ("seq", "fsdp"), axis=0, tiled=True),
            lax.all_gather(in_weight[current], ("seq", "fsdp"), axis=0, tiled=True),
            lax.all_gather(conv_kernel[current], ("seq", "fsdp"), axis=1, tiled=True),
            lax.all_gather(conv_shift[current], ("seq", "fsdp"), axis=0, tiled=True),
            lax.all_gather(gate_gain[current], ("seq", "fsdp"), axis=0, tiled=True),
            lax.all_gather(out_weight[current], ("seq", "fsdp"), axis=0, tiled=True),
        )
        grad_residual, partial_grads, head_sums = layer_backward(
            grad_residual, weights, record, start_at
        )
        halfway = (
            lax.psum_scatter(
                partial_grads[0].astype(jnp.bfloat16), "seq", scatter_dimension=0, tiled=True
            ).astype(jnp.float32),
            lax.psum_scatter(
                partial_grads[1].astype(jnp.bfloat16), "seq", scatter_dimension=0, tiled=True
            ).astype(jnp.float32),
            lax.psum_scatter(
                partial_grads[2].astype(jnp.bfloat16), "seq", scatter_dimension=1, tiled=True
            ).astype(jnp.float32),
            lax.psum_scatter(
                partial_grads[3].astype(jnp.bfloat16), "seq", scatter_dimension=0, tiled=True
            ).astype(jnp.float32),
            lax.psum_scatter(
                partial_grads[4].astype(jnp.bfloat16), "seq", scatter_dimension=0, tiled=True
            ).astype(jnp.float32),
            lax.psum_scatter(
                partial_grads[5].astype(jnp.bfloat16), "seq", scatter_dimension=0, tiled=True
            ).astype(jnp.float32),
        )
        reduced = (
            lax.psum_scatter(
                halfway[0].astype(jnp.bfloat16), "fsdp", scatter_dimension=0, tiled=True
            ).astype(jnp.float32),
            lax.psum_scatter(
                halfway[1].astype(jnp.bfloat16), "fsdp", scatter_dimension=0, tiled=True
            ).astype(jnp.float32),
            lax.psum_scatter(
                halfway[2].astype(jnp.bfloat16), "fsdp", scatter_dimension=1, tiled=True
            ).astype(jnp.float32),
            lax.psum_scatter(
                halfway[3].astype(jnp.bfloat16), "fsdp", scatter_dimension=0, tiled=True
            ).astype(jnp.float32),
            lax.psum_scatter(
                halfway[4].astype(jnp.bfloat16), "fsdp", scatter_dimension=0, tiled=True
            ).astype(jnp.float32),
            lax.psum_scatter(
                halfway[5].astype(jnp.bfloat16), "fsdp", scatter_dimension=0, tiled=True
            ).astype(jnp.float32),
        )
        reduced_all.insert(0, reduced)
        head_all.insert(0, head_sums)
    stacked = [jnp.stack([entry[member] for entry in reduced_all]) for member in range(6)]
    return (
        residual.astype(jnp.bfloat16)[None],
        grad_residual[None],
        stacked[0],
        stacked[1],
        stacked[2],
        stacked[3],
        jnp.stack([entry[0] for entry in head_all]),
        jnp.stack([entry[1] for entry in head_all]),
        jnp.stack([entry[2] for entry in head_all]),
        stacked[4],
        stacked[5],
    )


def solution(mesh):
    placed = (
        P("fsdp", "seq", None),
        P("fsdp", "seq", None),
        P(None, ("seq", "fsdp")),
        P(None, ("seq", "fsdp"), None),
        P(None, None, ("seq", "fsdp")),
        P(None, ("seq", "fsdp")),
        P(None, "seq"),
        P(None, "seq"),
        P(None, "seq"),
        P(None, ("seq", "fsdp")),
        P(None, ("seq", "fsdp"), None),
    )
    return jax.shard_map(
        local,
        mesh=mesh,
        in_specs=placed,
        out_specs=(
            P("fsdp", "seq", None),
            P("fsdp", "seq", None),
            P(None, ("seq", "fsdp")),
            P(None, ("seq", "fsdp"), None),
            P(None, None, ("seq", "fsdp")),
            P(None, ("seq", "fsdp")),
            P(None, "seq"),
            P(None, "seq"),
            P(None, "seq"),
            P(None, ("seq", "fsdp")),
            P(None, ("seq", "fsdp"), None),
        ),
        check_vma=False,
    )
```

profile of v0, /device:TPU:0, one launch (start us, length us, event | category | flops | bytes accessed | tf_op | source)
XLA Modules:
  0.0 2036.6 jit_solution(14388185359943328303)
XLA Ops:
  14.2 44.0 %all-reduce.71 = (bf16[1536]{0:T(1024)(128)(2,1)S(1)}, bf16[3328]{0:T(1024)(128)(2,1)S(1)}, bf16[3072]{0:T(1024)(128)(2,1)}, bf16[1536]{0:T(1024)(128)(2,1)}, bf...) all-reduce(bf16[1536]{0:T(1024)(128)(2,1)S(1)} %dynamic-update-slic, ...), channel_id=4, replica_groups=mesh['seq'=8,'fsdp'=4] {'seq','fsdp'}, use_global_device_ids=true, to_apply=%add.49 | all-reduce | flops 15872 | bytes 63488
  60.1 94.4 %all-gather.1 = bf16[1,4,3328]{1,0,2:T(2,128)(2,1)S(1)} all-gather(bf16[1,4,104]{1,0,2:T(2,128)(2,1)S(1)} %copy.788), channel_id=3, replica_groups=mesh['seq'=8,'fsdp'=4] {'seq','fsdp'}, dimensions={2}, use_global_device_ids=true | all-gather | bytes 27456 | tf_op jit(solution)/shard_map/all_gather | solution.py:246
  169.9 12.0 fusion.16
  187.2 14.9 all-gather.4
  212.7 12.5 copy.1017
  225.3 17.9 reduce.52
  250.9 17.1 reduce.53
  276.0 22.9 %all-to-all-done.1 = bf16[8,2,24576]{2,1,0:T(2,128)(2,1)S(1)} async-done(((bf16[8,2,24576]{2,1,0:T(2,128)(2,1)}), bf16[8,2,24576]{2,1,0:T(2,128)(2,1)S(1)}, u32[]{:S(2)}, u32[]{:S(2)}) %all-to-all-start.1) | async-done | bytes 786464 | tf_op jit(solution)/shard_map/all_to_all | solution.py:111
  366.1 105.4 %all-gather.8 = bf16[1,4,3328]{1,0,2:T(2,128)(2,1)S(1)} all-gather(bf16[1,4,104]{1,0,2:T(2,128)(2,1)S(1)} %copy.789), channel_id=10, replica_groups=mesh['seq'=8,'fsdp'=4] {'seq','fsdp'}, dimensions={2}, use_global_device_ids=true | all-gather | bytes 27456 | tf_op jit(solution)/shard_map/all_gather | solution.py:246
  492.4 12.1 fusion.19
  507.0 11.7 all-to-all-start.4
  518.7 14.2 all-gather.11
  547.8 13.0 copy.1014
  560.8 17.8 reduce.56
  586.4 17.8 reduce.57
  611.9 19.9 all-to-all-done.5
  706.3 19.0 all-to-all-done.7
  748.5 18.9 reduce.59
  979.3 23.0 %reduce-scatter.39.cloned.1.call-done = bf16[128,256]{1,0:T(8,128)(2,1)} async-done(((bf16[1024,256]{1,0:T(8,128)(2,1)}), bf16[128,256]{1,0:T(8,128)(2,1)}) %reduce-scatter.39.cloned.1.call-update) | async-done | bytes 65552
  1021.1 13.3 multiply_reduce_fusion.25
  1047.8 18.0 reduce.63
  1265.3 26.2 %all-to-all-done.14 = bf16[8,2,24576]{2,1,0:T(2,128)(2,1)} async-done(((bf16[8,2,24576]{2,1,0:T(2,128)(2,1)}), bf16[8,2,24576]{2,1,0:T(2,128)(2,1)}, u32[]{:S(2)}, u32[]{:S(2)}) %all-to-all-start.14) | async-done | bytes 786464 | tf_op jit(solution)/shard_map/all_to_all | solution.py:185
  1304.9 13.7 all-to-all-done.13
  1334.9 81.5 %reduce-scatter.31.cloned.1.call-done = bf16[384,1536]{1,0:T(8,128)(2,1)} async-done(((bf16[3072,1536]{1,0:T(8,128)(2,1)}), bf16[384,1536]{1,0:T(8,128)(2,1)}) %reduce-scatter.31.cloned.1.call-update) | async-done | bytes 1179664 | tf_op jit(solution)/shard_map/reduce_scatter | solution.py:288
  1416.5 199.7 %reduce-scatter.29.cloned.1.call-done = bf16[192,6448]{1,0:T(8,128)(2,1)} async-done(((bf16[1536,6448]{1,0:T(8,128)(2,1)}), bf16[192,6448]{1,0:T(8,128)(2,1)}) %reduce-scatter.29.cloned.1.call-update) | async-done | bytes 2476048 | tf_op jit(solution)/shard_map/reduce_scatter | solution.py:276
  1622.9 193.0 %reduce-scatter.27.cloned.1.call-done = bf16[192,6448]{1,0:T(8,128)(2,1)} async-done(((bf16[1536,6448]{1,0:T(8,128)(2,1)}), bf16[192,6448]{1,0:T(8,128)(2,1)}) %reduce-scatter.27.cloned.1.call-update) | async-done | bytes 2476048 | tf_op jit(solution)/shard_map/reduce_scatter | solution.py:276
  1822.9 26.2 %reduce-scatter.45.cloned.1.call-done = bf16[416,4]{1,0:T(8,128)(2,1)} async-done(((bf16[3328,4]{1,0:T(8,128)(2,1)}), bf16[416,4]{1,0:T(8,128)(2,1)}) %reduce-scatter.45.cloned.1.call-update) | async-done | bytes 3344
  1864.5 17.2 reduce-scatter.43.cloned.1.call-done
  1893.1 26.4 %all-reduce.72 = (bf16[1536]{0:T(1024)(128)(2,1)S(1)}, bf16[1536]{0:T(1024)(128)(2,1)S(1)}, bf16[3328]{0:T(1024)(128)(2,1)S(1)}, bf16[3328]{0:T(1024)(128)(2,1)S...) all-reduce(bf16[1536]{0:T(1024)(128)(2,1)S(1)} %copy-done.212, ...), channel_id=20, replica_groups=mesh['seq'=8,'fsdp'=4] {'seq'}, use_global_device_ids=true, to_apply=%region_33.35.clone | all-reduce | flops 15872 | bytes 63488
  1920.0 16.5 all-reduce.73
  1945.0 39.7 %reduce-scatter.49.cloned.1.call-done = bf16[48,6448]{1,0:T(8,128)(2,1)} async-done(((bf16[192,6448]{1,0:T(8,128)(2,1)}), bf16[48,6448]{1,0:T(8,128)(2,1)}) %reduce-scatter.49.cloned.1.call-update) | async-done | bytes 619024
  1984.6 42.1 %reduce-scatter.47.cloned.1.call-done = bf16[48,6448]{1,0:T(8,128)(2,1)} async-done(((bf16[192,6448]{1,0:T(8,128)(2,1)}), bf16[48,6448]{1,0:T(8,128)(2,1)}) %reduce-scatter.47.cloned.1.call-update) | async-done | bytes 619024
  (936 shorter events, 792.9 us)
Async XLA Ops:
  7.2 162.7 %all-gather.19.cloned.1.call-start = ((), (), s32[]{:S(2)}) async-start(), calls=%async_computation.34 | async-start | bytes 20680704 | tf_op jit(solution)/shard_map/all_gather | solution.py:245
  9.7 476.4 %all-gather.21.cloned.1.call-start = ((), (), s32[]{:S(2)}) async-start(), calls=%async_computation.35 | async-start | bytes 9732096 | tf_op jit(solution)/shard_map/all_gather | solution.py:249
  10.7 481.2 %all-gather.23.cloned.1.call-start = ((), (), s32[]{:S(2)}) async-start(), calls=%async_computation.36 | async-start | bytes 20680704 | tf_op jit(solution)/shard_map/all_gather | solution.py:245
  11.4 723.2 %all-gather.25.cloned.1.call-start = ((), (), s32[]{:S(2)}) async-start(), calls=%async_computation.37 | async-start | bytes 9732096 | tf_op jit(solution)/shard_map/all_gather | solution.py:249
  183.9 85.2 %all-to-all-start = ((bf16[8,2,384]{2,1,0:T(2,128)(2,1)}), bf16[8,2,384]{2,1,0:T(2,128)(2,1)S(1)}, u32[]{:S(2)}, u32[]{:S(2)}) async-start(bf16[8,2,384]{2,1,0:T(2,128)(2,1)} %reshape.820), calls=%async_computation | async-start | bytes 24576 | tf_op jit(solution)/shard_map/all_to_all | solution.py:114
  269.0 29.9 %all-to-all-start.1 = ((bf16[8,2,24576]{2,1,0:T(2,128)(2,1)}), bf16[8,2,24576]{2,1,0:T(2,128)(2,1)S(1)}, u32[]{:S(2)}, u32[]{:S(2)}) async-start(bf16[8,2,24576]{2,1,0:T(2,128)(2,1)} %reshape.822), calls=%async_computation.1 | async-start | bytes 1572864 | tf_op jit(solution)/shard_map/all_to_all | solution.py:111
  298.9 43.0 %all-to-all-start.2 = ((bf16[8,2,24576]{2,1,0:T(2,128)(2,1)}), bf16[8,2,24576]{2,1,0:T(2,128)(2,1)}, u32[]{:S(2)}, u32[]{:S(2)}) async-start(bf16[8,2,24576]{2,1,0:T(2,128)(2,1)} %reshape.824), calls=%async_computation.2 | async-start | bytes 1572864 | tf_op jit(solution)/shard_map/all_to_all | solution.py:110
  360.5 120.9 %all-to-all-start.3 = ((bf16[8,2,24576]{2,1,0:T(2,128)(2,1)}), bf16[8,2,24576]{2,1,0:T(2,128)(2,1)}, u32[]{:S(2)}, u32[]{:S(2)}) async-start(bf16[8,2,24576]{2,1,0:T(2,128)(2,1)} %reshape.826), calls=%async_computation.3 | async-start | bytes 1572864 | tf_op jit(solution)/shard_map/all_to_all | solution.py:142
  507.0 100.2 %all-to-all-start.4 = ((bf16[8,2,384]{2,1,0:T(2,128)(2,1)}), bf16[8,2,384]{2,1,0:T(2,128)(2,1)S(1)}, u32[]{:S(2)}, u32[]{:S(2)}) async-start(bf16[8,2,384]{2,1,0:T(2,128)(2,1)} %reshape.828), calls=%async_computation.4 | async-start | bytes 24576 | tf_op jit(solution)/shard_map/all_to_all | solution.py:114
  607.2 24.5 %all-to-all-start.5 = ((bf16[8,2,24576]{2,1,0:T(2,128)(2,1)}), bf16[8,2,24576]{2,1,0:T(2,128)(2,1)S(1)}, u32[]{:S(2)}, u32[]{:S(2)}) async-start(bf16[8,2,24576]{2,1,0:T(2,128)(2,1)} %reshape.830), calls=%async_computation.5 | async-start | bytes 1572864 | tf_op jit(solution)/shard_map/all_to_all | solution.py:111
  632.7 39.1 %all-to-all-start.6 = ((bf16[8,2,24576]{2,1,0:T(2,128)(2,1)}), bf16[8,2,24576]{2,1,0:T(2,128)(2,1)}, u32[]{:S(2)}, u32[]{:S(2)}) async-start(bf16[8,2,24576]{2,1,0:T(2,128)(2,1)} %reshape.832), calls=%async_computation.6 | async-start | bytes 1572864 | tf_op jit(solution)/shard_map/all_to_all | solution.py:110
  698.9 26.5 %all-to-all-start.7 = ((bf16[8,2,24576]{2,1,0:T(2,128)(2,1)}), bf16[8,2,24576]{2,1,0:T(2,128)(2,1)}, u32[]{:S(2)}, u32[]{:S(2)}) async-start(bf16[8,2,24576]{2,1,0:T(2,128)(2,1)} %reshape.834), calls=%async_computation.7 | async-start | bytes 1572864 | tf_op jit(solution)/shard_map/all_to_all | solution.py:142
  770.3 28.0 %all-to-all-start.8 = ((bf16[8,2,24576]{2,1,0:T(2,128)(2,1)}), bf16[8,2,24576]{2,1,0:T(2,128)(2,1)}, u32[]{:S(2)}, u32[]{:S(2)}) async-start(bf16[8,2,24576]{2,1,0:T(2,128)(2,1)} %reshape.836), calls=%async_computation.8 | async-start | bytes 1572864 | tf_op jit(solution)/shard_map/all_to_all | solution.py:163
  870.8 50.1 %all-to-all-start.11 = ((bf16[8,2,384]{2,1,0:T(2,128)(2,1)}), bf16[8,2,384]{2,1,0:T(2,128)(2,1)}, u32[]{:S(2)}, u32[]{:S(2)}) async-start(bf16[8,2,384]{2,1,0:T(2,128)(2,1)} %reshape.838), calls=%async_computation.11 | async-start | bytes 24576 | tf_op jit(solution)/shard_map/all_to_all | solution.py:188
  920.8 37.4 %all-to-all-start.10 = ((bf16[8,2,24576]{2,1,0:T(2,128)(2,1)}), bf16[8,2,24576]{2,1,0:T(2,128)(2,1)}, u32[]{:S(2)}, u32[]{:S(2)}) async-start(bf16[8,2,24576]{2,1,0:T(2,128)(2,1)} %reshape.840), calls=%async_computation.10 | async-start | bytes 1572864 | tf_op jit(solution)/shard_map/all_to_all | solution.py:185
  958.3 52.3 %all-to-all-start.9 = ((bf16[8,2,24576]{2,1,0:T(2,128)(2,1)}), bf16[8,2,24576]{2,1,0:T(2,128)(2,1)}, u32[]{:S(2)}, u32[]{:S(2)}) async-start(bf16[8,2,24576]{2,1,0:T(2,128)(2,1)} %reshape.842), calls=%async_computation.9 | async-start | bytes 1572864 | tf_op jit(solution)/shard_map/all_to_all | solution.py:182
  963.5 38.8 %reduce-scatter.39.cloned.1.call-start = ((), (), s32[]{:S(2)}) async-start(), calls=%async_computation.38 | async-start | bytes 589824
  1068.8 25.2 %all-to-all-start.12 = ((bf16[8,2,24576]{2,1,0:T(2,128)(2,1)}), bf16[8,2,24576]{2,1,0:T(2,128)(2,1)}, u32[]{:S(2)}, u32[]{:S(2)}) async-start(bf16[8,2,24576]{2,1,0:T(2,128)(2,1)} %reshape.844), calls=%async_computation.12 | async-start | bytes 1572864 | tf_op jit(solution)/shard_map/all_to_all | solution.py:163
  1073.1 223.6 %reduce-scatter.41.cloned.1.call-start = ((), (), s32[]{:S(2)}) async-start(), calls=%async_computation.39 | async-start | bytes 589824
  1156.6 177.6 %reduce-scatter.35.cloned.1.call-start = ((), (), s32[]{:S(2)}) async-start(), calls=%async_computation.32 | async-start | bytes 10616832 | tf_op jit(solution)/shard_map/reduce_scatter | solution.py:288
  1168.7 247.7 %reduce-scatter.31.cloned.1.call-start = ((), (), s32[]{:S(2)}) async-start(), calls=%async_computation.30 | async-start | bytes 10616832 | tf_op jit(solution)/shard_map/reduce_scatter | solution.py:288
  1175.7 440.5 %reduce-scatter.29.cloned.1.call-start = ((), (), s32[]{:S(2)}) async-start(), calls=%async_computation.29 | async-start | bytes 22560768 | tf_op jit(solution)/shard_map/reduce_scatter | solution.py:276
  1214.2 37.9 %all-to-all-start.15 = ((bf16[8,2,384]{2,1,0:T(2,128)(2,1)}), bf16[8,2,384]{2,1,0:T(2,128)(2,1)S(1)}, u32[]{:S(2)}, u32[]{:S(2)}) async-start(bf16[8,2,384]{2,1,0:T(2,128)(2,1)} %reshape.846), calls=%async_computation.15 | async-start | bytes 24576 | tf_op jit(solution)/shard_map/all_to_all | solution.py:188
  1252.1 39.4 %all-to-all-start.14 = ((bf16[8,2,24576]{2,1,0:T(2,128)(2,1)}), bf16[8,2,24576]{2,1,0:T(2,128)(2,1)}, u32[]{:S(2)}, u32[]{:S(2)}) async-start(bf16[8,2,24576]{2,1,0:T(2,128)(2,1)} %reshape.848), calls=%async_computation.14 | async-start | bytes 1572864 | tf_op jit(solution)/shard_map/all_to_all | solution.py:185
  1291.5 27.1 %all-to-all-start.13 = ((bf16[8,2,24576]{2,1,0:T(2,128)(2,1)}), bf16[8,2,24576]{2,1,0:T(2,128)(2,1)S(1)}, u32[]{:S(2)}, u32[]{:S(2)}) async-start(bf16[8,2,24576]{2,1,0:T(2,128)(2,1)} %reshape.850), calls=%async_computation.13 | async-start | bytes 1572864 | tf_op jit(solution)/shard_map/all_to_all | solution.py:182
  1295.0 520.8 %reduce-scatter.27.cloned.1.call-start = ((), (), s32[]{:S(2)}) async-start(), calls=%async_computation.28 | async-start | bytes 22560768 | tf_op jit(solution)/shard_map/reduce_scatter | solution.py:276
  1330.4 518.8 %reduce-scatter.45.cloned.1.call-start = ((), (), s32[]{:S(2)}) async-start(), calls=%async_computation.41 | async-start | bytes 958464
  1332.3 549.4 %reduce-scatter.43.cloned.1.call-start = ((), (), s32[]{:S(2)}) async-start(), calls=%async_computation.40 | async-start | bytes 958464
  1334.1 606.4 %reduce-scatter.37.cloned.1.call-start = ((), (), s32[]{:S(2)}) async-start(), calls=%async_computation.33 | async-start | bytes 1474560 | tf_op jit(solution)/shard_map/reduce_scatter | solution.py:308
  1334.9 607.9 %reduce-scatter.33.cloned.1.call-start = ((), (), s32[]{:S(2)}) async-start(), calls=%async_computation.31 | async-start | bytes 1474560 | tf_op jit(solution)/shard_map/reduce_scatter | solution.py:308
  1416.4 568.2 %reduce-scatter.49.cloned.1.call-start = ((), (), s32[]{:S(2)}) async-start(), calls=%async_computation.43 | async-start | bytes 3133440
  1616.3 410.4 %reduce-scatter.47.cloned.1.call-start = ((), (), s32[]{:S(2)}) async-start(), calls=%async_computation.42 | async-start | bytes 3133440
  (233 other events, 4260.5 us)
Sparse Core Ops, SparseCore 0:
  11.5 158.3 all-gather.18
  172.8 81.3 all-gather.20
  257.1 168.6 all-gather.22
  429.1 87.9 all-gather.24
  971.6 30.6 reduce-scatter.38
  1156.7 29.6 reduce-scatter.40
  1188.7 110.4 reduce-scatter.34
  1301.5 114.8 reduce-scatter.30
  1418.8 197.4 reduce-scatter.28
  1618.4 197.4 reduce-scatter.26
  1818.7 30.3 reduce-scatter.44
  1851.9 29.6 reduce-scatter.42
  1884.6 26.7 reduce-scatter.36
  1914.1 28.6 reduce-scatter.32
  1945.7 38.8 reduce-scatter.48
  1987.8 38.8 reduce-scatter.46
where the time goes:
time: 2050 us; the launch traced here: 2040 us
  waiting for transfers between devices  748 us (36%)
  local copies, waits for them, and re-layouts  342 us (17%)
  blocking collectives  325 us (16%)
  matrix products  276 us (13%)
  other arithmetic  245 us (12%)
  starting transfers between devices  78 us (4%)
  between operations  21.6 us (1%)
    reduce_scatter x2, waiting for transfers between devices, local(): lax.psum_scatter(partial_grads[1].astype(jnp.bfloat16), 'seq', scatter_di...  393 us
    all_gather x2, blocking collectives, local(): lax.all_gather(conv_kernel[current], ('seq', 'fsdp'), axis=1, tiled=True)  200 us
    dot_general x50, matrix products, exact_product(): jnp.einsum(form, left, right, precision=lax.Precision.HIGHEST, preferred_...  168 us
    unnamed x16, other arithmetic  154 us
    unnamed x22, waiting for transfers between devices  150 us
    unnamed x550, local copies, waits for them, and re-layouts  139 us
    unnamed x3, blocking collectives  87 us
    reduce_scatter x2, waiting for transfers between devices, local(): lax.psum_scatter(partial_grads[5].astype(jnp.bfloat16), 'seq', scatter_di...  81.5 us
  transfers between devices with their start and end apart: 32, of which 17 were waited for; matrix products, arithmetic and copies ran while one was open for 30% of the time, Pallas kernels for 0%

commit v1 on v0

v1 whole, which is shorter than its diff:
```python
import functools

import jax
import jax.numpy as jnp
from jax import lax
from jax.experimental import pallas as pl
from jax.experimental.pallas import tpu as pltpu
from jax.sharding import Mesh
from jax.sharding import PartitionSpec as P

HD = 64
NSTATE = 128
STRETCH = 256
DI = 3072
CONV = 4
LANES = 128
BC = 2 * NSTATE

eps = 1e-05

EVERY = ("a", "b", "c", "p", "q")
SEQ = ("a", "b", "c")
FSDP = ("p", "q")
TEAM = ("q", "b", "c")
COPIES = ("p", "a")
SWAP = [(0, 0), (1, 2), (2, 1), (3, 3)]

F32 = jnp.float32
BF16 = jnp.bfloat16
EXACT = lax.Precision.HIGHEST


def mm(left, right):
    return jnp.dot(left, right, preferred_element_type=F32)


def mm_nt(left, right):
    return lax.dot_general(left, right, (((1,), (1,)), ((), ())), preferred_element_type=F32)


def mm_tn(left, right):
    return lax.dot_general(left, right, (((0,), (0,)), ((), ())), preferred_element_type=F32)


def mm_exact(left, right):
    return jnp.dot(left, right, precision=EXACT, preferred_element_type=F32)


def iota(shape, dim):
    return lax.broadcasted_iota(jnp.int32, shape, dim)


def head_spread(width):
    return (iota((LANES, width), 0) == iota((LANES, width), 1) // HD).astype(F32)


def head_fold(width):
    return (iota((width, LANES), 0) // HD == iota((width, LANES), 1)).astype(F32)


def steps_of(raw, head_rows):
    shifted = raw + head_rows[0:1]
    step = jnp.maximum(shifted, 0.0) + jnp.log1p(jnp.exp(-jnp.abs(shifted)))
    return shifted, step


def pairs(width):
    return [(at, min(at + LANES, width)) for at in range(0, width, LANES)]


def mix_forward_kernel(
    proj_ref, conv_ref, head_ref, skip_ref, gated_ref, y_ref, enter_ref, state_ref, ext_ref
):
    rows = proj_ref.shape[0]
    wide = gated_ref.shape[1]
    chans = wide + BC

    @pl.when(pl.program_id(0) == 0)
    def _():
        state_ref[...] = jnp.zeros_like(state_ref)
        ext_ref[0:8, :] = jnp.zeros((8, chans), F32)

    ext_ref[8 : 8 + rows, :] = proj_ref[:, wide : wide + chans].astype(F32)
    pre = conv_ref[CONV : CONV + 1, :] + conv_ref[0:1, :] * ext_ref[5 : 5 + rows, :]
    for lag in range(1, CONV):
        pre = pre + conv_ref[lag : lag + 1, :] * ext_ref[5 + lag : 5 + lag + rows, :]
    ext_ref[0:8, :] = ext_ref[rows : rows + 8, :]
    act = pre * jax.nn.sigmoid(pre)
    x = act[:, :wide]
    b_low = act[:, wide : wide + NSTATE].astype(BF16)
    c_low = act[:, wide + NSTATE :].astype(BF16)

    _, step = steps_of(proj_ref[:, wide + chans :].astype(F32), head_ref)
    decay = -step * head_ref[1:2, :]
    lower = iota((rows, rows), 0) >= iota((rows, rows), 1)
    cum = mm_exact(lower.astype(F32), decay)
    cum_t = jnp.transpose(cum)
    spread = head_spread(wide)
    cum_wide = mm_exact(cum, spread)
    step_wide = mm_exact(step, spread)
    total = cum_wide[rows - 1 : rows, :]

    scores = mm_nt(c_low, b_low)
    weighted = x * step_wide
    weighted_low = weighted.astype(BF16)
    within = []
    for start, end in pairs(wide):
        both = weighted_low[:, start:end]
        parts = []
        for head in range(start // HD, end // HD):
            gap = cum[:, head : head + 1] - cum_t[head : head + 1, :]
            mixed = jnp.where(lower, jnp.exp(gap), 0.0) * scores
            parts.append(mm(mixed.astype(BF16), both))
        if len(parts) == 2:
            first = iota((rows, end - start), 1) < HD
            within.append(jnp.where(first, parts[0], parts[1]))
        else:
            within.append(parts[0])
    within = jnp.concatenate(within, axis=1)
    state = state_ref[...]
    enter_ref[0] = state
    carried = jnp.exp(cum_wide) * mm(c_low, state.astype(BF16))
    y = within + carried + skip_ref[0:1, :] * x
    gate = proj_ref[:, :wide].astype(F32)
    gated_ref[...] = (y * (gate * jax.nn.sigmoid(gate))).astype(BF16)
    y_ref[...] = y.astype(BF16)
    ending = (weighted * jnp.exp(total - cum_wide)).astype(BF16)
    state_ref[...] = state * jnp.exp(total) + mm_tn(b_low, ending)


def mix_forward(proj, conv_rows, head_rows, wide_rows):
    length, width = proj.shape
    wide = wide_rows.shape[1]
    count = length // STRETCH
    whole = lambda shape: pl.BlockSpec(shape, lambda i: (0,) * len(shape))
    part = lambda cols: pl.BlockSpec((STRETCH, cols), lambda i: (i, 0))
    return pl.pallas_call(
        mix_forward_kernel,
        grid=(count,),
        in_specs=[
            part(width),
            whole(conv_rows.shape),
            whole(head_rows.shape),
            whole(wide_rows.shape),
        ],
        out_specs=[
            part(wide),
            part(wide),
            pl.BlockSpec((1, NSTATE, wide), lambda i: (i, 0, 0)),
        ],
        out_shape=[
            jax.ShapeDtypeStruct((length, wide), BF16),
            jax.ShapeDtypeStruct((length, wide), BF16),
            jax.ShapeDtypeStruct((count, NSTATE, wide), F32),
        ],
        scratch_shapes=[
            pltpu.VMEM((NSTATE, wide), F32),
            pltpu.VMEM((STRETCH + 8, wide + BC), F32),
        ],
        compiler_params=pltpu.CompilerParams(
            dimension_semantics=("arbitrary",), vmem_limit_bytes=48 * 1024 * 1024
        ),
        cost_estimate=pl.CostEstimate(
            flops=length * 2 * STRETCH * wide * 4, bytes_accessed=length * 6000, transcendentals=0
        ),
        name="mix_forward",
    )(proj, conv_rows, head_rows, wide_rows)


def mix_backward_kernel(
    proj_ref,
    before_ref,
    y_ref,
    pulled_ref,
    kappa_ref,
    enter_ref,
    conv_ref,
    head_ref,
    wide_ref,
    out_ref,
    conv_grad_ref,
    head_grad_ref,
    skip_grad_ref,
    dstate_ref,
    ext_ref,
    gext_ref,
    rows_ref,
):
    rows = proj_ref.shape[0]
    wide = y_ref.shape[1]
    chans = wide + BC
    turn = pl.program_id(0)

    @pl.when(turn == 0)
    def _():
        dstate_ref[...] = jnp.zeros_like(dstate_ref)
        gext_ref[rows : rows + 8, :] = jnp.zeros((8, chans), F32)
        conv_grad_ref[...] = jnp.zeros_like(conv_grad_ref)
        head_grad_ref[...] = jnp.zeros_like(head_grad_ref)
        skip_grad_ref[...] = jnp.zeros_like(skip_grad_ref)
        rows_ref[...] = jnp.zeros_like(rows_ref)

    before = before_ref[8:16, wide : wide + chans].astype(F32)
    ext_ref[0:8, :] = jnp.where(turn == pl.num_programs(0) - 1, 0.0, before)
    ext_ref[8 : 8 + rows, :] = proj_ref[:, wide : wide + chans].astype(F32)
    pre = conv_ref[CONV : CONV + 1, :] + conv_ref[0:1, :] * ext_ref[5 : 5 + rows, :]
    for lag in range(1, CONV):
        pre = pre + conv_ref[lag : lag + 1, :] * ext_ref[5 + lag : 5 + lag + rows, :]
    sig = jax.nn.sigmoid(pre)
    act = pre * sig
    slope = sig * (1.0 + pre * (1.0 - sig))
    x = act[:, :wide]
    x_low = x.astype(BF16)
    b_low = act[:, wide : wide + NSTATE].astype(BF16)
    c_low = act[:, wide + NSTATE :].astype(BF16)

    shifted, step = steps_of(proj_ref[:, wide + chans :].astype(F32), head_ref)
    rate = head_ref[1:2, :]
    decay = -step * rate
    lower = iota((rows, rows), 0) >= iota((rows, rows), 1)
    upper = iota((rows, rows), 0) <= iota((rows, rows), 1)
    cum = mm_exact(lower.astype(F32), decay)
    cum_t = jnp.transpose(cum)
    spread = head_spread(wide)
    fold = head_fold(wide)
    cum_wide = mm_exact(cum, spread)
    step_wide = mm_exact(step, spread)
    total = cum_wide[rows - 1 : rows, :]
    grown = jnp.exp(cum_wide)
    to_end = jnp.exp(total - cum_wide)

    gate = proj_ref[:, :wide].astype(F32)
    y = y_ref[...].astype(F32)
    gate_sig = jax.nn.sigmoid(gate)
    gate_act = gate * gate_sig
    gain = wide_ref[1:2, :]
    g_gated = gain * pulled_ref[...].astype(F32) - (y * gate_act) * kappa_ref[...]
    dy = g_gated * gate_act
    out_ref[:, :wide] = (g_gated * y * (gate_sig * (1.0 + gate * (1.0 - gate_sig)))).astype(BF16)
    dy_low = dy.astype(BF16)
    skip_grad_ref[0:1, :] += jnp.sum(x * dy, axis=0, keepdims=True)

    scores_t = mm_nt(b_low, c_low)
    lane = iota((rows, LANES), 1)
    d_scores = jnp.zeros((rows, rows), F32)
    column = jnp.zeros((rows, LANES), F32)
    inner = []
    for start, end in pairs(wide):
        both_dy = dy_low[:, start:end]
        both_x = x_low[:, start:end]
        side = iota((rows, end - start), 1) // HD
        parts = []
        for head in range(start // HD, end // HD):
            gap = cum_t[head : head + 1, :] - cum[:, head : head + 1]
            fade = jnp.where(upper, jnp.exp(gap), 0.0)
            own = jnp.where(side == head - start // HD, both_x, jnp.zeros_like(both_x))
            faded = fade * mm_nt(own, both_dy)
            stepped = faded * step[:, head : head + 1]
            d_scores = d_scores + stepped
            parts.append(mm((scores_t * fade).astype(BF16), both_dy))
            column = jnp.where(
                lane == head, jnp.sum(scores_t * faded, axis=1, keepdims=True), column
            )
            rows_ref[head : head + 1, :] = jnp.sum(scores_t * stepped, axis=0, keepdims=True)
        if len(parts) == 2:
            inner.append(jnp.where(side == 0, parts[0], parts[1]))
        else:
            inner.append(parts[0])
    inner = jnp.concatenate(inner, axis=1)

    enter = enter_ref[0]
    enter_low = enter.astype(BF16)
    dstate = dstate_ref[...]
    dstate_low = dstate.astype(BF16)
    outer = to_end * mm(b_low, dstate_low)
    g_x = step_wide * (inner + outer) + wide_ref[0:1, :] * dy
    dy_grown = dy * grown
    dy_grown_low = dy_grown.astype(BF16)
    carried_sum = mm_exact(dy_grown * mm(c_low, enter_low), fold)
    outer_sum = mm_exact(x * outer, fold)
    state_sum = mm_exact(
        jnp.broadcast_to(jnp.sum(enter * dstate, axis=0, keepdims=True), (8, wide)), fold
    )[0:1, :]
    step_outer = step * outer_sum
    g_cum = jnp.transpose(rows_ref[...]) + carried_sum - step * column - step_outer
    g_total = (
        jnp.sum(step_outer, axis=0, keepdims=True)
        + jnp.exp(cum[rows - 1 : rows, :]) * state_sum
    )
    g_decay = mm_exact(upper.astype(F32), g_cum) + g_total
    scaled_decay = rate * g_decay
    g_raw = (column + outer_sum - scaled_decay) * jax.nn.sigmoid(shifted)
    head_grad_ref[0:1, :] += jnp.sum(g_raw, axis=0, keepdims=True)
    head_grad_ref[1:2, :] -= jnp.sum(step * scaled_decay, axis=0, keepdims=True)
    out_ref[:, wide + chans :] = g_raw.astype(BF16)

    d_low = d_scores.astype(BF16)
    ending = (x * (step_wide * to_end)).astype(BF16)
    g_b = mm(d_low, c_low) + mm_nt(ending, dstate_low)
    g_c = mm_tn(d_low, b_low) + mm_nt(dy_grown_low, enter_low)
    dstate_ref[...] = dstate * jnp.exp(total) + mm_tn(c_low, dy_grown_low)

    gext_ref[0:rows, :wide] = g_x * slope[:, :wide]
    gext_ref[0:rows, wide : wide + NSTATE] = g_b * slope[:, wide : wide + NSTATE]
    gext_ref[0:rows, wide + NSTATE :] = g_c * slope[:, wide + NSTATE :]
    g_pre = gext_ref[0:rows, :]
    g_in = conv_ref[CONV - 1 : CONV, :] * g_pre
    for lag in range(CONV - 1):
        g_in = g_in + conv_ref[lag : lag + 1, :] * gext_ref[3 - lag : 3 - lag + rows, :]
    out_ref[:, wide : wide + chans] = g_in.astype(BF16)
    for lag in range(CONV):
        conv_grad_ref[lag : lag + 1, :] += jnp.sum(
            ext_ref[5 + lag : 5 + lag + rows, :] * g_pre, axis=0, keepdims=True
        )
    conv_grad_ref[CONV : CONV + 1, :] += jnp.sum(g_pre, axis=0, keepdims=True)
    gext_ref[rows : rows + 8, :] = gext_ref[0:8, :]


def mix_backward(proj, y, pulled, kappa, enter, conv_rows, head_rows, wide_rows):
    length, width = proj.shape
    wide = wide_rows.shape[1]
    count = length // STRETCH
    whole = lambda shape: pl.BlockSpec(shape, lambda i: (0,) * len(shape))
    part = lambda cols: pl.BlockSpec((STRETCH, cols), lambda i: (count - 1 - i, 0))
    before = pl.BlockSpec(
        (16, width), lambda i: (jnp.maximum((count - 1 - i) * (STRETCH // 16) - 1, 0), 0)
    )
    return pl.pallas_call(
        mix_backward_kernel,
        grid=(count,),
        in_specs=[
            part(width),
            before,
            part(wide),
            part(wide),
            part(1),
            pl.BlockSpec((1, NSTATE, wide), lambda i: (count - 1 - i, 0, 0)),
            whole(conv_rows.shape),
            whole(head_rows.shape),
            whole(wide_rows.shape),
        ],
        out_specs=[
            part(width),
            whole((8, wide + BC)),
            whole((8, LANES)),
            whole((8, wide)),
        ],
        out_shape=[
            jax.ShapeDtypeStruct((length, width), BF16),
            jax.ShapeDtypeStruct((8, wide + BC), F32),
            jax.ShapeDtypeStruct((8, LANES), F32),
            jax.ShapeDtypeStruct((8, wide), F32),
        ],
        scratch_shapes=[
            pltpu.VMEM((NSTATE, wide), F32),
            pltpu.VMEM((STRETCH + 8, wide + BC), F32),
            pltpu.VMEM((STRETCH + 8, wide + BC), F32),
            pltpu.VMEM((LANES, STRETCH), F32),
        ],
        compiler_params=pltpu.CompilerParams(
            dimension_semantics=("arbitrary",), vmem_limit_bytes=48 * 1024 * 1024
        ),
        cost_estimate=pl.CostEstimate(
            flops=length * 2 * STRETCH * wide * 8, bytes_accessed=length * 9000, transcendentals=0
        ),
        name="mix_backward",
    )(proj, proj, y, pulled, kappa, enter, conv_rows, head_rows, wide_rows)


def team_gather(rows):
    return lax.all_gather(rows, TEAM, axis=0, tiled=True)


def team_scatter(rows):
    return lax.psum_scatter(rows, TEAM, scatter_dimension=0, tiled=True)


def swap(values):
    return lax.ppermute(values, ("a", "q"), SWAP)


def rms(values):
    return lax.rsqrt(jnp.mean(values * values, axis=-1, keepdims=True) + eps)


def local(
    tokens,
    cotangent,
    norm_gain,
    in_weight,
    conv_kernel,
    conv_shift,
    dt_bias,
    a_log,
    skip_gain,
    gate_gain,
    out_weight,
):
    layers, depth, columns = in_weight.shape
    heads = dt_bias.shape[1]
    wide = heads * HD
    chans = wide + BC
    team = lax.axis_size(TEAM)
    sizes = tuple(lax.axis_size(name) for name in EVERY)
    model = in_weight.shape[1] * team * lax.axis_size(COPIES)
    rank = lax.axis_index(TEAM)
    tail = columns - 2 * DI

    small = jnp.concatenate(
        [
            norm_gain,
            conv_kernel.reshape(layers, -1),
            conv_shift,
            gate_gain,
        ],
        axis=1,
    )
    small = lax.all_gather(small, EVERY, axis=0)
    n_norm, n_conv, n_gate = norm_gain.shape[1], conv_shift.shape[1], gate_gain.shape[1]
    cuts = [n_norm, n_norm + CONV * n_conv, n_norm + (CONV + 1) * n_conv]
    head_all = swap(jnp.stack([dt_bias, a_log, skip_gain]))

    def parameters(layer):
        mine = small[:, layer]
        norm = mine[:, : cuts[0]].reshape(-1).astype(F32)
        kernel = mine[:, cuts[0] : cuts[1]].reshape(-1, CONV, n_conv)
        kernel = kernel.transpose(1, 0, 2).reshape(CONV, -1).astype(F32)
        shift = mine[:, cuts[1] : cuts[2]].reshape(1, -1).astype(F32)
        gate = mine[:, cuts[2] :].reshape(1, -1).astype(F32)
        rows = jnp.concatenate([kernel, shift, jnp.zeros((3, kernel.shape[1]), F32)], axis=0)
        conv_rows = jnp.concatenate(
            [lax.dynamic_slice_in_dim(rows, rank * wide, wide, 1), rows[:, DI:]], axis=1
        )
        head_rows = jnp.zeros((8, LANES), F32)
        head_rows = head_rows.at[0, :heads].set(head_all[0, layer])
        head_rows = head_rows.at[1, :heads].set(jnp.exp(head_all[1, layer]))
        wide_rows = jnp.concatenate(
            [
                jnp.repeat(head_all[2, layer], HD)[None],
                lax.dynamic_slice_in_dim(gate, rank * wide, wide, 1),
                jnp.zeros((6, wide), F32),
            ],
            axis=0,
        )
        return norm, conv_rows, head_rows, wide_rows

    def in_columns(layer):
        mine = in_weight[layer]
        parts = mine[:, : 2 * DI].reshape(depth, 2, team, wide).transpose(2, 0, 1, 3)
        parts = parts.reshape(team, depth, 2 * wide)
        parts = lax.all_to_all(parts, TEAM, split_axis=0, concat_axis=0)
        parts = lax.all_gather(parts, COPIES, axis=0)
        parts = parts.reshape(sizes[3], 2, 2, *sizes[1:3], depth, 2 * wide)
        parts = parts.transpose(1, 3, 4, 0, 2, 5, 6).reshape(model, 2 * wide)
        rest = lax.all_gather(mine[:, 2 * DI :], EVERY, axis=0, tiled=True)
        steps = lax.dynamic_slice_in_dim(rest, BC + rank * heads, heads, 1)
        steps = jnp.pad(steps, ((0, 0), (0, LANES - heads)))
        return jnp.concatenate([parts, rest[:, :BC], steps], axis=1)

    def out_rows(layer):
        return lax.all_gather(swap(out_weight[layer]), COPIES, axis=0, tiled=True)

    residual = swap(tokens[0]).astype(F32)
    records = []
    for layer in range(layers):
        params = parameters(layer)
        norm, conv_rows, head_rows, wide_rows = params
        weight_in, weight_out = in_columns(layer), out_rows(layer)
        rho = rms(residual)
        normed = team_gather((residual * rho * norm).astype(BF16))
        proj = mm(normed, weight_in).astype(BF16)
        gated, y, enter = mix_forward(proj, conv_rows, head_rows, wide_rows)
        gated_wide = gated.astype(F32)
        squares = jnp.sum(gated_wide * gated_wide, axis=1, keepdims=True)
        branch = mm((gated_wide * wide_rows[1:2]).astype(BF16), weight_out)
        sent = jnp.concatenate([branch, jnp.broadcast_to(squares, (gated.shape[0], LANES))], axis=1)
        got = team_scatter(sent.astype(BF16)).astype(F32)
        branch = got[:, :model]
        gate_rho = lax.rsqrt(got[:, model : model + 1] / DI + eps)
        records.append(
            (residual, rho, normed, proj, gated, y, enter, branch, gate_rho, weight_in, weight_out, params)
        )
        residual = residual + gate_rho * branch

    out = swap(residual.astype(BF16))
    grad = swap(cotangent[0]).astype(F32)
    in_grads, out_grads, vectors, head_grads = [], [], [], []
    for layer in reversed(range(layers)):
        (before, rho, normed, proj, gated, y, enter, branch, gate_rho, weight_in, weight_out, params) = records[layer]
        norm, conv_rows, head_rows, wide_rows = params
        pulled = grad * gate_rho
        kappa = gate_rho * gate_rho * jnp.sum(pulled * branch, axis=1, keepdims=True) / DI
        sent = jnp.concatenate([pulled, jnp.broadcast_to(kappa, (pulled.shape[0], LANES))], axis=1)
        got = team_gather(sent.astype(BF16))
        g_branch = got[:, :model]
        kappa = got[:, model : model + 1].astype(F32)
        g_scaled = mm_nt(g_branch, weight_out)
        outer = mm_tn(gated, g_branch)
        g_gate_gain = jnp.sum(outer * weight_out.astype(F32), axis=1)
        g_out = (outer * wide_rows[1][:, None]).astype(BF16)
        g_proj, g_conv, g_heads, g_skip = mix_backward(
            proj, y, g_scaled, kappa, enter, conv_rows, head_rows, wide_rows
        )
        g_normed = team_scatter(mm_nt(g_proj, weight_in).astype(BF16)).astype(F32)
        g_in = mm_tn(normed, g_proj).astype(BF16)

        g_out = swap(lax.psum_scatter(g_out, COPIES, scatter_dimension=0, tiled=True))
        out_grads.insert(0, g_out.astype(F32))
        parts = g_in[:, : 2 * wide].reshape(*sizes[:4], 2, depth, 2 * wide)
        parts = parts.transpose(3, 0, 4, 1, 2, 5, 6).reshape(-1, team, depth, 2 * wide)
        parts = lax.psum_scatter(parts, COPIES, scatter_dimension=0)
        parts = lax.all_to_all(parts, TEAM, split_axis=0, concat_axis=0)
        parts = parts.reshape(team, depth, 2, wide).transpose(1, 2, 0, 3).reshape(depth, 2 * DI)
        rest = jnp.zeros((model, tail - BC), BF16)
        rest = lax.dynamic_update_slice_in_dim(
            rest, g_in[:, 2 * wide + BC : 2 * wide + BC + heads], rank * heads, 1
        )
        rest = jnp.concatenate([g_in[:, 2 * wide : 2 * wide + BC], rest], axis=1)
        rest = lax.psum_scatter(rest, EVERY, scatter_dimension=0, tiled=True)
        in_grads.insert(0, jnp.concatenate([parts, rest], axis=1).astype(F32))

        weighed = g_normed * norm
        mean = jnp.mean(weighed * before, axis=1, keepdims=True)
        grad = grad + rho * weighed - before * (rho * rho * rho * mean)
        g_norm = jnp.sum(g_normed * before * rho, axis=0)
        g_conv_all = jnp.concatenate(
            [
                lax.dynamic_update_slice_in_dim(
                    jnp.zeros((CONV + 1, DI), F32), g_conv[: CONV + 1, :wide], rank * wide, 1
                ),
                g_conv[: CONV + 1, wide:],
            ],
            axis=1,
        )
        g_gate_all = lax.dynamic_update_slice_in_dim(
            jnp.zeros((DI,), F32), g_gate_gain, rank * wide, 0
        )
        vectors.insert(0, (g_norm, g_conv_all, g_gate_all))
        head_grads.insert(
            0,
            jnp.stack(
                [
                    g_heads[0, :heads],
                    g_heads[1, :heads],
                    jnp.sum(g_skip[0].reshape(heads, HD), axis=1),
                ]
            ),
        )

    norm_all = jnp.stack([entry[0] for entry in vectors])
    conv_all = jnp.stack([entry[1] for entry in vectors])
    gate_all = jnp.stack([entry[2] for entry in vectors])
    norm_all, conv_all, gate_all = lax.psum((norm_all, conv_all, gate_all), EVERY)
    place = lax.axis_index(EVERY)
    norm_all = lax.dynamic_slice_in_dim(norm_all, place * n_norm, n_norm, 1)
    conv_all = lax.dynamic_slice_in_dim(conv_all, place * n_conv, n_conv, 2)
    gate_all = lax.dynamic_slice_in_dim(gate_all, place * n_gate, n_gate, 1)
    head_all = swap(lax.psum(jnp.stack(head_grads), COPIES))
    grad_tokens = swap(grad)
    return (
        out[None],
        grad_tokens[None],
        norm_all,
        jnp.stack(in_grads),
        conv_all[:, :CONV],
        conv_all[:, CONV],
        head_all[:, 0],
        head_all[:, 1],
        head_all[:, 2],
        gate_all,
        jnp.stack(out_grads),
    )


def solution(mesh):
    seq, fsdp = mesh.shape["seq"], mesh.shape["fsdp"]
    fine = Mesh(mesh.devices.reshape(2, seq // 4, 2, fsdp // 2, 2), EVERY)
    acts = P(FSDP, SEQ, None)
    flat = P(None, SEQ + FSDP)
    rows = P(None, SEQ + FSDP, None)
    taps = P(None, None, SEQ + FSDP)
    head = P(None, SEQ)
    return jax.shard_map(
        local,
        mesh=fine,
        in_specs=(acts, acts, flat, rows, taps, flat, head, head, head, flat, rows),
        out_specs=(acts, acts, flat, rows, taps, flat, head, head, head, flat, rows),
        check_vma=False,
    )
```

time: 2050 us -> 1280 us (0.62)
  local copies, waits for them, and re-layouts: 342 us -> 63.2 us
  matrix products: 276 us -> 62.5 us
  other arithmetic: 245 us -> 31.5 us
  waiting for transfers between devices: 748 us -> 626 us
  blocking collectives: 325 us -> 388 us
  Pallas kernels: 0 us -> 62.2 us
  starting transfers between devices: 78 us -> 21.9 us
    dot_general x62 -> x12, matrix products: 276 us -> 62.5 us  [the longest x4 21.6 us: mm_nt(): lax.dot_general(left, right, (((1,), (1,)), ((), ())), preferred_element_...]
    unnamed x16 -> x1, other arithmetic: 154 us -> 0.08 us
    unnamed x22 -> x19, waiting for transfers between devices: 150 us -> 0.31 us
    psum x0 -> x1, waiting for transfers between devices: none -> 123 us  [local(): lax.psum((norm_all, conv_all, gate_all), EVERY)]
    unnamed x550 -> x131, local copies, waits for them, and re-layouts: 139 us -> 20 us
    all_to_all x16 -> x2, waiting for transfers between devices: 116 us -> 0.01 us  [local(): parts = lax.all_to_all(parts, TEAM, split_axis=0, concat_axis=0)]
    unnamed x3 -> x0, blocking collectives: 87 us -> none
    all_to_all x16 -> x2, starting transfers between devices: 77.1 us -> 7.21 us  [local(): parts = lax.all_to_all(parts, TEAM, split_axis=0, concat_axis=0)]
  transfers between devices with their start and end apart: 32 -> 31, of which waited for: 17 -> 15; matrix products, arithmetic and copies ran while one was open for 30% -> 8% of each run, Pallas kernels for 0% -> 3%
where the time goes in v1:
time: 1280 us; the launch traced here: 1270 us
  waiting for transfers between devices  626 us (49%)
  blocking collectives  388 us (30%)
  local copies, waits for them, and re-layouts  63.2 us (5%)
  matrix products  62.5 us (5%)
  Pallas kernels  62.2 us (5%)
  other arithmetic  31.5 us (2%)
  starting transfers between devices  21.9 us (2%)
  between operations  15.8 us (1%)
    all_gather x2, blocking collectives, in_columns(): rest = lax.all_gather(mine[:, 2 * DI:], EVERY, axis=0, tiled=True)  209 us
    reduce_scatter x2, waiting for transfers between devices, local(): rest = lax.psum_scatter(rest, EVERY, scatter_dimension=0, tiled=True)  196 us
    reduce_scatter x4, waiting for transfers between devices, team_scatter(): return lax.psum_scatter(rows, TEAM, scatter_dimension=0, tiled=True)  143 us
    psum x1, waiting for transfers between devices, local(): lax.psum((norm_all, conv_all, gate_all), EVERY)  123 us
    reduce_scatter x2, waiting for transfers between devices, local(): lax.psum_scatter(g_out, COPIES, scatter_dimension=0, tiled=True)  84.1 us
    all_gather x1, blocking collectives, local(): small = lax.all_gather(small, EVERY, axis=0)  69.2 us
    pallas_call x2, Pallas kernels, mix_backward(): pl.pallas_call(mix_backward_kernel, grid=(count,), in_specs=[part(width),...  44.4 us
    psum x1, blocking collectives, local(): lax.psum((norm_all, conv_all, gate_all), EVERY)  40.6 us
  transfers between devices with their start and end apart: 31, of which 15 were waited for; matrix products, arithmetic and copies ran while one was open for 8% of the time, Pallas kernels for 3%

profile of v1, /device:TPU:0, one launch (start us, length us, event | category | flops | bytes accessed | tf_op | source)
XLA Modules:
  0.0 1271.8 jit_solution(15559379440616300069)
XLA Ops:
  10.4 15.6 %all_to_all.20 = bf16[8,48,768]{2,1,0:T(8,128)(2,1)} all-to-all(bf16[8,48,768]{2,1,0:T(8,128)(2,1)S(1)} %reshape.393), channel_id=1, replica_groups=mesh['a'=2,'b'=2,'c'=2,'p'=2,'q'=2] {'q','b','c'}, dimensions={0} | all-to-all | bytes 1179648 | tf_op jit(solution)/shard_map/all_to_all | solution.py:451
  27.9 69.2 %all-gather.3 = bf16[32,2,664]{2,1,0:T(2,128)(2,1)S(1)} all-gather(bf16[1,2,664]{2,1,0:T(2,128)(2,1)S(1)} %maximum_bitcast_fusion.1), channel_id=2, replica_groups=mesh['a'=2,'b'=2,'c'=2,'p'=2,'q'=2] {'a','b','c','p','q'}, dimensions={0}, use_global_device_ids=true | all-gather | bytes 87648 | tf_op jit(solution)/shard_map/all_gather | solution.py:418
  103.0 104.2 %all_gather.47 = bf16[1536,304]{1,0:T(8,128)(2,1)S(1)} all-gather(bf16[48,304]{1,0:T(8,128)(2,1)S(1)} %slice.295), channel_id=1, replica_groups=mesh['a'=2,'b'=2,'c'=2,'p'=2,'q'=2] {'a','b','c','p','q'}, dimensions={0}, use_global_device_ids=true | all-gather | bytes 963072 | tf_op jit(solution)/shard_map/all_gather | solution.py:455
  214.5 7.0 convolution_convert_fusion.5.proj_ref.before_ref
  221.5 8.9 mix_forward.2
  232.4 12.1 all-gather.15.cloned.1.call-done
  251.9 20.2 %all_to_all.21 = bf16[8,48,768]{2,1,0:T(8,128)(2,1)} all-to-all(bf16[8,48,768]{2,1,0:T(8,128)(2,1)S(1)} %reshape.398), channel_id=1, replica_groups=mesh['a'=2,'b'=2,'c'=2,'p'=2,'q'=2] {'q','b','c'}, dimensions={0} | all-to-all | bytes 1179648 | tf_op jit(solution)/shard_map/all_to_all | solution.py:451
  272.3 24.7 %reduce-scatter.15.cloned.1.call-done = bf16[128,1664]{1,0:T(8,128)(2,1)} async-done(((bf16[1024,1664]{1,0:T(8,128)(2,1)}), bf16[128,1664]{1,0:T(8,128)(2,1)}) %reduce-scatter.15.cloned.1.call-update) | async-done | bytes 426000 | tf_op jit(solution)/shard_map/reduce_scatter | solution.py:375
  302.4 104.7 %all_gather.52 = bf16[1536,304]{1,0:T(8,128)(2,1)S(1)} all-gather(bf16[48,304]{1,0:T(8,128)(2,1)S(1)} %slice.309), channel_id=1, replica_groups=mesh['a'=2,'b'=2,'c'=2,'p'=2,'q'=2] {'a','b','c','p','q'}, dimensions={0}, use_global_device_ids=true | all-gather | bytes 963072 | tf_op jit(solution)/shard_map/all_gather | solution.py:455
  413.8 7.2 convolution_convert_fusion.3.proj_ref.before_ref
  421.1 8.9 mix_forward.3
  432.9 4.8 all-gather.19.cloned.1.call-done
  445.0 43.3 %reduce-scatter.17.cloned.1.call-done = bf16[128,1664]{1,0:T(8,128)(2,1)} async-done(((bf16[1024,1664]{1,0:T(8,128)(2,1)}), bf16[128,1664]{1,0:T(8,128)(2,1)}) %reduce-scatter.17.cloned.1.call-update) | async-done | bytes 426000 | tf_op jit(solution)/shard_map/reduce_scatter | solution.py:375
  491.9 29.1 %all-gather.21.cloned.1.call-done = bf16[1024,1664]{1,0:T(8,128)(2,1)} async-done(((bf16[128,1664]{1,0:T(8,128)(2,1)}), bf16[1024,1664]{1,0:T(8,128)(2,1)}) %all-gather.21.cloned.1.call-update) | async-done | bytes 3407888 | tf_op jit(solution)/shard_map/all_gather | solution.py:371
  526.0 22.2 %mix_backward.2 = (bf16[1024,1152]{1,0:T(8,128)(2,1)S(1)}, f32[8,640]{1,0:T(8,128)S(1)}, f32[8,128]{1,0:T(8,128)S(1)}, f32[8,384]{1,0:T(8,128)S(1)}) custom-call(bf16[1024,1152]{1,0:T(8,128)(2,1)} %copy-done.1, bf16[1024,1152]{1,0:T(8,128)(2,1)} %copy-done.1, bf16[1024,384]{1,0:T(8,128)(2,1)S(1)} %copy-done.9, f32[1024,384]{1,0:T(8,128)S(1)} %fusion.10.pulled_ref, ...), custom_call_target="tpu_custom_call" | custom-call | flops 1610612736 | bytes 9216000 | tf_op jit(solution)/shard_map/mix_backward/pallas_call | solution.py:328
  549.6 5.7 convolution_convert_fusion.7
  555.4 39.3 %reduce-scatter.19.cloned.1.call-done = bf16[128,1536]{1,0:T(8,128)(2,1)} async-done(((bf16[1024,1536]{1,0:T(8,128)(2,1)}), bf16[128,1536]{1,0:T(8,128)(2,1)}) %reduce-scatter.19.cloned.1.call-update) | async-done | bytes 393232 | tf_op jit(solution)/shard_map/reduce_scatter | solution.py:375
  603.9 6.2 convolution_convert_fusion
  618.0 4.9 multiply_convert_fusion
  623.2 5.8 all-gather.23.cloned.1.call-done
  633.8 22.2 %mix_backward.3 = (bf16[1024,1152]{1,0:T(8,128)(2,1)S(1)}, f32[8,640]{1,0:T(8,128)S(1)}, f32[8,128]{1,0:T(8,128)S(1)}, f32[8,384]{1,0:T(8,128)S(1)}) custom-call(bf16[1024,1152]{1,0:T(8,128)(2,1)} %copy-done, bf16[1024,1152]{1,0:T(8,128)(2,1)} %copy-done, bf16[1024,384]{1,0:T(8,128)(2,1)S(1)} %copy-done.5, f32[1024,384]{1,0:T(8,128)S(1)} %fusion.6.pulled_ref, ...), custom_call_target="tpu_custom_call" | custom-call | flops 1610612736 | bytes 9216000 | tf_op jit(solution)/shard_map/mix_backward/pallas_call | solution.py:328
  671.5 5.0 multiply_convert_fusion.1
  677.9 8.0 convolution_convert_fusion.6
  695.5 48.3 %reduce-scatter.29.cloned.1.call-done = bf16[96,1536]{1,0:T(8,128)(2,1)} async-done(((bf16[384,1536]{1,0:T(8,128)(2,1)}), bf16[96,1536]{1,0:T(8,128)(2,1)}) %reduce-scatter.29.cloned.1.call-update) | async-done | bytes 294928 | tf_op jit(solution)/shard_map/reduce_scatter | solution.py:507
  748.4 33.8 %psum.30 = f32[2,3,6]{2,1,0:T(4,128)S(1)} all-reduce(f32[2,3,6]{2,1,0:T(4,128)S(1)} %pad_maximum_fusion.12), channel_id=1, replica_groups=mesh['a'=2,'b'=2,'c'=2,'p'=2,'q'=2] {'p','a'}, use_global_device_ids=true, to_apply=%region_22.23 | all-reduce | flops 36 | bytes 288 | tf_op jit(solution)/shard_map/psum | solution.py:558
  784.7 25.0 %reduce-scatter.23.cloned.1.call-done = bf16[1,8,48,768]{3,2,1,0:T(8,128)(2,1)} async-done(((bf16[4,8,48,768]{3,2,1,0:T(8,128)(2,1)}), bf16[1,8,48,768]{3,2,1,0:T(8,128)(2,1)}) %reduce-scatter.23.cloned.1.call-update) | async-done | bytes 589840 | tf_op jit(solution)/shard_map/reduce_scatter | solution.py:511
  813.5 35.8 %reduce-scatter.27.cloned.1.call-done = bf16[96,1536]{1,0:T(8,128)(2,1)} async-done(((bf16[384,1536]{1,0:T(8,128)(2,1)}), bf16[96,1536]{1,0:T(8,128)(2,1)}) %reduce-scatter.27.cloned.1.call-update) | async-done | bytes 294928 | tf_op jit(solution)/shard_map/reduce_scatter | solution.py:507
  851.4 122.8 %all-reduce.7.cloned.1.call-done = f32[2,5,3328]{2,0,1:T(2,128)} async-done(((f32[2,5,3328]{2,0,1:T(2,128)}), f32[2,5,3328]{2,0,1:T(2,128)}) %all-reduce.7.cloned.1.call-update) | async-done | bytes 133136 | tf_op jit(solution)/shard_map/psum | solution.py:553
  981.5 36.1 %reduce-scatter.21.cloned.1.call-done = bf16[128,1536]{1,0:T(8,128)(2,1)} async-done(((bf16[1024,1536]{1,0:T(8,128)(2,1)}), bf16[128,1536]{1,0:T(8,128)(2,1)}) %reduce-scatter.21.cloned.1.call-update) | async-done | bytes 393232 | tf_op jit(solution)/shard_map/reduce_scatter | solution.py:375
  1022.8 95.7 %reduce-scatter.33.cloned.1.call-done = bf16[48,304]{1,0:T(8,128)(2,1)} async-done(((bf16[1536,304]{1,0:T(8,128)(2,1)}), bf16[48,304]{1,0:T(8,128)(2,1)}) %reduce-scatter.33.cloned.1.call-update) | async-done | bytes 29200 | tf_op jit(solution)/shard_map/reduce_scatter | solution.py:519
  1118.5 100.4 %reduce-scatter.31.cloned.1.call-done = bf16[48,304]{1,0:T(8,128)(2,1)} async-done(((bf16[1536,304]{1,0:T(8,128)(2,1)}), bf16[48,304]{1,0:T(8,128)(2,1)}) %reduce-scatter.31.cloned.1.call-update) | async-done | bytes 29200 | tf_op jit(solution)/shard_map/reduce_scatter | solution.py:519
  1221.3 40.6 %all-reduce.4 = (f32[2,1536]{1,0:T(2,128)S(1)}, f32[2,3072]{1,0:T(2,128)S(1)}) all-reduce(f32[2,1536]{1,0:T(2,128)S(1)} %pad_maximum_fusion.11, f32[2,3072]{1,0:T(2,128)S(1)} %pad_maximum_fusion.8), channel_id=1, replica_groups=mesh['a'=2,'b'=2,'c'=2,'p'=2,'q'=2] {'a','b','c','p','q'}, use_global_device_ids=true, to_apply=%region_14.15 | all-reduce | flops 9216 | bytes 73728 | tf_op jit(solution)/shard_map/psum | solution.py:553
  (364 shorter events, 138.5 us)
Async XLA Ops:
  7.2 204.0 %all-gather.25.cloned.1.call-start = ((), (), s32[]{:S(2)}) async-start(), calls=%async_computation.29 | async-start | bytes 2949120 | tf_op jit(solution)/shard_map/all_gather | solution.py:452
  26.0 188.4 %all-gather.13.cloned.1.call-start = ((), (), s32[]{:S(2)}) async-start(), calls=%async_computation.14 | async-start | bytes 3538944 | tf_op jit(solution)/shard_map/all_gather | solution.py:371
  26.1 71.3 %collective-permute-start = (bf16[128,1536]{1,0:T(8,128)(2,1)}, bf16[128,1536]{1,0:T(8,128)(2,1)S(1)}, u32[]{:S(2)}, u32[]{:S(2)}) collective-permute-start(bf16[128,1536]{1,0:T(8,128)(2,1)} %bitcast), channel_id=1, source_target_pairs={{0,0},{1,16},{16,1},{17,17},{2,2},{3,18},{18,3},{19,19},{4,4},{5,2... | collective-permute-start | bytes 1179656 | tf_op jit(solution)/shard_map/ppermute | solution.py:379
  98.6 146.0 %all-gather.15.cloned.1.call-start = ((), (), s32[]{:S(2)}) async-start(), calls=%async_computation.15 | async-start | bytes 1474560 | tf_op jit(solution)/shard_map/all_gather | solution.py:461
  98.6 112.0 %collective-permute-start.1 = (f32[3,2,6]{2,1,0:T(2,128)S(1)}, f32[3,2,6]{2,1,0:T(2,128)S(1)}, u32[]{:S(2)}, u32[]{:S(2)}) collective-permute-start(f32[3,2,6]{2,1,0:T(2,128)S(1)} %pad_maximum_fusion.13), channel_id=1, source_target_pairs={{0,0},{1,16},{16,1},{17,17},{2,2},{3,18},{18,3},{19,19},{4,4},{5,2... | collective-permute-start | bytes 440 | tf_op jit(solution)/shard_map/ppermute | solution.py:379
  100.1 109.6 %collective-permute-start.2 = (bf16[96,1536]{1,0:T(8,128)(2,1)S(1)}, bf16[96,1536]{1,0:T(8,128)(2,1)S(1)}, u32[]{:S(2)}, u32[]{:S(2)}) collective-permute-start(bf16[96,1536]{1,0:T(8,128)(2,1)S(1)} %get-tuple-element.176), channel_id=1, source_target_pairs={{0,0},{1,16},{16,1},{17,17},{2,2},{3,18},{18,3},{19,19},{4,4},{5,2... | collective-permute-start | bytes 884744 | tf_op jit(solution)/shard_map/ppermute | solution.py:379
  210.4 86.6 %reduce-scatter.15.cloned.1.call-start = ((), (), s32[]{:S(2)}) async-start(), calls=%async_computation.16 | async-start | bytes 3833856 | tf_op jit(solution)/shard_map/reduce_scatter | solution.py:375
  249.9 160.6 %all-gather.27.cloned.1.call-start = ((), (), s32[]{:S(2)}) async-start(), calls=%async_computation.30 | async-start | bytes 2949120 | tf_op jit(solution)/shard_map/all_gather | solution.py:452
  272.1 141.7 %all-gather.17.cloned.1.call-start = ((), (), s32[]{:S(2)}) async-start(), calls=%async_computation.17 | async-start | bytes 3538944 | tf_op jit(solution)/shard_map/all_gather | solution.py:371
  300.8 136.9 %all-gather.19.cloned.1.call-start = ((), (), s32[]{:S(2)}) async-start(), calls=%async_computation.18 | async-start | bytes 1474560 | tf_op jit(solution)/shard_map/all_gather | solution.py:461
  300.9 0.7 collective-permute-start.3
  302.4 185.9 %reduce-scatter.17.cloned.1.call-start = ((), (), s32[]{:S(2)}) async-start(), calls=%async_computation.19 | async-start | bytes 3833856 | tf_op jit(solution)/shard_map/reduce_scatter | solution.py:375
  443.3 77.6 %all-gather.21.cloned.1.call-start = ((), (), s32[]{:S(2)}) async-start(), calls=%async_computation.20 | async-start | bytes 3833856 | tf_op jit(solution)/shard_map/all_gather | solution.py:371
  444.3 45.1 %collective-permute-start.5 = (bf16[128,1536]{1,0:T(8,128)(2,1)S(1)}, bf16[128,1536]{1,0:T(8,128)(2,1)S(1)}, u32[]{:S(2)}, u32[]{:S(2)}) collective-permute-start(bf16[128,1536]{1,0:T(8,128)(2,1)S(1)} %bitcast.147), channel_id=1, source_target_pairs={{0,0},{1,16},{16,1},{17,17},{2,2},{3,18},{18,3},{19,19},{4,4},{5,2... | collective-permute-start | bytes 1179656 | tf_op jit(solution)/shard_map/ppermute | solution.py:379
  491.6 103.0 %reduce-scatter.19.cloned.1.call-start = ((), (), s32[]{:S(2)}) async-start(), calls=%async_computation.21 | async-start | bytes 3538944 | tf_op jit(solution)/shard_map/reduce_scatter | solution.py:375
  555.3 73.6 %all-gather.23.cloned.1.call-start = ((), (), s32[]{:S(2)}) async-start(), calls=%async_computation.22 | async-start | bytes 3833856 | tf_op jit(solution)/shard_map/all_gather | solution.py:371
  603.8 85.2 %reduce-scatter.25.cloned.1.call-start = ((), (), s32[]{:S(2)}) async-start(), calls=%async_computation.25 | async-start | bytes 2949120 | tf_op jit(solution)/shard_map/reduce_scatter | solution.py:511
  618.0 125.8 %reduce-scatter.29.cloned.1.call-start = ((), (), s32[]{:S(2)}) async-start(), calls=%async_computation.28 | async-start | bytes 1474560 | tf_op jit(solution)/shard_map/reduce_scatter | solution.py:507
  622.9 186.8 %reduce-scatter.23.cloned.1.call-start = ((), (), s32[]{:S(2)}) async-start(), calls=%async_computation.24 | async-start | bytes 2949120 | tf_op jit(solution)/shard_map/reduce_scatter | solution.py:511
  671.5 177.8 %reduce-scatter.27.cloned.1.call-start = ((), (), s32[]{:S(2)}) async-start(), calls=%async_computation.27 | async-start | bytes 1474560 | tf_op jit(solution)/shard_map/reduce_scatter | solution.py:507
  676.5 297.7 %all-reduce.7.cloned.1.call-start = ((), (), s32[]{:S(2)}) async-start(), calls=%async_computation.26 | async-start | bytes 266240 | tf_op jit(solution)/shard_map/psum | solution.py:553
  677.6 340.0 %reduce-scatter.21.cloned.1.call-start = ((), (), s32[]{:S(2)}) async-start(), calls=%async_computation.23 | async-start | bytes 3538944 | tf_op jit(solution)/shard_map/reduce_scatter | solution.py:375
  689.0 58.5 %all-to-all-start.3 = ((bf16[8,48,768]{2,1,0:T(8,128)(2,1)}), bf16[8,48,768]{2,1,0:T(8,128)(2,1)S(1)}, u32[]{:S(2)}, u32[]{:S(2)}) async-start(bf16[8,48,768]{2,1,0:T(8,128)(2,1)} %bitcast.130), calls=%async_computation.9 | async-start | bytes 1179648 | tf_op jit(solution)/shard_map/all_to_all | solution.py:512
  692.5 426.0 %reduce-scatter.33.cloned.1.call-start = ((), (), s32[]{:S(2)}) async-start(), calls=%async_computation.32 | async-start | bytes 1216512 | tf_op jit(solution)/shard_map/reduce_scatter | solution.py:519
  692.6 2.6 collective-permute-start.4
  695.1 523.8 %reduce-scatter.31.cloned.1.call-start = ((), (), s32[]{:S(2)}) async-start(), calls=%async_computation.31 | async-start | bytes 1216512 | tf_op jit(solution)/shard_map/reduce_scatter | solution.py:519
  743.8 233.2 %collective-permute-start.9 = (bf16[96,1536]{1,0:T(8,128)(2,1)}, bf16[96,1536]{1,0:T(8,128)(2,1)}, u32[]{:S(2)}, u32[]{:S(2)}) collective-permute-start(bf16[96,1536]{1,0:T(8,128)(2,1)} %reduce-scatter.29.cloned.1.call-done), channel_id=1, source_target_pairs={{0,0},{1,16},{16,1},{17,17},{2,2},{3,18},{18,3},{19,19},{4,4},{5,2... | collective-permute-start | bytes 884744 | tf_op jit(solution)/shard_map/ppermute | solution.py:379
  782.2 68.6 %collective-permute-start.7 = (f32[2,3,6]{2,1,0:T(4,128)S(1)}, f32[2,3,6]{2,1,0:T(4,128)S(1)}, u32[]{:S(2)}, u32[]{:S(2)}) collective-permute-start(f32[2,3,6]{2,1,0:T(4,128)S(1)} %psum.30), channel_id=1, source_target_pairs={{0,0},{1,16},{16,1},{17,17},{2,2},{3,18},{18,3},{19,19},{4,4},{5,2... | collective-permute-start | bytes 440 | tf_op jit(solution)/shard_map/ppermute | solution.py:379
  809.7 169.2 %all-to-all-start.2 = ((bf16[8,48,768]{2,1,0:T(8,128)(2,1)}), bf16[8,48,768]{2,1,0:T(8,128)(2,1)S(1)}, u32[]{:S(2)}, u32[]{:S(2)}) async-start(bf16[8,48,768]{2,1,0:T(8,128)(2,1)} %bitcast.129), calls=%async_computation.7 | async-start | bytes 1179648 | tf_op jit(solution)/shard_map/all_to_all | solution.py:512
  849.2 127.7 %collective-permute-start.8 = (bf16[96,1536]{1,0:T(8,128)(2,1)}, bf16[96,1536]{1,0:T(8,128)(2,1)S(1)}, u32[]{:S(2)}, u32[]{:S(2)}) collective-permute-start(bf16[96,1536]{1,0:T(8,128)(2,1)} %reduce-scatter.27.cloned.1.call-done), channel_id=1, source_target_pairs={{0,0},{1,16},{16,1},{17,17},{2,2},{3,18},{18,3},{19,19},{4,4},{5,2... | collective-permute-start | bytes 884744 | tf_op jit(solution)/shard_map/ppermute | solution.py:379
  1018.9 244.3 %copy-start.32 = (bf16[128,1536]{1,0:T(8,128)(2,1)S(1)}, bf16[128,1536]{1,0:T(8,128)(2,1)}, u32[]{:S(2)}) copy-start(bf16[128,1536]{1,0:T(8,128)(2,1)} %copy-done.31) | copy-start | bytes 1179652
  1021.0 242.1 %collective-permute-start.6 = (f32[128,1536]{1,0:T(8,128)}, f32[128,1536]{1,0:T(8,128)S(1)}, u32[]{:S(2)}, u32[]{:S(2)}) collective-permute-start(f32[128,1536]{1,0:T(8,128)} %fusion.22), channel_id=1, source_target_pairs={{0,0},{1,16},{16,1},{17,17},{2,2},{3,18},{18,3},{19,19},{4,4},{5,2... | collective-permute-start | bytes 2359304 | tf_op jit(solution)/shard_map/ppermute | solution.py:379
  (65 other events, 2879.3 us)
Sparse Core Ops, SparseCore 0:
  26.2 68.2 all-gather.24
  98.7 52.9 all-gather.12
  210.5 33.9 all-gather.14
  250.0 46.9 reduce-scatter.14
  298.7 67.8 all-gather.26
  368.6 28.3 all-gather.16
  398.9 38.8 all-gather.18
  443.5 44.7 reduce-scatter.16
  491.7 29.1 all-gather.20
  555.5 39.1 reduce-scatter.18
  603.9 24.9 all-gather.22
  631.9 57.0 reduce-scatter.24
  692.5 51.2 reduce-scatter.28
  746.7 63.0 reduce-scatter.22
  812.5 36.7 reduce-scatter.26
  854.7 119.5 all-reduce.6
  976.4 41.1 reduce-scatter.20
  1023.1 95.3 reduce-scatter.32
  1123.6 95.2 reduce-scatter.30

commit v2 on v1

v2 whole, which is shorter than its diff:
```python
import functools

import jax
import jax.numpy as jnp
from jax import lax
from jax.experimental import pallas as pl
from jax.experimental.pallas import tpu as pltpu
from jax.sharding import Mesh
from jax.sharding import PartitionSpec as P

HD = 64
NSTATE = 128
STRETCH = 256
DI = 3072
CONV = 4
LANES = 128
BC = 2 * NSTATE

eps = 1e-05

F32 = jnp.float32
BF16 = jnp.bfloat16
EXACT = lax.Precision.HIGHEST
CAP = 48 * 1024 * 1024


def mm(left, right):
    return jnp.dot(left, right, preferred_element_type=F32)


def mm_nt(left, right):
    return lax.dot_general(left, right, (((1,), (1,)), ((), ())), preferred_element_type=F32)


def mm_tn(left, right):
    return lax.dot_general(left, right, (((0,), (0,)), ((), ())), preferred_element_type=F32)


def mm_exact(left, right):
    return jnp.dot(left, right, precision=EXACT, preferred_element_type=F32)


def iota(shape, dim):
    return lax.broadcasted_iota(jnp.int32, shape, dim)


def head_spread(width):
    return (iota((LANES, width), 0) == iota((LANES, width), 1) // HD).astype(F32)


def head_fold(width):
    return (iota((width, LANES), 0) // HD == iota((width, LANES), 1)).astype(F32)


def own_steps(raw, turned):
    return pltpu.roll(raw.astype(F32), turned, 1)


def steps_of(raw, head_rows):
    shifted = raw + head_rows[0:1]
    step = jnp.maximum(shifted, 0.0) + jnp.log1p(jnp.exp(-jnp.abs(shifted)))
    return shifted, step


def take(ref, core):
    half = ref.shape[0] // 2
    first = ref[pl.ds(pl.multiple_of(core * half, half), half), :]
    second = ref[pl.ds(pl.multiple_of((1 - core) * half, half), half), :]
    return jnp.concatenate([first, second], axis=0)


def put(ref, core, values, start, end):
    half = ref.shape[0] // 2
    ref[pl.ds(pl.multiple_of(core * half, half), half), start:end] = values[:half]
    ref[pl.ds(pl.multiple_of((1 - core) * half, half), half), start:end] = values[half:]


def pairs(width):
    return [(at, min(at + LANES, width)) for at in range(0, width, LANES)]


def mix_forward_kernel(
    place_ref, proj_ref, conv_ref, head_ref, skip_ref, *refs, with_sums
):
    gated_ref, y_ref, enter_ref = refs[with_sums : with_sums + 3]
    state_ref, ext_ref = refs[-2:]
    core, turned = place_ref[0] & 1, place_ref[1]
    rows = proj_ref.shape[0]
    wide = gated_ref.shape[1]
    chans = wide + BC

    @pl.when(pl.program_id(0) == 0)
    def _():
        state_ref[...] = jnp.zeros_like(state_ref)
        ext_ref[0:8, :] = jnp.zeros((8, chans), F32)

    proj = take(proj_ref, core)
    ext_ref[8 : 8 + rows, :] = proj[:, wide : wide + chans].astype(F32)
    pre = conv_ref[CONV : CONV + 1, :] + conv_ref[0:1, :] * ext_ref[5 : 5 + rows, :]
    for lag in range(1, CONV):
        pre = pre + conv_ref[lag : lag + 1, :] * ext_ref[5 + lag : 5 + lag + rows, :]
    ext_ref[0:8, :] = ext_ref[rows : rows + 8, :]
    act = pre * jax.nn.sigmoid(pre)
    x = act[:, :wide]
    b_low = act[:, wide : wide + NSTATE].astype(BF16)
    c_low = act[:, wide + NSTATE :].astype(BF16)

    _, step = steps_of(own_steps(proj[:, wide + chans :], turned), head_ref)
    decay = -step * head_ref[1:2, :]
    lower = iota((rows, rows), 0) >= iota((rows, rows), 1)
    cum = mm_exact(lower.astype(F32), decay)
    cum_t = jnp.transpose(cum)
    spread = head_spread(wide)
    cum_wide = mm_exact(cum, spread)
    step_wide = mm_exact(step, spread)
    total = cum_wide[rows - 1 : rows, :]

    scores = mm_nt(c_low, b_low)
    weighted = x * step_wide
    weighted_low = weighted.astype(BF16)
    within = []
    for start, end in pairs(wide):
        both = weighted_low[:, start:end]
        parts = []
        for head in range(start // HD, end // HD):
            gap = cum[:, head : head + 1] - cum_t[head : head + 1, :]
            mixed = jnp.where(lower, jnp.exp(gap), 0.0) * scores
            parts.append(mm(mixed.astype(BF16), both))
        if len(parts) == 2:
            first = iota((rows, end - start), 1) < HD
            within.append(jnp.where(first, parts[0], parts[1]))
        else:
            within.append(parts[0])
    within = jnp.concatenate(within, axis=1)
    state = state_ref[...]
    enter_ref[0] = state
    carried = jnp.exp(cum_wide) * mm(c_low, state.astype(BF16))
    y = within + carried + skip_ref[0:1, :] * x
    gate = proj[:, :wide].astype(F32)
    gated = (y * (gate * jax.nn.sigmoid(gate))).astype(BF16)
    put(gated_ref, core, gated, 0, wide)
    if with_sums:
        gated = gated.astype(F32)
        ones = jnp.ones((8, wide), BF16)
        product = gated * take(refs[0], core).astype(F32)
        squares = mm_nt(ones, (gated * gated).astype(BF16))
        product = mm_nt(ones, product.astype(BF16))
        refs[4][...] = jnp.where(iota((8, rows), 0) == 0, squares, product)
    put(y_ref, core, y.astype(BF16), 0, wide)
    ending = (weighted * jnp.exp(total - cum_wide)).astype(BF16)
    state_ref[...] = state * jnp.exp(total) + mm_tn(b_low, ending)


def mix_forward(place, proj, conv_rows, head_rows, wide_rows, pulled=None):
    with_sums = pulled is not None
    length, width = proj.shape
    wide = wide_rows.shape[1]
    count = length // STRETCH
    whole = lambda shape: pl.BlockSpec(shape, lambda i, at: (0,) * len(shape))
    part = lambda cols: pl.BlockSpec((STRETCH, cols), lambda i, at: (i ^ (at[0] >> 1), 0))
    return pl.pallas_call(
        functools.partial(mix_forward_kernel, with_sums=with_sums),
        grid_spec=pltpu.PrefetchScalarGridSpec(
            num_scalar_prefetch=1,
            grid=(count,),
            in_specs=[
                part(width),
                whole(conv_rows.shape),
                whole(head_rows.shape),
                whole(wide_rows.shape),
            ]
            + [part(wide)] * with_sums,
            out_specs=[
                part(wide),
                part(wide),
                pl.BlockSpec((1, NSTATE, wide), lambda i, at: (i, 0, 0)),
            ]
            + [pl.BlockSpec((8, STRETCH), lambda i, at: (0, i))] * with_sums,
            scratch_shapes=[
                pltpu.VMEM((NSTATE, wide), F32),
                pltpu.VMEM((STRETCH + 8, wide + BC), F32),
            ],
        ),
        out_shape=[
            jax.ShapeDtypeStruct((length, wide), BF16),
            jax.ShapeDtypeStruct((length, wide), BF16),
            jax.ShapeDtypeStruct((count, NSTATE, wide), F32),
        ]
        + [jax.ShapeDtypeStruct((8, length), F32)] * with_sums,
        compiler_params=pltpu.CompilerParams(
            dimension_semantics=("arbitrary",), vmem_limit_bytes=CAP
        ),
        cost_estimate=pl.CostEstimate(
            flops=length * wide * 30000, bytes_accessed=length * 6000, transcendentals=0
        ),
        name="mix_forward",
    )(place, proj, conv_rows, head_rows, wide_rows, *[pulled] * with_sums)


def mix_backward_kernel(
    place_ref,
    proj_ref,
    before_ref,
    y_ref,
    pulled_ref,
    kappa_ref,
    enter_ref,
    conv_ref,
    head_ref,
    wide_ref,
    *refs,
    as_rows,
):
    out_ref, conv_grad_ref, head_grad_ref, skip_grad_ref = refs[:4]
    dstate_ref, ext_ref, gext_ref, rows_ref = refs[-4:]
    core, turned = place_ref[0] & 1, place_ref[1]
    rows = proj_ref.shape[0]
    wide = y_ref.shape[1]
    chans = wide + BC
    turn = pl.program_id(0)

    @pl.when(turn == 0)
    def _():
        dstate_ref[...] = jnp.zeros_like(dstate_ref)
        gext_ref[rows : rows + 8, :] = jnp.zeros((8, chans), F32)
        conv_grad_ref[...] = jnp.zeros_like(conv_grad_ref)
        head_grad_ref[...] = jnp.zeros_like(head_grad_ref)
        skip_grad_ref[...] = jnp.zeros_like(skip_grad_ref)
        rows_ref[...] = jnp.zeros_like(rows_ref)

    before = before_ref[8:16, wide : wide + chans].astype(F32)
    ext_ref[0:8, :] = jnp.where(turn == pl.num_programs(0) - 1, 0.0, before)
    proj = take(proj_ref, core)
    ext_ref[8 : 8 + rows, :] = proj[:, wide : wide + chans].astype(F32)
    pre = conv_ref[CONV : CONV + 1, :] + conv_ref[0:1, :] * ext_ref[5 : 5 + rows, :]
    for lag in range(1, CONV):
        pre = pre + conv_ref[lag : lag + 1, :] * ext_ref[5 + lag : 5 + lag + rows, :]
    sig = jax.nn.sigmoid(pre)
    act = pre * sig
    slope = sig * (1.0 + pre * (1.0 - sig))
    x = act[:, :wide]
    x_low = x.astype(BF16)
    b_low = act[:, wide : wide + NSTATE].astype(BF16)
    c_low = act[:, wide + NSTATE :].astype(BF16)

    shifted, step = steps_of(own_steps(proj[:, wide + chans :], turned), head_ref)
    rate = head_ref[1:2, :]
    decay = -step * rate
    lower = iota((rows, rows), 0) >= iota((rows, rows), 1)
    upper = iota((rows, rows), 0) <= iota((rows, rows), 1)
    cum = mm_exact(lower.astype(F32), decay)
    cum_t = jnp.transpose(cum)
    spread = head_spread(wide)
    fold = head_fold(wide)
    cum_wide = mm_exact(cum, spread)
    step_wide = mm_exact(step, spread)
    total = cum_wide[rows - 1 : rows, :]
    grown = jnp.exp(cum_wide)
    to_end = jnp.exp(total - cum_wide)

    gate = proj[:, :wide].astype(F32)
    y = take(y_ref, core).astype(F32)
    gate_sig = jax.nn.sigmoid(gate)
    gate_act = gate * gate_sig
    g_gated = take(pulled_ref, core).astype(F32)
    gated = y * gate_act
    if as_rows:
        sums = jnp.transpose(kappa_ref[...])
        rho = lax.rsqrt(sums[:, 0:1] / DI + eps)
        kappa = rho * rho * rho * sums[:, 1:2] / DI
        g_gated = rho * g_gated - gated * kappa
        put(refs[4], core, (gated * rho).astype(BF16), 0, wide)
    else:
        g_gated = g_gated - gated * take(kappa_ref, core)[:, 0:1].astype(F32)
    dy = g_gated * gate_act
    g_gate = g_gated * y * (gate_sig * (1.0 + gate * (1.0 - gate_sig)))
    put(out_ref, core, g_gate.astype(BF16), 0, wide)
    dy_low = dy.astype(BF16)
    skip_grad_ref[0:1, :] += jnp.sum(x * dy, axis=0, keepdims=True)

    scores_t = mm_nt(b_low, c_low)
    lane = iota((rows, LANES), 1)
    d_scores = jnp.zeros((rows, rows), F32)
    column = jnp.zeros((rows, LANES), F32)
    inner = []
    for start, end in pairs(wide):
        both_dy = dy_low[:, start:end]
        both_x = x_low[:, start:end]
        side = iota((rows, end - start), 1) // HD
        parts = []
        for head in range(start // HD, end // HD):
            gap = cum_t[head : head + 1, :] - cum[:, head : head + 1]
            fade = jnp.where(upper, jnp.exp(gap), 0.0)
            own = jnp.where(side == head - start // HD, both_x, jnp.zeros_like(both_x))
            faded = fade * mm_nt(own, both_dy)
            stepped = faded * step[:, head : head + 1]
            d_scores = d_scores + stepped
            parts.append(mm((scores_t * fade).astype(BF16), both_dy))
            column = jnp.where(
                lane == head, jnp.sum(scores_t * faded, axis=1, keepdims=True), column
            )
            rows_ref[head : head + 1, :] = jnp.sum(scores_t * stepped, axis=0, keepdims=True)
        if len(parts) == 2:
            inner.append(jnp.where(side == 0, parts[0], parts[1]))
        else:
            inner.append(parts[0])
    inner = jnp.concatenate(inner, axis=1)

    enter = enter_ref[0]
    enter_low = enter.astype(BF16)
    dstate = dstate_ref[...]
    dstate_low = dstate.astype(BF16)
    outer = to_end * mm(b_low, dstate_low)
    g_x = step_wide * (inner + outer) + wide_ref[0:1, :] * dy
    dy_grown = dy * grown
    dy_grown_low = dy_grown.astype(BF16)
    carried_sum = mm_exact(dy_grown * mm(c_low, enter_low), fold)
    outer_sum = mm_exact(x * outer, fold)
    state_sum = mm_exact(
        jnp.broadcast_to(jnp.sum(enter * dstate, axis=0, keepdims=True), (8, wide)), fold
    )[0:1, :]
    step_outer = step * outer_sum
    g_cum = jnp.transpose(rows_ref[...]) + carried_sum - step * column - step_outer
    g_total = (
        jnp.sum(step_outer, axis=0, keepdims=True)
        + jnp.exp(cum[rows - 1 : rows, :]) * state_sum
    )
    g_decay = mm_exact(upper.astype(F32), g_cum) + g_total
    scaled_decay = rate * g_decay
    g_raw = (column + outer_sum - scaled_decay) * jax.nn.sigmoid(shifted)
    head_grad_ref[0:1, :] += jnp.sum(g_raw, axis=0, keepdims=True)
    head_grad_ref[1:2, :] -= jnp.sum(step * scaled_decay, axis=0, keepdims=True)
    g_raw = pltpu.roll(g_raw, lax.rem(LANES - turned, LANES), 1)
    put(out_ref, core, g_raw.astype(BF16), wide + chans, wide + chans + LANES)

    d_low = d_scores.astype(BF16)
    ending = (x * (step_wide * to_end)).astype(BF16)
    g_b = mm(d_low, c_low) + mm_nt(ending, dstate_low)
    g_c = mm_tn(d_low, b_low) + mm_nt(dy_grown_low, enter_low)
    dstate_ref[...] = dstate * jnp.exp(total) + mm_tn(c_low, dy_grown_low)

    gext_ref[0:rows, :wide] = g_x * slope[:, :wide]
    gext_ref[0:rows, wide : wide + NSTATE] = g_b * slope[:, wide : wide + NSTATE]
    gext_ref[0:rows, wide + NSTATE :] = g_c * slope[:, wide + NSTATE :]
    g_pre = gext_ref[0:rows, :]
    g_in = conv_ref[CONV - 1 : CONV, :] * g_pre
    for lag in range(CONV - 1):
        g_in = g_in + conv_ref[lag : lag + 1, :] * gext_ref[3 - lag : 3 - lag + rows, :]
    put(out_ref, core, g_in.astype(BF16), wide, wide + chans)
    for lag in range(CONV):
        conv_grad_ref[lag : lag + 1, :] += jnp.sum(
            ext_ref[5 + lag : 5 + lag + rows, :] * g_pre, axis=0, keepdims=True
        )
    conv_grad_ref[CONV : CONV + 1, :] += jnp.sum(g_pre, axis=0, keepdims=True)
    gext_ref[rows : rows + 8, :] = gext_ref[0:8, :]


def mix_backward(place, proj, y, pulled, kappa, enter, conv_rows, head_rows, wide_rows, as_rows):
    length, width = proj.shape
    wide = wide_rows.shape[1]
    count = length // STRETCH
    whole = lambda shape: pl.BlockSpec(shape, lambda i, at: (0,) * len(shape))
    part = lambda cols: pl.BlockSpec((STRETCH, cols), lambda i, at: ((count - 1 - i) ^ (at[0] >> 1), 0))
    half = STRETCH // 2

    def last_rows(i, at):
        pair = jnp.maximum(count - 2 - i, 0) ^ (at[0] >> 1)
        block = 2 * pair + 1 - (at[0] & 1)
        return block * (half // 16) + half // 16 - 1, 0

    before = pl.BlockSpec((16, width), last_rows)
    turn = lambda i, at: (count - 1 - i) ^ (at[0] >> 1)
    if as_rows:
        scales = pl.BlockSpec((8, STRETCH), lambda i, at: (0, count - 1 - i))
    else:
        last = kappa.shape[1] // LANES - 1
        scales = pl.BlockSpec((STRETCH, LANES), lambda i, at: (turn(i, at), last))
    return pl.pallas_call(
        functools.partial(mix_backward_kernel, as_rows=as_rows),
        grid_spec=pltpu.PrefetchScalarGridSpec(
            num_scalar_prefetch=1,
            grid=(count,),
            in_specs=[
                part(width),
                before,
                part(wide),
                part(wide),
                scales,
                pl.BlockSpec((1, NSTATE, wide), lambda i, at: (count - 1 - i, 0, 0)),
                whole(conv_rows.shape),
                whole(head_rows.shape),
                whole(wide_rows.shape),
            ],
            out_specs=[
                part(width),
                whole((8, wide + BC)),
                whole((8, LANES)),
                whole((8, wide)),
            ]
            + [part(wide)] * as_rows,
            scratch_shapes=[
                pltpu.VMEM((NSTATE, wide), F32),
                pltpu.VMEM((STRETCH + 8, wide + BC), F32),
                pltpu.VMEM((STRETCH + 8, wide + BC), F32),
                pltpu.VMEM((LANES, STRETCH), F32),
            ],
        ),
        out_shape=[
            jax.ShapeDtypeStruct((length, width), BF16),
            jax.ShapeDtypeStruct((8, wide + BC), F32),
            jax.ShapeDtypeStruct((8, LANES), F32),
            jax.ShapeDtypeStruct((8, wide), F32),
        ]
        + [jax.ShapeDtypeStruct((length, wide), BF16)] * as_rows,
        compiler_params=pltpu.CompilerParams(
            dimension_semantics=("arbitrary",), vmem_limit_bytes=CAP
        ),
        cost_estimate=pl.CostEstimate(
            flops=length * wide * 66000, bytes_accessed=length * 9000, transcendentals=0
        ),
        name="mix_backward",
    )(place, proj, proj, y, pulled, kappa, enter, conv_rows, head_rows, wide_rows)


def add_low(*terms):
    total = terms[0].astype(F32)
    for term in terms[1:]:
        total = total + term.astype(F32)
    return total.astype(BF16)


def rms(values):
    return lax.rsqrt(jnp.mean(values * values, axis=-1, keepdims=True) + eps)


def after(values, *others):
    return lax.optimization_barrier((values, others))[0]


def flip(values, axis):
    return lax.ppermute(values, axis, [(0, 1), (1, 0)])


class Axes:
    def __init__(self, seq, fsdp):
        between = tuple(f"b{i}" for i in range((seq // 4).bit_length() - 1))
        before = tuple(f"p{i}" for i in range((fsdp // 2).bit_length() - 1))
        self.seq = ("a",) + between + ("c",)
        self.fsdp = before + ("q",)
        self.every = self.seq + self.fsdp
        self.links = ("a",) + between
        self.team = self.seq
        self.copies = self.fsdp

    def bits(self, names, at):
        value = 0
        for spot, name in enumerate(names):
            if at >> (len(names) - 1 - spot) & 1:
                value |= 1 << (len(self.every) - 1 - self.every.index(name))
        return value

    def at(self, me, r, k, relative):
        if relative:
            me = me ^ self.bits(self.copies, r)
        else:
            me = me & ~self.bits(self.copies, -1) | self.bits(self.copies, r)
        return me & ~self.bits(self.team, -1) | self.bits(self.team, k)


def all_vmem(count):
    return [pl.BlockSpec(memory_space=pltpu.VMEM)] * count


SMEM = pl.BlockSpec(memory_space=pltpu.SMEM)


def split_in(axes, weights, gain, spare, layer):
    team = 2 ** len(axes.team)
    depth, columns = weights.shape[1:]
    wide = DI // team
    parts = 2 + 3 * LANES // wide

    def kernel(weight_ref, gain_ref, spare_ref, out_ref):
        scale = gain_ref[...].astype(F32)
        tail = (weight_ref[0, :, 2 * DI :].astype(F32) * scale).astype(BF16)
        tail = jnp.concatenate([tail, spare_ref[...]], axis=1)
        for k in range(team):
            for part in range(2):
                base = (1 - part) * DI + k * wide
                cut = weight_ref[0, :, base : base + wide].astype(F32)
                out_ref[k, part] = (cut * scale).astype(BF16)
            for part in range(2, parts):
                out_ref[k, part] = tail[:, (part - 2) * wide : (part - 1) * wide]

    whole = lambda shape: pl.BlockSpec(shape, lambda i: (0,) * len(shape))
    return pl.pallas_call(
        kernel,
        grid=(1,),
        in_specs=[
            pl.BlockSpec((1, depth, columns), lambda i: (layer, 0, 0)),
            whole((depth, 1)),
            whole(spare.shape),
        ],
        out_specs=whole((team, parts, depth, wide)),
        out_shape=jax.ShapeDtypeStruct((team, parts, depth, wide), BF16),
        compiler_params=pltpu.CompilerParams(vmem_limit_bytes=CAP),
        name="split_in",
    )(weights, gain[:, None], spare)


def columns_of(part, wide):
    return (1 - part if part < 2 else part) * wide


def join_in(axes, place, lists, relative):
    copies, team = len(lists), 2 ** len(axes.team)
    parts = len(lists[0]) // team
    depth, wide = lists[0][0][0].shape[-2:]
    rows = copies * team * depth
    extra = min(depth, 32)
    if depth % 16:
        flat = jnp.stack([jnp.stack([array[index] for array, index in row]) for row in lists])
        flat = flat.reshape(copies * team, parts, depth, wide)
        flat = jnp.concatenate(
            [flat[:, 1], flat[:, 0]] + [flat[:, part] for part in range(2, parts)], axis=-1
        )
        at = [axes.at(place[2], r, k, relative) for r in range(copies) for k in range(team)]
        flat = jnp.zeros_like(flat).at[jnp.stack(at)].set(flat)
        return flat.reshape(rows, -1), flat[:, :extra, -LANES:]

    arrays = []
    for row in lists:
        for array, _ in row:
            if not any(array is known for known in arrays):
                arrays.append(array)
    which = lambda array: next(i for i, known in enumerate(arrays) if known is array)

    def kernel(place_ref, *refs):
        out_ref, spare_ref = refs[-2:]
        for r in range(copies):
            for k in range(team):
                spot = axes.at(place_ref[2], r, k, relative)
                at = pl.ds(pl.multiple_of(spot * depth, 16), depth)
                for part in range(parts):
                    array, index = lists[r][parts * k + part]
                    base = columns_of(part, wide)
                    out_ref[at, base : base + wide] = refs[which(array)][index]
                index = index if isinstance(index, tuple) else (index,)
                index += (slice(0, extra), slice(wide - LANES, wide))
                spare_ref[spot] = refs[which(array)][index]

    return pl.pallas_call(
        kernel,
        in_specs=[SMEM] + all_vmem(len(arrays)),
        out_specs=all_vmem(2),
        out_shape=[
            jax.ShapeDtypeStruct((rows, parts * wide), BF16),
            jax.ShapeDtypeStruct((copies * team, extra, LANES), BF16),
        ],
        compiler_params=pltpu.CompilerParams(vmem_limit_bytes=CAP),
        name="join_in",
    )(place, *arrays)


def cut_in(axes, place, grad, spare, depth, wide, relative):
    copies, team = 2 ** len(axes.copies), 2 ** len(axes.team)
    parts = grad.shape[1] // wide
    extra, room = spare.shape[1:]
    if depth % 16:
        flat = grad.reshape(copies * team, depth, -1).at[:, :extra, -room:].set(spare)
        at = [axes.at(place[2], r, k, relative) for r in range(copies) for k in range(team)]
        flat = jnp.take(flat, jnp.stack(at), axis=0)
        flat = [
            flat[:, :, columns_of(part, wide) : columns_of(part, wide) + wide]
            for part in range(parts)
        ]
        return jnp.stack(flat, axis=1).reshape(copies, team * parts, depth, wide)

    def kernel(place_ref, grad_ref, spare_ref, out_ref):
        for r in range(copies):
            for k in range(team):
                spot = axes.at(place_ref[2], r, k, relative)
                rows = pl.ds(pl.multiple_of(spot * depth, 16), depth)
                for part in range(parts):
                    base = columns_of(part, wide)
                    out_ref[r, parts * k + part] = grad_ref[rows, base : base + wide]
                out_ref[r, parts * k + parts - 1, 0:extra, wide - room :] = spare_ref[spot]

    return pl.pallas_call(
        kernel,
        in_specs=[SMEM] + all_vmem(2),
        out_specs=pl.BlockSpec(memory_space=pltpu.VMEM),
        out_shape=jax.ShapeDtypeStruct((copies, team * parts, depth, wide), BF16),
        compiler_params=pltpu.CompilerParams(vmem_limit_bytes=CAP),
        name="cut_in",
    )(place, grad, spare)


def finish_in(axes, grads, weight, gain):
    layers, depth, columns = weight.shape
    team = 2 ** len(axes.team)
    wide = DI // team
    parts = grads[0].shape[1]
    room = parts * wide - 2 * wide - (columns - 2 * DI)

    def kernel(weight_ref, gain_ref, *refs):
        grad_ref, sum_ref, spare_ref = refs[-3:]
        for layer in range(layers):
            blocks_ref = refs[layer]
            scale = gain_ref[layer].astype(F32)
            tails = []
            for part in range(2, parts):
                tail = blocks_ref[0, part].astype(F32)
                for k in range(1, team):
                    tail = tail + blocks_ref[k, part].astype(F32)
                tails.append(tail)
            tail = jnp.concatenate(tails, axis=1)
            spare_ref[layer] = tail[:, columns - 2 * DI :]
            tail = tail[:, : columns - 2 * DI]
            grad_ref[layer, :, 2 * DI :] = tail * scale
            total = jnp.sum(tail * weight_ref[layer, :, 2 * DI :].astype(F32), 1, keepdims=True)
            for k in range(team):
                for part in range(2):
                    values = blocks_ref[k, part].astype(F32)
                    base = (1 - part) * DI + k * wide
                    grad_ref[layer, :, base : base + wide] = values * scale
                    total = total + jnp.sum(
                        values * weight_ref[layer, :, base : base + wide].astype(F32),
                        1,
                        keepdims=True,
                    )
            sum_ref[layer] = jnp.broadcast_to(total, (depth, LANES))

    grads, sums, spares = pl.pallas_call(
        kernel,
        in_specs=all_vmem(2 + layers),
        out_specs=all_vmem(3),
        out_shape=[
            jax.ShapeDtypeStruct((layers, depth, columns), F32),
            jax.ShapeDtypeStruct((layers, depth, LANES), F32),
            jax.ShapeDtypeStruct((layers, depth, room), F32),
        ],
        compiler_params=pltpu.CompilerParams(vmem_limit_bytes=CAP),
        name="finish_in",
    )(weight, gain[..., None], *grads)
    return grads, sums[:, :, 0], spares


def copies_gather(axes, whole):
    slow, fast = axes.copies
    half = whole.shape[0] // 2
    one, two = flip(whole, fast), flip(whole, slow)
    corner = [flip(one[:half], slow), flip(two[half:], fast)]
    every = [(index,) for index in range(whole.shape[0])]
    lists = [[(array, at) for (at,) in every] for array in (whole, one, two)]
    return lists + [[(corner[at // half], at % half) for (at,) in every]]


def sum_start(axes, pieces):
    slow, fast = axes.copies
    half = pieces.shape[1] // 2
    corner = [flip(pieces[3, :half], slow), flip(pieces[3, half:], fast)]
    to_fast = jnp.concatenate([add_low(pieces[1, :half], corner[0]), pieces[1, half:]], axis=0)
    to_slow = jnp.concatenate([pieces[2, :half], add_low(pieces[2, half:], corner[1])], axis=0)
    return pieces[0], to_fast, to_slow


def sum_end(axes, parts):
    own, to_fast, to_slow = parts
    slow, fast = axes.copies
    return add_low(own, flip(to_fast, fast), flip(to_slow, slow))


def team_gather(axes, rows):
    if len(axes.links) != 2:
        whole = rows[None]
        for name in reversed(axes.links):
            whole = jnp.concatenate([whole, flip(whole, name)], axis=0)
        whole = jnp.stack([whole, flip(whole, "c")], axis=1)
        return [whole.reshape(-1, rows.shape[1])]
    far, near = axes.links
    half = rows.shape[0] // 2
    from_far, from_near = flip(rows, far), flip(rows, near)
    own = jnp.concatenate([rows, flip(rows, "c")], axis=0)
    corner = jnp.concatenate([flip(from_near[:half], far), flip(from_far[half:], near)], axis=0)
    sides = jnp.stack([from_near, from_far])
    sides = jnp.stack([sides, flip(sides, "c")], axis=1).reshape(-1, rows.shape[1])
    corner = jnp.concatenate([corner, flip(corner, "c")], axis=0)
    return [own, sides, corner]


def scatter_start(axes, product, rows):
    team = 2 ** len(axes.team)
    if len(axes.links) != 2:
        whole = product(0, team * rows).reshape(team // 2, 2, rows, -1)
        whole = add_low(whole[:, 0], flip(whole[:, 1], "c"))
        for name in axes.links[:-1]:
            half = whole.shape[0] // 2
            whole = add_low(whole[:half], flip(whole[half:], name))
        return whole[0], whole[1:]
    far, near = axes.links
    half = rows // 2
    corner = product(6 * rows, 8 * rows)
    corner = add_low(corner[:rows], flip(corner[rows:], "c"))
    sides = product(2 * rows, 6 * rows).reshape(2, 2, rows, -1)
    sides = add_low(sides[:, 0], flip(sides[:, 1], "c"))
    own = product(0, 2 * rows)
    own = add_low(own[:rows], flip(own[rows:], "c"))
    got_far, got_near = flip(corner[:half], far), flip(corner[half:], near)
    to_near = jnp.concatenate([add_low(sides[0, :half], got_far), sides[0, half:]], axis=0)
    to_far = jnp.concatenate([sides[1, :half], add_low(sides[1, half:], got_near)], axis=0)
    return own, to_near, to_far


def scatter_end(axes, parts):
    if len(axes.links) != 2:
        return parts[0].astype(F32) + flip(parts[1], axes.links[-1])[0].astype(F32)
    own, to_near, to_far = parts
    far, near = axes.links
    return own.astype(F32) + flip(to_near, near).astype(F32) + flip(to_far, far).astype(F32)


def team_scatter(axes, product, rows):
    return scatter_end(axes, scatter_start(axes, product, rows))


def local(
    axes,
    tokens,
    cotangent,
    norm_gain,
    in_weight,
    conv_kernel,
    conv_shift,
    dt_bias,
    a_log,
    skip_gain,
    gate_gain,
    out_weight,
):
    layers, depth, columns = in_weight.shape
    rows = tokens.shape[1]
    model = tokens.shape[2]
    heads = dt_bias.shape[1]
    wide = heads * HD
    team = 2 ** len(axes.team)
    copies = 2 ** len(axes.copies)
    me = lax.axis_index(axes.team)
    all_at = lax.axis_index(axes.every)
    place = jnp.stack([me, lax.rem(LANES - me * heads, LANES), all_at]).astype(jnp.int32)

    n_conv = conv_shift.shape[1]
    room = 3 * LANES - (columns - 2 * DI)
    cuts = [(at, min(at + room, n_conv)) for at in range(0, n_conv, room)]
    taps = CONV + 1
    conv = jnp.concatenate([conv_kernel, conv_shift[:, None]], axis=1).reshape(-1, n_conv)
    conv = [jnp.pad(conv[:, at:end], ((0, 0), (0, room - end + at))) for at, end in cuts]
    conv = jnp.concatenate(conv, axis=0)
    spare = jnp.pad(conv, ((0, depth - conv.shape[0]), (0, 0)))

    def team_swap(blocks):
        return lax.all_to_all(blocks, axes.team, split_axis=0, concat_axis=0)

    def in_blocks(layer, start):
        blocks = split_in(axes, in_weight, after(norm_gain[layer], start), spare, layer)
        return team_swap(blocks).reshape(-1, depth, wide)

    def in_columns(blocks, at_once):
        relative = at_once and len(axes.copies) == 2
        if relative:
            lists = copies_gather(axes, blocks)
        else:
            got = lax.all_gather(blocks, axes.copies)
            lists = [[(got, (r, k)) for k in range(blocks.shape[0])] for r in range(copies)]
        return join_in(axes, place, lists, relative)

    def out_rows(layer):
        mine = out_weight[layer].astype(F32) * gate_gain[layer].astype(F32)[:, None]
        return lax.all_gather(mine.astype(BF16), axes.copies, axis=0, tiled=True)

    blocks = in_blocks(0, tokens)
    parts = blocks.shape[0] // team
    weight_in, beside = in_columns(blocks, True)
    weight_out = out_rows(0)
    residual = after(tokens[0], blocks).astype(F32)

    conv = beside[:, : conv.shape[0], LANES - room :]
    conv = conv.reshape(-1, len(cuts), layers * taps, room).transpose(0, 2, 1, 3)
    conv = conv.reshape(-1, layers * taps, len(cuts) * room)[:, :, :n_conv]
    conv = conv.reshape(-1, layers, taps, n_conv)
    conv = conv.transpose(1, 2, 0, 3).reshape(layers, CONV + 1, -1).astype(F32)
    conv = jnp.pad(conv, ((0, 0), (0, 7 - CONV), (0, 0)))
    conv = jnp.concatenate(
        [lax.dynamic_slice_in_dim(conv, me * wide, wide, 2), conv[:, :, DI:]], axis=2
    )
    head = jnp.stack([dt_bias, a_log, skip_gain], axis=1)
    skip = jnp.pad(jnp.repeat(head[:, 2:], HD, axis=2), ((0, 0), (0, 7), (0, 0)))
    head = jnp.stack([head[:, 0], jnp.exp(head[:, 1])], axis=1)
    head = jnp.pad(head, ((0, 0), (0, 6), (0, LANES - heads)))

    records = []
    for layer in range(layers):
        rho = rms(residual)
        pieces = team_gather(axes, (residual * rho).astype(BF16))
        more = layer + 1 < layers
        if more:
            blocks = in_blocks(layer + 1, pieces[-1])
            cot_pieces = team_gather(axes, after(cotangent[0], blocks))
            g_scaled = None
        else:
            g_scaled = [mm_nt(piece, weight_out) for piece in cot_pieces]
            g_scaled = jnp.concatenate(g_scaled, axis=0).astype(BF16)
        proj = jnp.concatenate([mm(piece, weight_in).astype(BF16) for piece in pieces], axis=0)
        gated, y, enter, *sums = mix_forward(
            place, proj, conv[layer], head[layer], skip[layer], g_scaled
        )
        normed = jnp.concatenate(pieces, axis=0)
        records.append((residual, rho, normed, proj, gated, y, enter, weight_in, weight_out))
        if not more:
            break
        gated = after(gated, blocks, cot_pieces)

        def branch_rows(begin, end):
            cut = gated[begin:end]
            squares = jnp.sum(jnp.square(cut.astype(F32)), axis=1, keepdims=True)
            squares = jnp.broadcast_to(squares, (end - begin, LANES))
            return jnp.concatenate([mm(cut, weight_out), squares], axis=1).astype(BF16)

        got = team_scatter(axes, branch_rows, rows)
        branch = got[:, :model]
        gate_rho = lax.rsqrt(got[:, model : model + 1] / DI + eps)
        records[-1] += (branch, gate_rho)
        residual = residual + gate_rho * branch
        weight_in = in_columns(blocks, False)[0]
        weight_out = out_rows(layer + 1)

    in_grads, out_grads = [], []
    grad = cotangent[0].astype(F32)

    def spare_rows(g_conv, g_head, g_skip):
        g_conv = jnp.concatenate(
            [
                lax.dynamic_update_slice_in_dim(
                    jnp.zeros((taps, DI), F32), g_conv[:taps, :wide], me * wide, 1
                ),
                g_conv[:taps, wide:],
            ],
            axis=1,
        )
        g_conv = g_conv.reshape(taps, -1, n_conv).transpose(1, 0, 2)
        g_conv = [
            jnp.pad(g_conv[..., at:end], ((0, 0), (0, 0), (0, room - end + at)))
            for at, end in cuts
        ]
        g_head = jnp.stack(
            [g_head[0, :heads], g_head[1, :heads], jnp.sum(g_skip[0].reshape(heads, HD), 1)]
        )
        g_head = jnp.pad(g_head, ((0, 0), (0, room - heads)))
        sharers = team * copies // team
        owner = jnp.arange(team * copies) // sharers == me
        g_head = jnp.where(owner[:, None, None], g_head, 0.0)
        spare = jnp.concatenate(g_conv + [g_head], axis=1)
        more = -spare.shape[1] % 16 if depth % 16 == 0 else 0
        return jnp.pad(spare, ((0, 0), (0, more), (0, 0))).astype(BF16)

    for layer in reversed(range(layers)):
        last = layer == layers - 1
        if last:
            residual_in, rho, normed, proj, gated, y, enter, weight_in, weight_out = records[layer]
            pieces = cot_pieces
        else:
            (
                residual_in,
                rho,
                normed,
                proj,
                gated,
                y,
                enter,
                weight_in,
                weight_out,
                branch,
                gate_rho,
            ) = records[layer]
            pulled = grad * gate_rho
            kappa = gate_rho * gate_rho * jnp.sum(pulled * branch, axis=1, keepdims=True) / DI
            pulled = after(pulled, g_out, blocks)
            sent = jnp.concatenate([pulled, jnp.broadcast_to(kappa, (rows, LANES))], axis=1)
            pieces = team_gather(axes, sent.astype(BF16))
        got = jnp.concatenate(pieces, axis=0)
        if last:
            sums = sums[0]
            for name in axes.team:
                sums = sums + flip(sums, name)
            branch = scatter_start(
                axes, lambda begin, end: mm(gated[begin:end], weight_out).astype(BF16), rows
            )
            scales = after(sums, branch)
        else:
            g_scaled = [mm_nt(piece[:, :model], weight_out) for piece in pieces]
            g_scaled = jnp.concatenate(g_scaled, axis=0).astype(BF16)
            scales = after(got, summed)
        outs = mix_backward(
            place, proj, y, g_scaled, scales, enter, conv[layer], head[layer], skip[layer], last
        )
        g_proj, g_conv, g_head, g_skip = outs[:4]
        if last:
            branch = scatter_end(axes, branch)
            gate_rho = lax.dynamic_slice_in_dim(sums, me * rows, rows, 1)[0][:, None]
            out = (residual + lax.rsqrt(gate_rho / DI + eps) * branch).astype(BF16)
            g_proj = after(g_proj, branch)
        else:
            in_grads.insert(0, team_swap(summed.reshape(team, parts, depth, wide)))
            g_proj = after(g_proj, in_grads)
        g_in = mm_tn(normed, g_proj).astype(BF16)
        spare = spare_rows(g_conv, g_head, g_skip)
        quick = layer == 0 and len(axes.copies) == 2
        blocks = cut_in(axes, place, g_in, spare, depth, wide, quick)
        g_out = mm_tn(outs[4] if last else gated, after(got, g_proj)[:, :model]).astype(BF16)
        if layer == 0:
            g_proj = after(g_proj, blocks)
        weighed = scatter_start(
            axes, lambda begin, end: mm_nt(g_proj[begin:end], weight_in).astype(BF16), rows
        )
        if quick:
            summed = sum_end(axes, after(sum_start(axes, blocks), weighed))
        else:
            summed = lax.psum_scatter(blocks, axes.copies, scatter_dimension=0)
        weighed = scatter_end(axes, weighed)
        mean = jnp.mean(weighed * residual_in, axis=1, keepdims=True)
        grad = grad + rho * weighed - residual_in * (rho * rho * rho * mean)
        out_grads.insert(0, lax.psum_scatter(g_out, axes.copies, scatter_dimension=0, tiled=True))
    in_grads.insert(0, team_swap(after(summed, weighed).reshape(team, parts, depth, wide)))

    grad_in, grad_norm, spare = finish_in(axes, in_grads, in_weight, norm_gain)
    grad_out = jnp.stack(out_grads).astype(F32)
    grad_gate = jnp.sum(grad_out * out_weight.astype(F32), axis=2)
    grad_out = grad_out * gate_gain.astype(F32)[:, :, None]

    conv_grad = [
        spare[:, at * taps : (at + 1) * taps, : end - start] for at, (start, end) in enumerate(cuts)
    ]
    conv_grad = jnp.concatenate(conv_grad, axis=2)
    head_grad = spare[:, len(cuts) * taps : len(cuts) * taps + 3, :heads]
    return (
        out[None],
        grad[None],
        grad_norm,
        grad_in,
        conv_grad[:, :CONV],
        conv_grad[:, CONV],
        head_grad[:, 0],
        head_grad[:, 1],
        head_grad[:, 2],
        grad_gate,
        grad_out,
    )


def solution(mesh):
    axes = Axes(mesh.shape["seq"], mesh.shape["fsdp"])
    fine = Mesh(mesh.devices.reshape((2,) * len(axes.every)), axes.every)
    acts = P(axes.fsdp, axes.seq, None)
    flat = P(None, axes.every)
    rows = P(None, axes.every, None)
    taps = P(None, None, axes.every)
    head = P(None, axes.seq)
    return jax.shard_map(
        functools.partial(local, axes),
        mesh=fine,
        in_specs=(acts, acts, flat, rows, taps, flat, head, head, head, flat, rows),
        out_specs=(acts, acts, flat, rows, taps, flat, head, head, head, flat, rows),
        check_vma=False,
    )
```

time: 1280 us -> 600 us (0.47)
  blocking collectives: 388 us -> 0 us
  waiting for transfers between devices: 626 us -> 272 us
  starting transfers between devices: 21.9 us -> 77.8 us
  local copies, waits for them, and re-layouts: 63.2 us -> 39.5 us
  Pallas kernels: 62.2 us -> 85.3 us
    reduce_scatter x10 -> x2, waiting for transfers between devices: 452 us -> 0.25 us  [local(): lax.psum_scatter(g_out, axes.copies, scatter_dimension=0, tiled=True)]
    all_gather x3 -> x0, blocking collectives: 278 us -> none  [the longest x2 209 us: in_columns(): rest = lax.all_gather(mine[:, 2 * DI:], EVERY, axis=0, tiled=True)]
    ppermute x10 -> x67, waiting for transfers between devices: 0.03 us -> 230 us  [flip(): return lax.ppermute(values, axis, [(0, 1), (1, 0)])]
    psum x1 -> x0, waiting for transfers between devices: 123 us -> none  [local(): lax.psum((norm_all, conv_all, gate_all), EVERY)]
    psum x2 -> x0, blocking collectives: 74.4 us -> none  [the longest x1 40.6 us: local(): lax.psum((norm_all, conv_all, gate_all), EVERY)]
    all_gather x8 -> x3, waiting for transfers between devices: 51.8 us -> 0.02 us  [the longest x2 0.02 us: out_rows(): return lax.all_gather(mine.astype(BF16), axes.copies, axis=0, tiled=True)]
    ppermute x10 -> x67, starting transfers between devices: 12.8 us -> 56.6 us  [flip(): return lax.ppermute(values, axis, [(0, 1), (1, 0)])]
    all_to_all x2 -> x4, waiting for transfers between devices: 0.01 us -> 41.9 us  [team_swap(): return lax.all_to_all(blocks, axes.team, split_axis=0, concat_axis=0)]
  transfers between devices with their start and end apart: 31 -> 77, of which waited for: 15 -> 42; matrix products, arithmetic and copies ran while one was open for 8% -> 17% of each run, Pallas kernels for 3% -> 7%
where the time goes in v2:
time: 600 us; the launch traced here: 591 us
  waiting for transfers between devices  272 us (45%)
  Pallas kernels  85.3 us (14%)
  starting transfers between devices  77.8 us (13%)
  matrix products  61.7 us (10%)
  local copies, waits for them, and re-layouts  39.5 us (7%)
  other arithmetic  39 us (6%)
  between operations  16.3 us (3%)
    ppermute x67, waiting for transfers between devices, flip(): return lax.ppermute(values, axis, [(0, 1), (1, 0)])  230 us
    ppermute x67, starting transfers between devices, flip(): return lax.ppermute(values, axis, [(0, 1), (1, 0)])  56.6 us
    pallas_call x2, Pallas kernels, mix_backward(): pl.pallas_call(functools.partial(mix_backward_kernel, as_rows=as_rows), g...  46.9 us
    all_to_all x4, waiting for transfers between devices, team_swap(): return lax.all_to_all(blocks, axes.team, split_axis=0, concat_axis=0)  41.9 us
    unnamed x165, local copies, waits for them, and re-layouts  25.7 us
    dot_general x4, matrix products, mm_tn(): lax.dot_general(left, right, (((0,), (0,)), ((), ())), preferred_element_...  22.2 us
    pallas_call x2, Pallas kernels, mix_forward(): pl.pallas_call(functools.partial(mix_forward_kernel, with_sums=with_sums)...  21.1 us
    dot_general x12, matrix products, mm(): return jnp.dot(left, right, preferred_element_type=F32)  20.5 us
  transfers between devices with their start and end apart: 77, of which 42 were waited for; matrix products, arithmetic and copies ran while one was open for 17% of the time, Pallas kernels for 7%

profile of v2, /device:TPU:0, one launch (start us, length us, event | category | flops | bytes accessed | tf_op | source)
XLA Modules:
  0.0 591.5 jit_solution(16510473328586560724)
XLA Ops:
  11.9 6.5 %all-to-all-start = ((bf16[8,3,48,384]{3,2,1,0:T(8,128)(2,1)}), bf16[8,3,48,384]{3,2,1,0:T(8,128)(2,1)S(1)}, u32[]{:S(2)}, u32[]{:S(2)}) async-start(bf16[8,3,48,384]{3,2,1,0:T(8,128)(2,1)} %split_in.2), calls=%async_computation | async-start | bytes 1769472 | tf_op jit(solution)/shard_map/all_to_all | solution.py:762
  19.5 21.9 %all-to-all-done = bf16[8,3,48,384]{3,2,1,0:T(8,128)(2,1)S(1)} async-done(((bf16[8,3,48,384]{3,2,1,0:T(8,128)(2,1)}), bf16[8,3,48,384]{3,2,1,0:T(8,128)(2,1)S(1)}, u32[]{:S(2)}, u32[]{:S(2)}) %all-to-all-start) | async-done | bytes 884768 | tf_op jit(solution)/shard_map/all_to_all | solution.py:762
  47.7 14.0 %collective-permute-done.6 = bf16[128,1536]{1,0:T(8,128)(2,1)S(1)} collective-permute-done((bf16[128,1536]{1,0:T(8,128)(2,1)S(1)}, bf16[128,1536]{1,0:T(8,128)(2,1)S(1)}, u32[]{:S(2)}, u32[]{:S(2)}) %collective-permute-start.6) | collective-permute-done | bytes 393248 | tf_op jit(solution)/shard_map/ppermute | solution.py:441
  65.0 8.1 %collective-permute-done.9 = bf16[64,1536]{1,0:T(8,128)(2,1)S(1)} collective-permute-done((bf16[64,1536]{1,0:T(8,128)(2,1)S(1)}, bf16[64,1536]{1,0:T(8,128)(2,1)S(1)}, u32[]{:S(2)}, u32[]{:S(2)}) %collective-permute-start.9) | collective-permute-done | bytes 196640 | tf_op jit(solution)/shard_map/ppermute | solution.py:441
  85.1 4.2 all-to-all-start.1
  89.4 5.4 collective-permute-done.4.refs_4_
  101.1 4.2 convolution_convert_fusion.12
  115.7 15.8 %collective-permute-done.13 = bf16[128,1536]{1,0:T(8,128)(2,1)S(1)} collective-permute-done((bf16[128,1536]{1,0:T(8,128)(2,1)S(1)}, bf16[128,1536]{1,0:T(8,128)(2,1)S(1)}, u32[]{:S(2)}, u32[]{:S(2)}) %collective-permute-start.13) | collective-permute-done | bytes 393248 | tf_op jit(solution)/shard_map/ppermute | solution.py:441
  132.7 9.7 %mix_forward.2 = (bf16[1024,384]{1,0:T(8,128)(2,1)S(1)}, bf16[1024,384]{1,0:T(8,128)(2,1)S(1)}, f32[4,128,384]{2,1,0:T(8,128)S(1)}) custom-call(s32[3]{0:T(128)S(1)} %pad_add_fusion.place_ref, bf16[1024,1152]{1,0:T(8,128)(2,1)S(1)} %pad_maximum_fusion.proj_ref.before_ref, f32[8,640]{1,0:T(8,128)S(1)} %get-tuple-element.168.conv_ref, ...), custom_call_target="tpu_custom_call" | custom-call | flops 11796480000 | bytes 6144000 | tf_op jit(solution)/shard_map/mix_forward/pallas_call | solution.py:161
  150.4 5.2 collective-permute-done.16
  173.8 9.3 %collective-permute-done.21 = bf16[64,1664]{1,0:T(8,128)(2,1)S(1)} collective-permute-done((bf16[64,1664]{1,0:T(8,128)(2,1)S(1)}, bf16[64,1664]{1,0:T(8,128)(2,1)S(1)}, u32[]{:S(2)}, u32[]{:S(2)}) %collective-permute-start.21) | collective-permute-done | bytes 213024 | tf_op jit(solution)/shard_map/ppermute | solution.py:441
  187.3 17.8 %collective-permute-done.24 = bf16[128,1664]{1,0:T(8,128)(2,1)S(1)} collective-permute-done((bf16[128,1664]{1,0:T(8,128)(2,1)}, bf16[128,1664]{1,0:T(8,128)(2,1)S(1)}, u32[]{:S(2)}, u32[]{:S(2)}) %collective-permute-start.24) | collective-permute-done | bytes 426016 | tf_op jit(solution)/shard_map/ppermute | solution.py:441
  216.5 11.7 %collective-permute-done.27 = bf16[128,1536]{1,0:T(8,128)(2,1)S(1)} collective-permute-done((bf16[128,1536]{1,0:T(8,128)(2,1)}, bf16[128,1536]{1,0:T(8,128)(2,1)S(1)}, u32[]{:S(2)}, u32[]{:S(2)}) %collective-permute-start.27) | collective-permute-done | bytes 393248 | tf_op jit(solution)/shard_map/ppermute | solution.py:441
  233.8 7.0 %collective-permute-done.30 = bf16[64,1536]{1,0:T(8,128)(2,1)S(1)} collective-permute-done((bf16[64,1536]{1,0:T(8,128)(2,1)S(1)}, bf16[64,1536]{1,0:T(8,128)(2,1)S(1)}, u32[]{:S(2)}, u32[]{:S(2)}) %collective-permute-start.30) | collective-permute-done | bytes 196640 | tf_op jit(solution)/shard_map/ppermute | solution.py:441
  256.7 11.4 %mix_forward.3 = (bf16[1024,384]{1,0:T(8,128)(2,1)S(1)}, bf16[1024,384]{1,0:T(8,128)(2,1)S(1)}, f32[4,128,384]{2,1,0:T(8,128)S(1)}, f32[8,1024]{1,0:T(8,128)S(1)}) custom-call(s32[3]{0:T(128)S(1)} %pad_add_fusion.place_ref, bf16[1024,1152]{1,0:T(8,128)(2,1)S(1)} %pad_maximum_fusion.1.proj_ref.before_ref, f32[8,640]{1,0:T(8,128)S(1)} %get-tuple-element.167.conv_ref, ...), custom_call_target="tpu_custom_call" | custom-call | flops 11796480000 | bytes 6144000 | tf_op jit(solution)/shard_map/mix_forward/pallas_call | solution.py:161
  279.8 9.6 %collective-permute-done.38 = bf16[64,1536]{1,0:T(8,128)(2,1)S(1)} collective-permute-done((bf16[64,1536]{1,0:T(8,128)(2,1)S(1)}, bf16[64,1536]{1,0:T(8,128)(2,1)S(1)}, u32[]{:S(2)}, u32[]{:S(2)}) %collective-permute-start.38) | collective-permute-done | bytes 196640 | tf_op jit(solution)/shard_map/ppermute | solution.py:441
  294.1 15.4 %collective-permute-done.41 = bf16[128,1536]{1,0:T(8,128)(2,1)S(1)} collective-permute-done((bf16[128,1536]{1,0:T(8,128)(2,1)S(1)}, bf16[128,1536]{1,0:T(8,128)(2,1)S(1)}, u32[]{:S(2)}, u32[]{:S(2)}) %collective-permute-start.41) | collective-permute-done | bytes 393248 | tf_op jit(solution)/shard_map/ppermute | solution.py:441
  310.6 23.4 %mix_backward.2 = (bf16[1024,1152]{1,0:T(8,128)(2,1)S(1)}, f32[8,640]{1,0:T(8,128)S(1)}, f32[8,128]{1,0:T(8,128)S(1)}, f32[8,384]{1,0:T(8,128)S(1)}, bf16[1024,384]{1,0:T(8,128)(2,1)S(1)}) custom-call(s32[3]{0:T(128)S(1)} %pad_add_fusion.place_ref, bf16[1024,1152]{1,0:T(8,128)(2,1)} %copy-done.5, bf16[1024,1152]{1,0:T(8,128)(2,1)} %copy-done.5, ...), custom_call_target="tpu_custom_call" | custom-call | flops 25952256000 | bytes 9216000 | tf_op jit(solution)/shard_map/mix_backward/pallas_call | solution.py:378
  336.2 8.7 %convolution_convert_fusion.1.grad_ref = bf16[1536,1152]{1,0:T(8,128)(2,1)} fusion(bf16[1024,1536]{1,0:T(8,128)(2,1)} %constant_dynamic-update-slice_fusion.14, bf16[1024,1152]{1,0:T(8,128)(2,1)} %copy-done.10), kind=kOutput, calls=%fused_computation.1 | convolution fusion | flops 3625648128 | bytes 9043968 | tf_op jit(solution)/shard_map/dot_general | solution.py:36
  344.9 4.2 cut_in.2
  360.8 9.1 %collective-permute-done.45 = bf16[64,1536]{1,0:T(8,128)(2,1)S(1)} collective-permute-done((bf16[64,1536]{1,0:T(8,128)(2,1)S(1)}, bf16[64,1536]{1,0:T(8,128)(2,1)S(1)}, u32[]{:S(2)}, u32[]{:S(2)}) %collective-permute-start.45) | collective-permute-done | bytes 196640 | tf_op jit(solution)/shard_map/ppermute | solution.py:441
  376.6 14.3 %collective-permute-done.48 = bf16[128,1536]{1,0:T(8,128)(2,1)} collective-permute-done((bf16[128,1536]{1,0:T(8,128)(2,1)}, bf16[128,1536]{1,0:T(8,128)(2,1)}, u32[]{:S(2)}, u32[]{:S(2)}) %collective-permute-start.48) | collective-permute-done | bytes 393248 | tf_op jit(solution)/shard_map/ppermute | solution.py:441
  401.8 16.7 %collective-permute-done.50 = bf16[128,1664]{1,0:T(8,128)(2,1)S(1)} collective-permute-done((bf16[128,1664]{1,0:T(8,128)(2,1)S(1)}, bf16[128,1664]{1,0:T(8,128)(2,1)S(1)}, u32[]{:S(2)}, u32[]{:S(2)}) %collective-permute-start.50) | collective-permute-done | bytes 426016 | tf_op jit(solution)/shard_map/ppermute | solution.py:441
  421.5 8.3 %collective-permute-done.53 = bf16[64,1664]{1,0:T(8,128)(2,1)S(1)} collective-permute-done((bf16[64,1664]{1,0:T(8,128)(2,1)S(1)}, bf16[64,1664]{1,0:T(8,128)(2,1)S(1)}, u32[]{:S(2)}, u32[]{:S(2)}) %collective-permute-start.53) | collective-permute-done | bytes 213024 | tf_op jit(solution)/shard_map/ppermute | solution.py:441
  435.5 3.6 all-to-all-start.2
  441.6 23.5 %mix_backward.3 = (bf16[1024,1152]{1,0:T(8,128)(2,1)S(1)}, f32[8,640]{1,0:T(8,128)S(1)}, f32[8,128]{1,0:T(8,128)S(1)}, f32[8,384]{1,0:T(8,128)S(1)}) custom-call(s32[3]{0:T(128)S(1)} %pad_add_fusion.place_ref, bf16[1024,1152]{1,0:T(8,128)(2,1)} %copy-done.4, bf16[1024,1152]{1,0:T(8,128)(2,1)} %copy-done.4, bf16[1024,384]{1,0:T(8,128)(2,1)S(1)} %copy-done.15, ...), custom_call_target="tpu_custom_call" | custom-call | flops 25952256000 | bytes 9216000 | tf_op jit(solution)/shard_map/mix_backward/pallas_call | solution.py:378
  467.3 8.7 %convolution_convert_fusion.grad_ref = bf16[1536,1152]{1,0:T(8,128)(2,1)} fusion(bf16[1024,1536]{1,0:T(8,128)(2,1)} %copy-done.54, bf16[1024,1152]{1,0:T(8,128)(2,1)} %copy-done.12), kind=kOutput, calls=%fused_computation | convolution fusion | flops 3625648128 | bytes 9043968 | tf_op jit(solution)/shard_map/dot_general | solution.py:36
  492.4 7.5 %collective-permute-done.59 = bf16[64,1536]{1,0:T(8,128)(2,1)S(1)} collective-permute-done((bf16[64,1536]{1,0:T(8,128)(2,1)S(1)}, bf16[64,1536]{1,0:T(8,128)(2,1)S(1)}, u32[]{:S(2)}, u32[]{:S(2)}) %collective-permute-start.59) | collective-permute-done | bytes 196640 | tf_op jit(solution)/shard_map/ppermute | solution.py:441
  506.3 13.1 %collective-permute-done.62 = bf16[128,1536]{1,0:T(8,128)(2,1)S(1)} collective-permute-done((bf16[128,1536]{1,0:T(8,128)(2,1)S(1)}, bf16[128,1536]{1,0:T(8,128)(2,1)S(1)}, u32[]{:S(2)}, u32[]{:S(2)}) %collective-permute-start.62) | collective-permute-done | bytes 393248 | tf_op jit(solution)/shard_map/ppermute | solution.py:441
  526.0 20.7 %collective-permute-done.65 = bf16[24,48,384]{2,1,0:T(8,128)(2,1)} collective-permute-done((bf16[24,48,384]{2,1,0:T(8,128)(2,1)}, bf16[24,48,384]{2,1,0:T(8,128)(2,1)}, u32[]{:S(2)}, u32[]{:S(2)}) %collective-permute-start.65) | collective-permute-done | bytes 884768 | tf_op jit(solution)/shard_map/ppermute | solution.py:441
  550.3 6.3 %all-to-all-start.3 = ((bf16[8,3,48,384]{3,2,1,0:T(8,128)(2,1)}), bf16[8,3,48,384]{3,2,1,0:T(8,128)(2,1)S(1)}, u32[]{:S(2)}, u32[]{:S(2)}) async-start(bf16[8,3,48,384]{3,2,1,0:T(8,128)(2,1)} %bitcast.290), calls=%async_computation.3 | async-start | bytes 1769472 | tf_op jit(solution)/shard_map/all_to_all | solution.py:762
  562.7 17.0 %all-to-all-done.3.refs_0_ = bf16[8,3,48,384]{3,2,1,0:T(8,128)(2,1)S(1)} async-done(((bf16[8,3,48,384]{3,2,1,0:T(8,128)(2,1)}), bf16[8,3,48,384]{3,2,1,0:T(8,128)(2,1)S(1)}, u32[]{:S(2)}, u32[]{:S(2)}) %all-to-all-start.3) | async-done | bytes 884768 | tf_op jit(solution)/shard_map/all_to_all | solution.py:762
  (512 shorter events, 213.0 us)
Async XLA Ops:
  11.9 29.5 %all-to-all-start = ((bf16[8,3,48,384]{3,2,1,0:T(8,128)(2,1)}), bf16[8,3,48,384]{3,2,1,0:T(8,128)(2,1)S(1)}, u32[]{:S(2)}, u32[]{:S(2)}) async-start(bf16[8,3,48,384]{3,2,1,0:T(8,128)(2,1)} %split_in.2), calls=%async_computation | async-start | bytes 1769472 | tf_op jit(solution)/shard_map/all_to_all | solution.py:762
  18.4 146.4 %all-gather.4.cloned.1.call-start = ((), (), s32[]{:S(2)}) async-start(), calls=%async_computation.7 | async-start | bytes 1474560 | tf_op jit(solution)/shard_map/all_gather | solution.py:779
  19.5 192.4 %all-gather.8.cloned.1.call-start = ((), (), s32[]{:S(2)}) async-start(), calls=%async_computation.9 | async-start | bytes 1474560 | tf_op jit(solution)/shard_map/all_gather | solution.py:779
  42.5 19.1 %collective-permute-start.6 = (bf16[128,1536]{1,0:T(8,128)(2,1)S(1)}, bf16[128,1536]{1,0:T(8,128)(2,1)S(1)}, u32[]{:S(2)}, u32[]{:S(2)}) collective-permute-start(bf16[128,1536]{1,0:T(8,128)(2,1)S(1)} %get-tuple-element.93), channel_id=1, source_target_pairs={{0,16},{16,0},{1,17},{17,1},{2,18},{18,2},{3,19},{19,3},{4,20},{20... | collective-permute-start | bytes 1179656 | tf_op jit(solution)/shard_map/ppermute | solution.py:441
  42.5 19.3 %collective-permute-start.5 = (bf16[128,1536]{1,0:T(8,128)(2,1)S(1)}, bf16[128,1536]{1,0:T(8,128)(2,1)S(1)}, u32[]{:S(2)}, u32[]{:S(2)}) collective-permute-start(bf16[128,1536]{1,0:T(8,128)(2,1)S(1)} %get-tuple-element.93), channel_id=1, source_target_pairs={{0,8},{8,0},{1,9},{9,1},{2,10},{10,2},{3,11},{11,3},{4,12},{12,4},... | collective-permute-start | bytes 1179656 | tf_op jit(solution)/shard_map/ppermute | solution.py:441
  44.6 30.3 %collective-permute-start.2 = (bf16[24,48,384]{2,1,0:T(8,128)(2,1)S(1)}, bf16[24,48,384]{2,1,0:T(8,128)(2,1)S(1)}, u32[]{:S(2)}, u32[]{:S(2)}) collective-permute-start(bf16[24,48,384]{2,1,0:T(8,128)(2,1)S(1)} %bitcast.270), channel_id=1, source_target_pairs={{0,2},{2,0},{1,3},{3,1},{4,6},{6,4},{5,7},{7,5},{8,10},{10,8},{9,1... | collective-permute-start | bytes 2654216 | tf_op jit(solution)/shard_map/ppermute | solution.py:441
  46.2 31.0 %collective-permute-start.1 = (bf16[24,48,384]{2,1,0:T(8,128)(2,1)S(1)}, bf16[24,48,384]{2,1,0:T(8,128)(2,1)S(1)}, u32[]{:S(2)}, u32[]{:S(2)}) collective-permute-start(bf16[24,48,384]{2,1,0:T(8,128)(2,1)S(1)} %bitcast.271), channel_id=1, source_target_pairs={{0,1},{1,0},{2,3},{3,2},{4,5},{5,4},{6,7},{7,6},{8,9},{9,8},{10,11... | collective-permute-start | bytes 2654216 | tf_op jit(solution)/shard_map/ppermute | solution.py:441
  85.1 27.3 %all-to-all-start.1 = ((bf16[8,3,48,384]{3,2,1,0:T(8,128)(2,1)}), bf16[8,3,48,384]{3,2,1,0:T(8,128)(2,1)}, u32[]{:S(2)}, u32[]{:S(2)}) async-start(bf16[8,3,48,384]{3,2,1,0:T(8,128)(2,1)} %split_in.3), calls=%async_computation.1 | async-start | bytes 1769472 | tf_op jit(solution)/shard_map/all_to_all | solution.py:762
  89.3 157.4 %all-gather.6.cloned.1.call-start = ((), (), s32[]{:S(2)}) async-start(), calls=%async_computation.8 | async-start | bytes 4423680 | tf_op jit(solution)/shard_map/all_gather | solution.py:773
  112.4 19.3 %collective-permute-start.12 = (bf16[128,1536]{1,0:T(8,128)(2,1)S(1)}, bf16[128,1536]{1,0:T(8,128)(2,1)S(1)}, u32[]{:S(2)}, u32[]{:S(2)}) collective-permute-start(bf16[128,1536]{1,0:T(8,128)(2,1)S(1)} %bitcast.292), channel_id=1, source_target_pairs={{0,8},{8,0},{1,9},{9,1},{2,10},{10,2},{3,11},{11,3},{4,12},{12,4},... | collective-permute-start | bytes 1179656 | tf_op jit(solution)/shard_map/ppermute | solution.py:441
  115.7 33.7 %collective-permute-start.11 = (bf16[128,1536]{1,0:T(8,128)(2,1)S(1)}, bf16[128,1536]{1,0:T(8,128)(2,1)}, u32[]{:S(2)}, u32[]{:S(2)}) collective-permute-start(bf16[128,1536]{1,0:T(8,128)(2,1)S(1)} %bitcast.293), channel_id=1, source_target_pairs={{0,4},{4,0},{1,5},{5,1},{2,6},{6,2},{3,7},{7,3},{8,12},{12,8},{9,1... | collective-permute-start | bytes 1179656 | tf_op jit(solution)/shard_map/ppermute | solution.py:441
  132.7 26.5 %collective-permute-start.14 = (bf16[2,128,1536]{2,1,0:T(8,128)(2,1)}, bf16[2,128,1536]{2,1,0:T(8,128)(2,1)}, u32[]{:S(2)}, u32[]{:S(2)}) collective-permute-start(bf16[2,128,1536]{2,1,0:T(8,128)(2,1)} %get-tuple-element.131), channel_id=1, source_target_pairs={{0,4},{4,0},{1,5},{5,1},{2,6},{6,2},{3,7},{7,3},{8,12},{12,8},{9,1... | collective-permute-start | bytes 2359304 | tf_op jit(solution)/shard_map/ppermute | solution.py:441
  144.2 291.3 %reduce-scatter.10.cloned.1.call-start = ((), (), s32[]{:S(2)}) async-start(), calls=%async_computation.12 | async-start | bytes 4423680
  184.3 20.9 %collective-permute-start.24 = (bf16[128,1664]{1,0:T(8,128)(2,1)}, bf16[128,1664]{1,0:T(8,128)(2,1)S(1)}, u32[]{:S(2)}, u32[]{:S(2)}) collective-permute-start(bf16[128,1664]{1,0:T(8,128)(2,1)} %pad_maximum_fusion.27), channel_id=1, source_target_pairs={{0,16},{16,0},{1,17},{17,1},{2,18},{18,2},{3,19},{19,3},{4,20},{20... | collective-permute-start | bytes 1277960 | tf_op jit(solution)/shard_map/ppermute | solution.py:441
  185.4 20.9 %collective-permute-start.22 = (bf16[128,1664]{1,0:T(8,128)(2,1)}, bf16[128,1664]{1,0:T(8,128)(2,1)}, u32[]{:S(2)}, u32[]{:S(2)}) collective-permute-start(bf16[128,1664]{1,0:T(8,128)(2,1)} %pad_maximum_fusion.26), channel_id=1, source_target_pairs={{0,8},{8,0},{1,9},{9,1},{2,10},{10,2},{3,11},{11,3},{4,12},{12,4},... | collective-permute-start | bytes 1277960 | tf_op jit(solution)/shard_map/ppermute | solution.py:441
  270.0 24.1 %collective-permute-start.35 = (bf16[128,1536]{1,0:T(8,128)(2,1)S(1)}, bf16[128,1536]{1,0:T(8,128)(2,1)S(1)}, u32[]{:S(2)}, u32[]{:S(2)}) collective-permute-start(bf16[128,1536]{1,0:T(8,128)(2,1)S(1)} %slice.533), channel_id=1, source_target_pairs={{0,4},{4,0},{1,5},{5,1},{2,6},{6,2},{3,7},{7,3},{8,12},{12,8},{9,1... | collective-permute-start | bytes 1179656 | tf_op jit(solution)/shard_map/ppermute | solution.py:441
  289.5 20.0 %collective-permute-start.41 = (bf16[128,1536]{1,0:T(8,128)(2,1)S(1)}, bf16[128,1536]{1,0:T(8,128)(2,1)S(1)}, u32[]{:S(2)}, u32[]{:S(2)}) collective-permute-start(bf16[128,1536]{1,0:T(8,128)(2,1)S(1)} %pad_maximum_fusion.34), channel_id=1, source_target_pairs={{0,16},{16,0},{1,17},{17,1},{2,18},{18,2},{3,19},{19,3},{4,20},{20... | collective-permute-start | bytes 1179656 | tf_op jit(solution)/shard_map/ppermute | solution.py:441
  290.2 19.4 %collective-permute-start.39 = (bf16[128,1536]{1,0:T(8,128)(2,1)S(1)}, bf16[128,1536]{1,0:T(8,128)(2,1)S(1)}, u32[]{:S(2)}, u32[]{:S(2)}) collective-permute-start(bf16[128,1536]{1,0:T(8,128)(2,1)S(1)} %pad_maximum_fusion.33), channel_id=1, source_target_pairs={{0,8},{8,0},{1,9},{9,1},{2,10},{10,2},{3,11},{11,3},{4,12},{12,4},... | collective-permute-start | bytes 1179656 | tf_op jit(solution)/shard_map/ppermute | solution.py:441
  349.1 210.1 %reduce-scatter.8.cloned.1.call-start = ((), (), s32[]{:S(2)}) async-start(), calls=%async_computation.11 | async-start | bytes 1474560 | tf_op jit(solution)/shard_map/reduce_scatter | solution.py:932
  353.6 23.0 %collective-permute-start.42 = (bf16[128,1536]{1,0:T(8,128)(2,1)}, bf16[128,1536]{1,0:T(8,128)(2,1)S(1)}, u32[]{:S(2)}, u32[]{:S(2)}) collective-permute-start(bf16[128,1536]{1,0:T(8,128)(2,1)} %slice.545), channel_id=1, source_target_pairs={{0,4},{4,0},{1,5},{5,1},{2,6},{6,2},{3,7},{7,3},{8,12},{12,8},{9,1... | collective-permute-start | bytes 1179656 | tf_op jit(solution)/shard_map/ppermute | solution.py:441
  370.9 20.0 %collective-permute-start.48 = (bf16[128,1536]{1,0:T(8,128)(2,1)}, bf16[128,1536]{1,0:T(8,128)(2,1)}, u32[]{:S(2)}, u32[]{:S(2)}) collective-permute-start(bf16[128,1536]{1,0:T(8,128)(2,1)} %pad_maximum_fusion.36), channel_id=1, source_target_pairs={{0,16},{16,0},{1,17},{17,1},{2,18},{18,2},{3,19},{19,3},{4,20},{20... | collective-permute-start | bytes 1179656 | tf_op jit(solution)/shard_map/ppermute | solution.py:441
  372.0 19.8 %collective-permute-start.46 = (bf16[128,1536]{1,0:T(8,128)(2,1)}, bf16[128,1536]{1,0:T(8,128)(2,1)}, u32[]{:S(2)}, u32[]{:S(2)}) collective-permute-start(bf16[128,1536]{1,0:T(8,128)(2,1)} %pad_maximum_fusion.35), channel_id=1, source_target_pairs={{0,8},{8,0},{1,9},{9,1},{2,10},{10,2},{3,11},{11,3},{4,12},{12,4},... | collective-permute-start | bytes 1179656 | tf_op jit(solution)/shard_map/ppermute | solution.py:441
  399.3 19.1 %collective-permute-start.50 = (bf16[128,1664]{1,0:T(8,128)(2,1)S(1)}, bf16[128,1664]{1,0:T(8,128)(2,1)S(1)}, u32[]{:S(2)}, u32[]{:S(2)}) collective-permute-start(bf16[128,1664]{1,0:T(8,128)(2,1)S(1)} %get-tuple-element.139), channel_id=1, source_target_pairs={{0,8},{8,0},{1,9},{9,1},{2,10},{10,2},{3,11},{11,3},{4,12},{12,4},... | collective-permute-start | bytes 1277960 | tf_op jit(solution)/shard_map/ppermute | solution.py:441
  399.3 20.9 %collective-permute-start.51 = (bf16[128,1664]{1,0:T(8,128)(2,1)S(1)}, bf16[128,1664]{1,0:T(8,128)(2,1)S(1)}, u32[]{:S(2)}, u32[]{:S(2)}) collective-permute-start(bf16[128,1664]{1,0:T(8,128)(2,1)S(1)} %get-tuple-element.139), channel_id=1, source_target_pairs={{0,16},{16,0},{1,17},{17,1},{2,18},{18,2},{3,19},{19,3},{4,20},{20... | collective-permute-start | bytes 1277960 | tf_op jit(solution)/shard_map/ppermute | solution.py:441
  401.7 28.9 %collective-permute-start.49 = (bf16[128,1664]{1,0:T(8,128)(2,1)S(1)}, bf16[128,1664]{1,0:T(8,128)(2,1)S(1)}, u32[]{:S(2)}, u32[]{:S(2)}) collective-permute-start(bf16[128,1664]{1,0:T(8,128)(2,1)S(1)} %get-tuple-element.139), channel_id=1, source_target_pairs={{0,4},{4,0},{1,5},{5,1},{2,6},{6,2},{3,7},{7,3},{8,12},{12,8},{9,1... | collective-permute-start | bytes 1277960 | tf_op jit(solution)/shard_map/ppermute | solution.py:441
  435.5 31.8 %all-to-all-start.2 = ((bf16[8,3,48,384]{3,2,1,0:T(8,128)(2,1)}), bf16[8,3,48,384]{3,2,1,0:T(8,128)(2,1)S(1)}, u32[]{:S(2)}, u32[]{:S(2)}) async-start(bf16[8,3,48,384]{3,2,1,0:T(8,128)(2,1)} %bitcast.307), calls=%async_computation.2 | async-start | bytes 1769472 | tf_op jit(solution)/shard_map/all_to_all | solution.py:762
  439.1 120.4 %reduce-scatter.6.cloned.1.call-start = ((), (), s32[]{:S(2)}) async-start(), calls=%async_computation.10 | async-start | bytes 1474560 | tf_op jit(solution)/shard_map/reduce_scatter | solution.py:932
  486.0 20.4 %collective-permute-start.56 = (bf16[128,1536]{1,0:T(8,128)(2,1)S(1)}, bf16[128,1536]{1,0:T(8,128)(2,1)S(1)}, u32[]{:S(2)}, u32[]{:S(2)}) collective-permute-start(bf16[128,1536]{1,0:T(8,128)(2,1)S(1)} %slice.564), channel_id=1, source_target_pairs={{0,4},{4,0},{1,5},{5,1},{2,6},{6,2},{3,7},{7,3},{8,12},{12,8},{9,1... | collective-permute-start | bytes 1179656 | tf_op jit(solution)/shard_map/ppermute | solution.py:441
  500.1 19.3 %collective-permute-start.62 = (bf16[128,1536]{1,0:T(8,128)(2,1)S(1)}, bf16[128,1536]{1,0:T(8,128)(2,1)S(1)}, u32[]{:S(2)}, u32[]{:S(2)}) collective-permute-start(bf16[128,1536]{1,0:T(8,128)(2,1)S(1)} %pad_maximum_fusion.38), channel_id=1, source_target_pairs={{0,16},{16,0},{1,17},{17,1},{2,18},{18,2},{3,19},{19,3},{4,20},{20... | collective-permute-start | bytes 1179656 | tf_op jit(solution)/shard_map/ppermute | solution.py:441
  520.8 26.0 %collective-permute-start.65 = (bf16[24,48,384]{2,1,0:T(8,128)(2,1)}, bf16[24,48,384]{2,1,0:T(8,128)(2,1)}, u32[]{:S(2)}, u32[]{:S(2)}) collective-permute-start(bf16[24,48,384]{2,1,0:T(8,128)(2,1)} %get-tuple-element.80), channel_id=1, source_target_pairs={{0,1},{1,0},{2,3},{3,2},{4,5},{5,4},{6,7},{7,6},{8,9},{9,8},{10,11... | collective-permute-start | bytes 2654216 | tf_op jit(solution)/shard_map/ppermute | solution.py:441
  522.0 25.6 %collective-permute-start.66 = (bf16[24,48,384]{2,1,0:T(8,128)(2,1)}, bf16[24,48,384]{2,1,0:T(8,128)(2,1)}, u32[]{:S(2)}, u32[]{:S(2)}) collective-permute-start(bf16[24,48,384]{2,1,0:T(8,128)(2,1)} %get-tuple-element.81), channel_id=1, source_target_pairs={{0,2},{2,0},{1,3},{3,1},{4,6},{6,4},{5,7},{7,5},{8,10},{10,8},{9,1... | collective-permute-start | bytes 2654216 | tf_op jit(solution)/shard_map/ppermute | solution.py:441
  550.3 29.4 %all-to-all-start.3 = ((bf16[8,3,48,384]{3,2,1,0:T(8,128)(2,1)}), bf16[8,3,48,384]{3,2,1,0:T(8,128)(2,1)S(1)}, u32[]{:S(2)}, u32[]{:S(2)}) async-start(bf16[8,3,48,384]{3,2,1,0:T(8,128)(2,1)} %bitcast.290), calls=%async_computation.3 | async-start | bytes 1769472 | tf_op jit(solution)/shard_map/all_to_all | solution.py:762
  (120 other events, 1206.7 us)
Sparse Core Ops, SparseCore 0:
  21.1 32.0 all-gather.3
  55.0 37.4 all-gather.7
  144.4 45.5 all-gather.5
  349.2 45.2 reduce-scatter.9
  401.8 26.4 reduce-scatter.7
  526.2 33.3 reduce-scatter.5

commit v3 on v2

--- a/solution.py
+++ b/solution.py
@@ -38,6 +38,23 @@
 
 def mm_exact(left, right):
     return jnp.dot(left, right, precision=EXACT, preferred_element_type=F32)
+
+
+def mm_low(left, right):
+    return mm(left.astype(BF16), right.astype(BF16))
+
+
+def mm_thirds(ones, right):
+    lane = iota(right.shape, 1)
+    high = right.astype(BF16).astype(F32)
+    left = right - high
+    middle = left.astype(BF16).astype(F32)
+    low = left - middle
+    packed = jnp.where(lane < 64, pltpu.roll(middle, 32, 1), pltpu.roll(low, 64, 1))
+    packed = jnp.where(lane < 32, high, jnp.where(lane < 96, packed, 0.0))
+    total = mm_low(ones, packed)
+    total = total + pltpu.roll(total, 96, 1) + pltpu.roll(total, 64, 1)
+    return jnp.where(lane < 32, total, 0.0)
 
 
 def iota(shape, dim):
@@ -108,12 +125,14 @@
     _, step = steps_of(own_steps(proj[:, wide + chans :], turned), head_ref)
     decay = -step * head_ref[1:2, :]
     lower = iota((rows, rows), 0) >= iota((rows, rows), 1)
-    cum = mm_exact(lower.astype(F32), decay)
+    cum = mm_thirds(lower.astype(F32), decay)
     cum_t = jnp.transpose(cum)
     spread = head_spread(wide)
-    cum_wide = mm_exact(cum, spread)
-    step_wide = mm_exact(step, spread)
-    total = cum_wide[rows - 1 : rows, :]
+    total = cum[rows - 1 : rows, :]
+    step_wide = mm_low(step, spread)
+    grown = mm_low(jnp.exp(cum), spread)
+    ending_wide = mm_low(step * jnp.exp(total - cum), spread)
+    kept = mm_exact(jnp.broadcast_to(jnp.exp(total), (8, LANES)), spread)[0:1, :]
 
     scores = mm_nt(c_low, b_low)
     weighted = x * step_wide
@@ -134,12 +153,14 @@
     within = jnp.concatenate(within, axis=1)
     state = state_ref[...]
     enter_ref[0] = state
-    carried = jnp.exp(cum_wide) * mm(c_low, state.astype(BF16))
+    carried = grown * mm(c_low, state.astype(BF16))
     y = within + carried + skip_ref[0:1, :] * x
     gate = proj[:, :wide].astype(F32)
     gated = (y * (gate * jax.nn.sigmoid(gate))).astype(BF16)
-    put(gated_ref, core, gated, 0, wide)
-    if with_sums:
+    if not with_sums:
+        put(gated_ref, core, gated, 0, wide)
+    else:
+        gated_ref[...] = gated
         gated = gated.astype(F32)
         ones = jnp.ones((8, wide), BF16)
         product = gated * take(refs[0], core).astype(F32)
@@ -147,8 +168,7 @@
         product = mm_nt(ones, product.astype(BF16))
         refs[4][...] = jnp.where(iota((8, rows), 0) == 0, squares, product)
     put(y_ref, core, y.astype(BF16), 0, wide)
-    ending = (weighted * jnp.exp(total - cum_wide)).astype(BF16)
-    state_ref[...] = state * jnp.exp(total) + mm_tn(b_low, ending)
+    state_ref[...] = state * kept + mm_tn(b_low, (x * ending_wide).astype(BF16))
 
 
 def mix_forward(place, proj, conv_rows, head_rows, wide_rows, pulled=None):
@@ -158,6 +178,7 @@
     count = length // STRETCH
     whole = lambda shape: pl.BlockSpec(shape, lambda i, at: (0,) * len(shape))
     part = lambda cols: pl.BlockSpec((STRETCH, cols), lambda i, at: (i ^ (at[0] >> 1), 0))
+    plain = pl.BlockSpec((STRETCH, wide), lambda i, at: (i, 0))
     return pl.pallas_call(
         functools.partial(mix_forward_kernel, with_sums=with_sums),
         grid_spec=pltpu.PrefetchScalarGridSpec(
@@ -171,7 +192,7 @@
             ]
             + [part(wide)] * with_sums,
             out_specs=[
-                part(wide),
+                plain if with_sums else part(wide),
                 part(wide),
                 pl.BlockSpec((1, NSTATE, wide), lambda i, at: (i, 0, 0)),
             ]
@@ -191,7 +212,7 @@
             dimension_semantics=("arbitrary",), vmem_limit_bytes=CAP
         ),
         cost_estimate=pl.CostEstimate(
-            flops=length * wide * 30000, bytes_accessed=length * 6000, transcendentals=0
+            flops=length * wide * 18000, bytes_accessed=length * 6000, transcendentals=0
         ),
         name="mix_forward",
     )(place, proj, conv_rows, head_rows, wide_rows, *[pulled] * with_sums)
@@ -248,29 +269,30 @@
     decay = -step * rate
     lower = iota((rows, rows), 0) >= iota((rows, rows), 1)
     upper = iota((rows, rows), 0) <= iota((rows, rows), 1)
-    cum = mm_exact(lower.astype(F32), decay)
+    cum = mm_thirds(lower.astype(F32), decay)
     cum_t = jnp.transpose(cum)
     spread = head_spread(wide)
     fold = head_fold(wide)
-    cum_wide = mm_exact(cum, spread)
-    step_wide = mm_exact(step, spread)
-    total = cum_wide[rows - 1 : rows, :]
-    grown = jnp.exp(cum_wide)
-    to_end = jnp.exp(total - cum_wide)
+    total = cum[rows - 1 : rows, :]
+    step_wide = mm_low(step, spread)
+    grown = mm_low(jnp.exp(cum), spread)
+    to_end = mm_low(jnp.exp(total - cum), spread)
+    kept = mm_exact(jnp.broadcast_to(jnp.exp(total), (8, LANES)), spread)[0:1, :]
 
     gate = proj[:, :wide].astype(F32)
     y = take(y_ref, core).astype(F32)
     gate_sig = jax.nn.sigmoid(gate)
     gate_act = gate * gate_sig
-    g_gated = take(pulled_ref, core).astype(F32)
     gated = y * gate_act
     if as_rows:
+        g_gated = take(pulled_ref, core).astype(F32)
         sums = jnp.transpose(kappa_ref[...])
         rho = lax.rsqrt(sums[:, 0:1] / DI + eps)
         kappa = rho * rho * rho * sums[:, 1:2] / DI
         g_gated = rho * g_gated - gated * kappa
         put(refs[4], core, (gated * rho).astype(BF16), 0, wide)
     else:
+        g_gated = take(pulled_ref, core).astype(F32)
         g_gated = g_gated - gated * take(kappa_ref, core)[:, 0:1].astype(F32)
     dy = g_gated * gate_act
     g_gate = g_gated * y * (gate_sig * (1.0 + gate * (1.0 - gate_sig)))
@@ -314,8 +336,8 @@
     g_x = step_wide * (inner + outer) + wide_ref[0:1, :] * dy
     dy_grown = dy * grown
     dy_grown_low = dy_grown.astype(BF16)
-    carried_sum = mm_exact(dy_grown * mm(c_low, enter_low), fold)
-    outer_sum = mm_exact(x * outer, fold)
+    carried_sum = mm_low(dy_grown * mm(c_low, enter_low), fold)
+    outer_sum = mm_low(x * outer, fold)
     state_sum = mm_exact(
         jnp.broadcast_to(jnp.sum(enter * dstate, axis=0, keepdims=True), (8, wide)), fold
     )[0:1, :]
@@ -323,9 +345,9 @@
     g_cum = jnp.transpose(rows_ref[...]) + carried_sum - step * column - step_outer
     g_total = (
         jnp.sum(step_outer, axis=0, keepdims=True)
-        + jnp.exp(cum[rows - 1 : rows, :]) * state_sum
+        + jnp.exp(total) * state_sum
     )
-    g_decay = mm_exact(upper.astype(F32), g_cum) + g_total
+    g_decay = mm_thirds(upper.astype(F32), g_cum) + g_total
     scaled_decay = rate * g_decay
     g_raw = (column + outer_sum - scaled_decay) * jax.nn.sigmoid(shifted)
     head_grad_ref[0:1, :] += jnp.sum(g_raw, axis=0, keepdims=True)
@@ -337,7 +359,7 @@
     ending = (x * (step_wide * to_end)).astype(BF16)
     g_b = mm(d_low, c_low) + mm_nt(ending, dstate_low)
     g_c = mm_tn(d_low, b_low) + mm_nt(dy_grown_low, enter_low)
-    dstate_ref[...] = dstate * jnp.exp(total) + mm_tn(c_low, dy_grown_low)
+    dstate_ref[...] = dstate * kept + mm_tn(c_low, dy_grown_low)
 
     gext_ref[0:rows, :wide] = g_x * slope[:, :wide]
     gext_ref[0:rows, wide : wide + NSTATE] = g_b * slope[:, wide : wide + NSTATE]
@@ -416,7 +438,7 @@
             dimension_semantics=("arbitrary",), vmem_limit_bytes=CAP
         ),
         cost_estimate=pl.CostEstimate(
-            flops=length * wide * 66000, bytes_accessed=length * 9000, transcendentals=0
+            flops=length * wide * 40000, bytes_accessed=length * 9000, transcendentals=0
         ),
         name="mix_backward",
     )(place, proj, proj, y, pulled, kappa, enter, conv_rows, head_rows, wide_rows)
@@ -439,6 +461,10 @@
 
 def flip(values, axis):
     return lax.ppermute(values, axis, [(0, 1), (1, 0)])
+
+
+def flip_both(values, names):
+    return lax.ppermute(values, names, [(0, 3), (1, 2), (2, 1), (3, 0)])
 
 
 class Axes:
@@ -646,82 +672,118 @@
     return grads, sums[:, :, 0], spares
 
 
-def copies_gather(axes, whole):
+def together(*values):
+    return lax.optimization_barrier(values)
+
+
+def copies_start(axes, whole):
     slow, fast = axes.copies
+    return whole, flip(whole, fast), flip(whole, slow)
+
+
+def copies_corner(axes, parts):
+    slow, fast = axes.copies
+    whole, one, two = parts
     half = whole.shape[0] // 2
-    one, two = flip(whole, fast), flip(whole, slow)
-    corner = [flip(one[:half], slow), flip(two[half:], fast)]
-    every = [(index,) for index in range(whole.shape[0])]
-    lists = [[(array, at) for (at,) in every] for array in (whole, one, two)]
-    return lists + [[(corner[at // half], at % half) for (at,) in every]]
-
-
-def sum_start(axes, pieces):
+    return flip(one[:half], slow), flip(two[half:], fast)
+
+
+def copies_lists(parts, corner):
+    count = parts[0].shape[0]
+    half = count // 2
+    lists = [[(array, at) for at in range(count)] for array in parts]
+    return lists + [[(corner[at // half], at % half) for at in range(count)]]
+
+
+def sum_corner(axes, pieces):
     slow, fast = axes.copies
     half = pieces.shape[1] // 2
-    corner = [flip(pieces[3, :half], slow), flip(pieces[3, half:], fast)]
+    return flip(pieces[3, :half], slow), flip(pieces[3, half:], fast)
+
+
+def sum_sides(axes, pieces, corner):
+    slow, fast = axes.copies
+    half = pieces.shape[1] // 2
     to_fast = jnp.concatenate([add_low(pieces[1, :half], corner[0]), pieces[1, half:]], axis=0)
     to_slow = jnp.concatenate([pieces[2, :half], add_low(pieces[2, half:], corner[1])], axis=0)
-    return pieces[0], to_fast, to_slow
-
-
-def sum_end(axes, parts):
-    own, to_fast, to_slow = parts
-    slow, fast = axes.copies
-    return add_low(own, flip(to_fast, fast), flip(to_slow, slow))
-
-
-def team_gather(axes, rows):
+    return flip(to_fast, fast), flip(to_slow, slow)
+
+
+def gather_start(axes, rows):
     if len(axes.links) != 2:
-        whole = rows[None]
+        return (rows,)
+    far, near = axes.links
+    return rows, flip(rows, "c"), flip(rows, far), flip(rows, near)
+
+
+def gather_corner(axes, parts):
+    if len(axes.links) != 2:
+        return parts, []
+    far, near = axes.links
+    rows, other, from_far, from_near = parts
+    half = rows.shape[0] // 2
+    sides = jnp.stack([from_near, from_far])
+    sides = jnp.stack([sides, flip(sides, "c")], axis=1).reshape(-1, rows.shape[1])
+    corner = flip(from_near[:half], far), flip(from_far[half:], near)
+    return corner, [jnp.concatenate([rows, other], axis=0), sides]
+
+
+def gather_end(axes, corner):
+    if len(axes.links) != 2:
+        whole = corner[0][None]
         for name in reversed(axes.links):
             whole = jnp.concatenate([whole, flip(whole, name)], axis=0)
         whole = jnp.stack([whole, flip(whole, "c")], axis=1)
-        return [whole.reshape(-1, rows.shape[1])]
-    far, near = axes.links
-    half = rows.shape[0] // 2
-    from_far, from_near = flip(rows, far), flip(rows, near)
-    own = jnp.concatenate([rows, flip(rows, "c")], axis=0)
-    corner = jnp.concatenate([flip(from_near[:half], far), flip(from_far[half:], near)], axis=0)
-    sides = jnp.stack([from_near, from_far])
-    sides = jnp.stack([sides, flip(sides, "c")], axis=1).reshape(-1, rows.shape[1])
-    corner = jnp.concatenate([corner, flip(corner, "c")], axis=0)
-    return [own, sides, corner]
-
-
-def scatter_start(axes, product, rows):
+        return whole.reshape(-1, corner[0].shape[1])
+    last = jnp.concatenate(corner, axis=0)
+    return jnp.concatenate([last, flip(last, "c")], axis=0)
+
+
+def core_sum(rows_of, first, last, rows):
+    both = rows_of(first, last).reshape(-1, 2, rows, rows_of.columns)
+    return add_low(both[:, 0], flip(both[:, 1], "c"))
+
+
+def scatter_corner(axes, rows_of, rows):
     team = 2 ** len(axes.team)
     if len(axes.links) != 2:
-        whole = product(0, team * rows).reshape(team // 2, 2, rows, -1)
-        whole = add_low(whole[:, 0], flip(whole[:, 1], "c"))
-        for name in axes.links[:-1]:
+        return (core_sum(rows_of, 0, team * rows, rows),)
+    far, near = axes.links
+    corner = core_sum(rows_of, 6 * rows, 8 * rows, rows)[0]
+    half = rows // 2
+    hops = flip(corner[:half], far), flip(corner[half:], near)
+    sides = core_sum(rows_of, 2 * rows, 6 * rows, rows)
+    return hops, sides, core_sum(rows_of, 0, 2 * rows, rows)[0]
+
+
+def scatter_sides(axes, parts):
+    if len(axes.links) != 2:
+        whole = parts[0]
+        for name in axes.links:
             half = whole.shape[0] // 2
             whole = add_low(whole[:half], flip(whole[half:], name))
-        return whole[0], whole[1:]
+        return (whole[0],)
     far, near = axes.links
-    half = rows // 2
-    corner = product(6 * rows, 8 * rows)
-    corner = add_low(corner[:rows], flip(corner[rows:], "c"))
-    sides = product(2 * rows, 6 * rows).reshape(2, 2, rows, -1)
-    sides = add_low(sides[:, 0], flip(sides[:, 1], "c"))
-    own = product(0, 2 * rows)
-    own = add_low(own[:rows], flip(own[rows:], "c"))
-    got_far, got_near = flip(corner[:half], far), flip(corner[half:], near)
-    to_near = jnp.concatenate([add_low(sides[0, :half], got_far), sides[0, half:]], axis=0)
-    to_far = jnp.concatenate([sides[1, :half], add_low(sides[1, half:], got_near)], axis=0)
-    return own, to_near, to_far
-
-
-def scatter_end(axes, parts):
-    if len(axes.links) != 2:
-        return parts[0].astype(F32) + flip(parts[1], axes.links[-1])[0].astype(F32)
-    own, to_near, to_far = parts
-    far, near = axes.links
-    return own.astype(F32) + flip(to_near, near).astype(F32) + flip(to_far, far).astype(F32)
-
-
-def team_scatter(axes, product, rows):
-    return scatter_end(axes, scatter_start(axes, product, rows))
+    hops, sides, own = parts
+    half = own.shape[0] // 2
+    to_near = jnp.concatenate([add_low(sides[0, :half], hops[0]), sides[0, half:]], axis=0)
+    to_far = jnp.concatenate([sides[1, :half], add_low(sides[1, half:], hops[1])], axis=0)
+    return own, flip(to_near, near), flip(to_far, far)
+
+
+def add_all(parts):
+    total = parts[0].astype(F32)
+    for part in parts[1:]:
+        total = total + part.astype(F32)
+    return total
+
+
+class Rows:
+    def __init__(self, make, columns):
+        self.make, self.columns = make, columns
+
+    def __call__(self, first, last):
+        return self.make(first, last)
 
 
 def local(
@@ -765,24 +827,41 @@
         blocks = split_in(axes, in_weight, after(norm_gain[layer], start), spare, layer)
         return team_swap(blocks).reshape(-1, depth, wide)
 
-    def in_columns(blocks, at_once):
-        relative = at_once and len(axes.copies) == 2
-        if relative:
-            lists = copies_gather(axes, blocks)
-        else:
-            got = lax.all_gather(blocks, axes.copies)
-            lists = [[(got, (r, k)) for k in range(blocks.shape[0])] for r in range(copies)]
-        return join_in(axes, place, lists, relative)
-
-    def out_rows(layer):
-        mine = out_weight[layer].astype(F32) * gate_gain[layer].astype(F32)[:, None]
+    def in_columns(blocks):
+        got = lax.all_gather(blocks, axes.copies)
+        lists = [[(got, (r, k)) for k in range(blocks.shape[0])] for r in range(copies)]
+        return join_in(axes, place, lists, False)
+
+    def out_rows(layer, start):
+        gain = after(gate_gain[layer], start)
+        mine = out_weight[layer].astype(F32) * gain.astype(F32)[:, None]
         return lax.all_gather(mine.astype(BF16), axes.copies, axis=0, tiled=True)
 
+    paired = len(axes.copies) == 2
+    assert layers == 2
+
+    weight_out_0 = out_rows(0, tokens)
     blocks = in_blocks(0, tokens)
     parts = blocks.shape[0] // team
-    weight_in, beside = in_columns(blocks, True)
-    weight_out = out_rows(0)
-    residual = after(tokens[0], blocks).astype(F32)
+    residual_0 = tokens[0].astype(F32)
+    rho_0 = rms(residual_0)
+    blocks, sent = together(blocks, (residual_0 * rho_0).astype(BF16))
+    gathered = gather_start(axes, sent)
+    if paired:
+        copied, gathered = together(copies_start(axes, blocks), gathered)
+    hops, pieces_0 = gather_corner(axes, gathered)
+    cot = gather_start(axes, after(cotangent[0], gathered))
+    if paired:
+        corner = copies_corner(axes, copied)
+        corner, hops, weight_out_0 = together(corner, hops, weight_out_0)
+        weight_in_0, beside = join_in(axes, place, copies_lists(copied, corner), True)
+    else:
+        weight_in_0, beside = in_columns(blocks)
+    last = gather_end(axes, hops)
+    last, cot = together(last, cot)
+    pieces_0 = pieces_0 + [last]
+    proj_0 = [mm(piece, weight_in_0).astype(BF16) for piece in pieces_0]
+    proj_0 = jnp.concatenate(proj_0, axis=0)
 
     conv = beside[:, : conv.shape[0], LANES - room :]
     conv = conv.reshape(-1, len(cuts), layers * taps, room).transpose(0, 2, 1, 3)
@@ -798,44 +877,61 @@
     head = jnp.stack([head[:, 0], jnp.exp(head[:, 1])], axis=1)
     head = jnp.pad(head, ((0, 0), (0, 6), (0, LANES - heads)))
 
-    records = []
-    for layer in range(layers):
-        rho = rms(residual)
-        pieces = team_gather(axes, (residual * rho).astype(BF16))
-        more = layer + 1 < layers
-        if more:
-            blocks = in_blocks(layer + 1, pieces[-1])
-            cot_pieces = team_gather(axes, after(cotangent[0], blocks))
-            g_scaled = None
-        else:
-            g_scaled = [mm_nt(piece, weight_out) for piece in cot_pieces]
-            g_scaled = jnp.concatenate(g_scaled, axis=0).astype(BF16)
-        proj = jnp.concatenate([mm(piece, weight_in).astype(BF16) for piece in pieces], axis=0)
-        gated, y, enter, *sums = mix_forward(
-            place, proj, conv[layer], head[layer], skip[layer], g_scaled
-        )
-        normed = jnp.concatenate(pieces, axis=0)
-        records.append((residual, rho, normed, proj, gated, y, enter, weight_in, weight_out))
-        if not more:
-            break
-        gated = after(gated, blocks, cot_pieces)
-
-        def branch_rows(begin, end):
-            cut = gated[begin:end]
-            squares = jnp.sum(jnp.square(cut.astype(F32)), axis=1, keepdims=True)
-            squares = jnp.broadcast_to(squares, (end - begin, LANES))
-            return jnp.concatenate([mm(cut, weight_out), squares], axis=1).astype(BF16)
-
-        got = team_scatter(axes, branch_rows, rows)
-        branch = got[:, :model]
-        gate_rho = lax.rsqrt(got[:, model : model + 1] / DI + eps)
-        records[-1] += (branch, gate_rho)
-        residual = residual + gate_rho * branch
-        weight_in = in_columns(blocks, False)[0]
-        weight_out = out_rows(layer + 1)
-
-    in_grads, out_grads = [], []
-    grad = cotangent[0].astype(F32)
+    blocks = in_blocks(1, last)
+    gated_0, y_0, enter_0 = mix_forward(place, proj_0, conv[0], head[0], skip[0])
+    cot_hops, cot = gather_corner(axes, cot)
+    gated_0, blocks, cot_hops = together(gated_0, blocks, cot_hops)
+    cot = cot + [gather_end(axes, cot_hops)]
+    weight_out_1 = out_rows(1, gated_0)
+
+    def branch_rows(begin, end):
+        cut = gated_0[begin:end]
+        squares = jnp.sum(jnp.square(cut.astype(F32)), axis=1, keepdims=True)
+        squares = jnp.broadcast_to(squares, (end - begin, LANES))
+        return jnp.concatenate([mm(cut, weight_out_0), squares], axis=1).astype(BF16)
+
+    got = together(*scatter_corner(axes, Rows(branch_rows, model + LANES), rows))
+    got = scatter_sides(axes, got)
+    if paired:
+        got, copied = together(got, copies_start(axes, blocks))
+    got = add_all(got)
+    branch_0 = got[:, :model]
+    gate_rho_0 = lax.rsqrt(got[:, model : model + 1] / DI + eps)
+
+    residual_1 = residual_0 + gate_rho_0 * branch_0
+    rho_1 = rms(residual_1)
+    gathered = gather_start(axes, (residual_1 * rho_1).astype(BF16))
+    g_scaled = jnp.concatenate([mm_nt(piece, weight_out_1).astype(BF16) for piece in cot], axis=0)
+    if paired:
+        gathered, corner, g_scaled = together(gathered, copies_corner(axes, copied), g_scaled)
+        weight_in_1 = join_in(axes, place, copies_lists(copied, corner), True)[0]
+    else:
+        weight_in_1 = in_columns(blocks)[0]
+    hops, pieces_1 = gather_corner(axes, gathered)
+    proj_1 = [mm(piece, weight_in_1).astype(BF16) for piece in pieces_1]
+    hops, proj_1 = together(hops, proj_1)
+    last = gather_end(axes, hops)
+    pieces_1 = pieces_1 + [last]
+    proj_1 = jnp.concatenate(proj_1 + [mm(last, weight_in_1).astype(BF16)], axis=0)
+    gated_1, y_1, enter_1, sums = mix_forward(
+        place, proj_1, conv[1], head[1], skip[1], g_scaled
+    )
+
+    sums = sums + flip(sums, "c")
+    if len(axes.links) == 2:
+        far, near = axes.links
+        sums = sums + flip(sums, far) + flip(sums, near) + flip_both(sums, axes.links)
+    else:
+        for name in axes.links:
+            sums = sums + flip(sums, name)
+    branch_1 = mm(gated_1, weight_out_1).astype(BF16)
+    sums, branch_1 = together(sums, branch_1)
+    branch_1 = lax.psum_scatter(branch_1, axes.team, scatter_dimension=0, tiled=True)
+    g_proj, g_conv, g_head, g_skip, scaled_1 = mix_backward(
+        place, proj_1, y_1, g_scaled, sums, enter_1, conv[1], head[1], skip[1], True
+    )
+    got_1 = jnp.concatenate(after(cot, g_proj), axis=0)
+    normed = jnp.concatenate(after(pieces_1, g_proj), axis=0)
 
     def spare_rows(g_conv, g_head, g_skip):
         g_conv = jnp.concatenate(
@@ -863,77 +959,75 @@
         more = -spare.shape[1] % 16 if depth % 16 == 0 else 0
         return jnp.pad(spare, ((0, 0), (0, more), (0, 0))).astype(BF16)
 
-    for layer in reversed(range(layers)):
-        last = layer == layers - 1
-        if last:
-            residual_in, rho, normed, proj, gated, y, enter, weight_in, weight_out = records[layer]
-            pieces = cot_pieces
-        else:
-            (
-                residual_in,
-                rho,
-                normed,
-                proj,
-                gated,
-                y,
-                enter,
-                weight_in,
-                weight_out,
-                branch,
-                gate_rho,
-            ) = records[layer]
-            pulled = grad * gate_rho
-            kappa = gate_rho * gate_rho * jnp.sum(pulled * branch, axis=1, keepdims=True) / DI
-            pulled = after(pulled, g_out, blocks)
-            sent = jnp.concatenate([pulled, jnp.broadcast_to(kappa, (rows, LANES))], axis=1)
-            pieces = team_gather(axes, sent.astype(BF16))
-        got = jnp.concatenate(pieces, axis=0)
-        if last:
-            sums = sums[0]
-            for name in axes.team:
-                sums = sums + flip(sums, name)
-            branch = scatter_start(
-                axes, lambda begin, end: mm(gated[begin:end], weight_out).astype(BF16), rows
-            )
-            scales = after(sums, branch)
-        else:
-            g_scaled = [mm_nt(piece[:, :model], weight_out) for piece in pieces]
-            g_scaled = jnp.concatenate(g_scaled, axis=0).astype(BF16)
-            scales = after(got, summed)
-        outs = mix_backward(
-            place, proj, y, g_scaled, scales, enter, conv[layer], head[layer], skip[layer], last
-        )
-        g_proj, g_conv, g_head, g_skip = outs[:4]
-        if last:
-            branch = scatter_end(axes, branch)
-            gate_rho = lax.dynamic_slice_in_dim(sums, me * rows, rows, 1)[0][:, None]
-            out = (residual + lax.rsqrt(gate_rho / DI + eps) * branch).astype(BF16)
-            g_proj = after(g_proj, branch)
-        else:
-            in_grads.insert(0, team_swap(summed.reshape(team, parts, depth, wide)))
-            g_proj = after(g_proj, in_grads)
+    def in_gradient(normed, g_proj, g_conv, g_head, g_skip, quick):
         g_in = mm_tn(normed, g_proj).astype(BF16)
         spare = spare_rows(g_conv, g_head, g_skip)
-        quick = layer == 0 and len(axes.copies) == 2
-        blocks = cut_in(axes, place, g_in, spare, depth, wide, quick)
-        g_out = mm_tn(outs[4] if last else gated, after(got, g_proj)[:, :model]).astype(BF16)
-        if layer == 0:
-            g_proj = after(g_proj, blocks)
-        weighed = scatter_start(
-            axes, lambda begin, end: mm_nt(g_proj[begin:end], weight_in).astype(BF16), rows
-        )
-        if quick:
-            summed = sum_end(axes, after(sum_start(axes, blocks), weighed))
-        else:
-            summed = lax.psum_scatter(blocks, axes.copies, scatter_dimension=0)
-        weighed = scatter_end(axes, weighed)
-        mean = jnp.mean(weighed * residual_in, axis=1, keepdims=True)
-        grad = grad + rho * weighed - residual_in * (rho * rho * rho * mean)
-        out_grads.insert(0, lax.psum_scatter(g_out, axes.copies, scatter_dimension=0, tiled=True))
-    in_grads.insert(0, team_swap(after(summed, weighed).reshape(team, parts, depth, wide)))
-
-    grad_in, grad_norm, spare = finish_in(axes, in_grads, in_weight, norm_gain)
-    grad_out = jnp.stack(out_grads).astype(F32)
+        return cut_in(axes, place, g_in, spare, depth, wide, quick)
+
+    def copies_scatter(values):
+        return lax.psum_scatter(values, axes.copies, scatter_dimension=0)
+
+    def owned(summed):
+        return team_swap(summed.reshape(team, parts, depth, wide))
+
+    def weighed_rows(g_proj, weight_in):
+        make = lambda begin, end: mm_nt(g_proj[begin:end], weight_in).astype(BF16)
+        return Rows(make, model)
+
+    weighed = scatter_corner(axes, weighed_rows(g_proj, weight_in_1), rows)
+    weighed, branch_1 = together(weighed, branch_1)
+    weighed = scatter_sides(axes, weighed)
+    blocks = in_gradient(normed, after(g_proj, weighed[0]), g_conv, g_head, g_skip, False)
+    weighed, blocks = together(weighed, blocks)
+    summed = copies_scatter(blocks)
+    squares = lax.dynamic_slice_in_dim(sums, me * rows, rows, 1)[0][:, None]
+    out = (residual_1 + lax.rsqrt(squares / DI + eps) * branch_1.astype(F32)).astype(BF16)
+    weighed = add_all(weighed)
+    mean = jnp.mean(weighed * residual_1, axis=1, keepdims=True)
+    grad = cotangent[0].astype(F32)
+    grad = grad + rho_1 * weighed - residual_1 * (rho_1 * rho_1 * rho_1 * mean)
+
+    pulled = grad * gate_rho_0
+    kappa = gate_rho_0 * gate_rho_0 * jnp.sum(pulled * branch_0, axis=1, keepdims=True) / DI
+    sent = jnp.concatenate([pulled, jnp.broadcast_to(kappa, (rows, LANES))], axis=1)
+    gathered = gather_start(axes, sent.astype(BF16))
+    g_out = mm_tn(scaled_1, got_1).astype(BF16)
+    gathered, g_out = together(gathered, g_out)
+    g_out_1 = lax.psum_scatter(g_out, axes.copies, scatter_dimension=0, tiled=True)
+    hops, pieces = gather_corner(axes, gathered)
+    g_scaled = [mm_nt(piece[:, :model], weight_out_0).astype(BF16) for piece in pieces]
+    hops, g_scaled = together(hops, g_scaled)
+    last = gather_end(axes, hops)
+    pieces = pieces + [last]
+    g_scaled = g_scaled + [mm_nt(last[:, :model], weight_out_0).astype(BF16)]
+    g_scaled = jnp.concatenate(g_scaled, axis=0)
+    kappa = jnp.concatenate([piece[:, model:] for piece in pieces], axis=0)
+    g_proj, g_conv, g_head, g_skip = mix_backward(
+        place, proj_0, y_0, g_scaled, after(kappa, summed), enter_0, conv[0], head[0], skip[0], False
+    )
+    g_proj, owned_1 = together(g_proj, owned(summed))
+    normed = jnp.concatenate(after(pieces_0, g_proj), axis=0)
+    got = jnp.concatenate([piece[:, :model] for piece in after(pieces, g_proj)], axis=0)
+    blocks = in_gradient(normed, g_proj, g_conv, g_head, g_skip, paired)
+    weighed = scatter_corner(axes, weighed_rows(after(g_proj, blocks), weight_in_0), rows)
+    g_out = mm_tn(gated_0, got).astype(BF16)
+    if paired:
+        corner = sum_corner(axes, blocks)
+        weighed, corner, g_out = together(weighed, corner, g_out)
+        weighed = scatter_sides(axes, weighed)
+        weighed, sides = together(weighed, sum_sides(axes, blocks, corner))
+        summed = add_low(blocks[0], *sides)
+    else:
+        weighed = scatter_sides(axes, weighed)
+        summed = copies_scatter(blocks)
+    g_out_0 = lax.psum_scatter(g_out, axes.copies, scatter_dimension=0, tiled=True)
+    owned_0 = owned(summed)
+    weighed = add_all(weighed)
+    mean = jnp.mean(weighed * residual_0, axis=1, keepdims=True)
+    grad = grad + rho_0 * weighed - residual_0 * (rho_0 * rho_0 * rho_0 * mean)
+
+    grad_in, grad_norm, spare = finish_in(axes, [owned_0, owned_1], in_weight, norm_gain)
+    grad_out = jnp.stack([g_out_0, g_out_1]).astype(F32)
     grad_gate = jnp.sum(grad_out * out_weight.astype(F32), axis=2)
     grad_out = grad_out * gate_gain.astype(F32)[:, :, None]
 

time: 600 us -> 548 us (0.913)
  waiting for transfers between devices: 272 us -> 182 us
  local copies, waits for them, and re-layouts: 39.5 us -> 58.3 us
  other arithmetic: 39 us -> 55.3 us
    ppermute x67 -> x64, waiting for transfers between devices: 230 us -> 145 us  [flip(): return lax.ppermute(values, axis, [(0, 1), (1, 0)])]
    another operation x13 -> x14, other arithmetic: 4.27 us -> 14.5 us  [the longest x8 11.5 us: gather_corner(): jnp.stack([sides, flip(sides, 'c')], axis=1).reshape(-1, rows.shape[1])]
    squeeze x11 -> x13, local copies, waits for them, and re-layouts: 0.55 us -> 7.68 us  [the longest x6 2.66 us: core_sum(): return add_low(both[:, 0], flip(both[:, 1], 'c'))]
    convert_element_type x14 -> x11, other arithmetic: 4.45 us -> 11 us  [add_low(): return total.astype(BF16)]
    dot_general x12 -> x10, matrix products: 20.5 us -> 26.6 us  [mm(): return jnp.dot(left, right, preferred_element_type=F32)]
    unnamed x165 -> x226, local copies, waits for them, and re-layouts: 25.7 us -> 28.8 us
    ppermute x67 -> x64, starting transfers between devices: 56.6 us -> 56.5 us  [flip(): return lax.ppermute(values, axis, [(0, 1), (1, 0)])]
  transfers between devices with their start and end apart: 77 -> 75, of which waited for: 42 -> 36; matrix products, arithmetic and copies ran while one was open for 17% -> 24% of each run, Pallas kernels for 7% -> 13%
where the time goes in v3:
time: 548 us; the launch traced here: 540 us
  waiting for transfers between devices  182 us (33%)
  Pallas kernels  83.2 us (15%)
  starting transfers between devices  78.5 us (14%)
  matrix products  65.7 us (12%)
  local copies, waits for them, and re-layouts  58.3 us (11%)
  other arithmetic  55.3 us (10%)
  between operations  16.5 us (3%)
    ppermute x64, waiting for transfers between devices, flip(): return lax.ppermute(values, axis, [(0, 1), (1, 0)])  145 us
    ppermute x64, starting transfers between devices, flip(): return lax.ppermute(values, axis, [(0, 1), (1, 0)])  56.5 us
    pallas_call x2, Pallas kernels, mix_backward(): pl.pallas_call(functools.partial(mix_backward_kernel, as_rows=as_rows), g...  50.8 us
    all_to_all x4, waiting for transfers between devices, team_swap(): return lax.all_to_all(blocks, axes.team, split_axis=0, concat_axis=0)  37.2 us
    unnamed x226, local copies, waits for them, and re-layouts  28.8 us
    dot_general x10, matrix products, mm(): return jnp.dot(left, right, preferred_element_type=F32)  26.6 us
    dot_general x4, matrix products, mm_tn(): lax.dot_general(left, right, (((0,), (0,)), ((), ())), preferred_element_...  21.5 us
    all_to_all x4, starting transfers between devices, team_swap(): return lax.all_to_all(blocks, axes.team, split_axis=0, concat_axis=0)  19.8 us
  transfers between devices with their start and end apart: 75, of which 36 were waited for; matrix products, arithmetic and copies ran while one was open for 24% of the time, Pallas kernels for 13%

profile of v3, /device:TPU:0, one launch (start us, length us, event | category | flops | bytes accessed | tf_op | source)
XLA Modules:
  0.0 539.6 jit_solution(1647381877575123722)
XLA Ops:
  12.4 6.5 %all-to-all-start = ((bf16[8,3,48,384]{3,2,1,0:T(8,128)(2,1)}), bf16[8,3,48,384]{3,2,1,0:T(8,128)(2,1)S(1)}, u32[]{:S(2)}, u32[]{:S(2)}) async-start(bf16[8,3,48,384]{3,2,1,0:T(8,128)(2,1)} %split_in.2), calls=%async_computation | async-start | bytes 1769472 | tf_op jit(solution)/shard_map/all_to_all | solution.py:824
  20.7 21.3 %all-to-all-done = bf16[8,3,48,384]{3,2,1,0:T(8,128)(2,1)S(1)} async-done(((bf16[8,3,48,384]{3,2,1,0:T(8,128)(2,1)}), bf16[8,3,48,384]{3,2,1,0:T(8,128)(2,1)S(1)}, u32[]{:S(2)}, u32[]{:S(2)}) %all-to-all-start) | async-done | bytes 884768 | tf_op jit(solution)/shard_map/all_to_all | solution.py:824
  48.4 16.4 %collective-permute-done.3 = bf16[128,1536]{1,0:T(8,128)(2,1)S(1)} collective-permute-done((bf16[128,1536]{1,0:T(8,128)(2,1)S(1)}, bf16[128,1536]{1,0:T(8,128)(2,1)S(1)}, u32[]{:S(2)}, u32[]{:S(2)}) %collective-permute-start.3) | collective-permute-done | bytes 393248 | tf_op jit(solution)/shard_map/ppermute | solution.py:463
  65.2 4.2 collective-permute-done.refs_1_
  77.4 3.8 collective-permute-done.7
  91.6 4.1 convolution_convert_fusion.11
  110.6 3.6 all-to-all-start.1
  123.5 7.2 %mix_forward.2 = (bf16[1024,384]{1,0:T(8,128)(2,1)S(1)}, bf16[1024,384]{1,0:T(8,128)(2,1)S(1)}, f32[4,128,384]{2,1,0:T(8,128)S(1)}) custom-call(s32[3]{0:T(128)S(1)} %pad_add_fusion.place_ref, bf16[1024,1152]{1,0:T(8,128)(2,1)S(1)} %pad_maximum_fusion.proj_ref.before_ref, f32[8,640]{1,0:T(8,128)S(1)} %get-tuple-element.294.conv_ref, ...), custom_call_target="tpu_custom_call" | custom-call | flops 7077888000 | bytes 6144000 | tf_op jit(solution)/shard_map/mix_forward/pallas_call | solution.py:182
  133.9 11.7 %collective-permute-done.14 = bf16[64,1536]{1,0:T(8,128)(2,1)S(1)} collective-permute-done((bf16[64,1536]{1,0:T(8,128)(2,1)}, bf16[64,1536]{1,0:T(8,128)(2,1)S(1)}, u32[]{:S(2)}, u32[]{:S(2)}) %collective-permute-start.14) | collective-permute-done | bytes 196640 | tf_op jit(solution)/shard_map/ppermute | solution.py:463
  163.3 9.5 %collective-permute-done.17 = bf16[64,1664]{1,0:T(8,128)(2,1)S(1)} collective-permute-done((bf16[64,1664]{1,0:T(8,128)(2,1)S(1)}, bf16[64,1664]{1,0:T(8,128)(2,1)S(1)}, u32[]{:S(2)}, u32[]{:S(2)}) %collective-permute-start.17) | collective-permute-done | bytes 213024 | tf_op jit(solution)/shard_map/ppermute | solution.py:463
  178.3 17.0 %collective-permute-done.22 = bf16[128,1664]{1,0:T(8,128)(2,1)S(1)} collective-permute-done((bf16[128,1664]{1,0:T(8,128)(2,1)S(1)}, bf16[128,1664]{1,0:T(8,128)(2,1)S(1)}, u32[]{:S(2)}, u32[]{:S(2)}) %collective-permute-start.22) | collective-permute-done | bytes 426016 | tf_op jit(solution)/shard_map/ppermute | solution.py:463
  208.7 9.2 %collective-permute-done.26 = bf16[128,1536]{1,0:T(8,128)(2,1)} collective-permute-done((bf16[128,1536]{1,0:T(8,128)(2,1)}, bf16[128,1536]{1,0:T(8,128)(2,1)}, u32[]{:S(2)}, u32[]{:S(2)}) %collective-permute-start.26) | collective-permute-done | bytes 393248 | tf_op jit(solution)/shard_map/ppermute | solution.py:463
  223.6 3.4 join_in.3
  229.1 3.5 convolution_convert_fusion.9
  242.0 8.1 %mix_forward.3 = (bf16[1024,384]{1,0:T(8,128)(2,1)S(1)}, bf16[1024,384]{1,0:T(8,128)(2,1)S(1)}, f32[4,128,384]{2,1,0:T(8,128)S(1)}, f32[8,1024]{1,0:T(8,128)S(1)}) custom-call(s32[3]{0:T(128)S(1)} %pad_add_fusion.place_ref, bf16[1024,1152]{1,0:T(8,128)(2,1)S(1)} %pad_maximum_fusion.1.proj_ref.before_ref, f32[8,640]{1,0:T(8,128)S(1)} %get-tuple-element.293.conv_ref, ...), custom_call_target="tpu_custom_call" | custom-call | flops 7077888000 | bytes 6144000 | tf_op jit(solution)/shard_map/mix_forward/pallas_call | solution.py:182
  258.4 5.0 convolution_convert_fusion.2
  265.8 30.7 %mix_backward.2 = (bf16[1024,1152]{1,0:T(8,128)(2,1)S(1)}, f32[8,640]{1,0:T(8,128)S(1)}, f32[8,128]{1,0:T(8,128)S(1)}, f32[8,384]{1,0:T(8,128)S(1)}, bf16[1024,384]{1,0:T(8,128)(2,1)S(1)}) custom-call(s32[3]{0:T(128)S(1)} %pad_add_fusion.place_ref, bf16[1024,1152]{1,0:T(8,128)(2,1)} %copy-done.8, bf16[1024,1152]{1,0:T(8,128)(2,1)} %copy-done.8, ...), custom_call_target="tpu_custom_call" | custom-call | flops 15728640000 | bytes 9216000 | tf_op jit(solution)/shard_map/mix_backward/pallas_call | solution.py:400
  298.2 3.4 convolution_convert_fusion.16
  310.1 8.2 %collective-permute-done.41 = bf16[64,1536]{1,0:T(8,128)(2,1)} collective-permute-done((bf16[64,1536]{1,0:T(8,128)(2,1)S(1)}, bf16[64,1536]{1,0:T(8,128)(2,1)}, u32[]{:S(2)}, u32[]{:S(2)}) %collective-permute-start.41) | collective-permute-done | bytes 196640 | tf_op jit(solution)/shard_map/ppermute | solution.py:463
  324.7 6.0 %convolution_convert_fusion.1.grad_ref = bf16[1536,1152]{1,0:T(8,128)(2,1)} fusion(bf16[1024,1152]{1,0:T(8,128)(2,1)S(1)} %get-tuple-element.198, bf16[256,1536]{1,0:T(8,128)(2,1)S(1)} %copy-done.88, bf16[512,1536]{1,0:T(8,128)(2,1)S(1)} %bitcast.331, bf16[256,1536]{1,0:T(8,128)(2,1)S(1)} %copy-done.84), kind=kOutput, calls=%fused_computation.1 | convolution fusion | flops 3635085312 | bytes 9043968 | tf_op jit(solution)/shard_map/dot_general | solution.py:36
  330.8 4.2 cut_in.2
  335.0 6.3 %collective-permute-done.46 = bf16[128,1536]{1,0:T(8,128)(2,1)S(1)} collective-permute-done((bf16[128,1536]{1,0:T(8,128)(2,1)}, bf16[128,1536]{1,0:T(8,128)(2,1)S(1)}, u32[]{:S(2)}, u32[]{:S(2)}) %collective-permute-start.46) | collective-permute-done | bytes 393248 | tf_op jit(solution)/shard_map/ppermute | solution.py:463
  350.9 4.3 fusion.25
  355.1 14.8 %collective-permute-done.48 = bf16[128,1664]{1,0:T(8,128)(2,1)S(1)} collective-permute-done((bf16[128,1664]{1,0:T(8,128)(2,1)S(1)}, bf16[128,1664]{1,0:T(8,128)(2,1)S(1)}, u32[]{:S(2)}, u32[]{:S(2)}) %collective-permute-start.48) | collective-permute-done | bytes 426016 | tf_op jit(solution)/shard_map/ppermute | solution.py:463
  381.8 5.3 collective-permute-done.50
  392.1 3.7 all-to-all-start.2
  397.0 20.1 %mix_backward.3 = (bf16[1024,1152]{1,0:T(8,128)(2,1)S(1)}, f32[8,640]{1,0:T(8,128)S(1)}, f32[8,128]{1,0:T(8,128)S(1)}, f32[8,384]{1,0:T(8,128)S(1)}) custom-call(s32[3]{0:T(128)S(1)} %pad_add_fusion.place_ref, bf16[1024,1152]{1,0:T(8,128)(2,1)} %copy-done.7, bf16[1024,1152]{1,0:T(8,128)(2,1)} %copy-done.7, bf16[1024,384]{1,0:T(8,128)(2,1)S(1)} %copy-done.24, ...), custom_call_target="tpu_custom_call" | custom-call | flops 15728640000 | bytes 9216000 | tf_op jit(solution)/shard_map/mix_backward/pallas_call | solution.py:400
  420.8 8.8 %convolution_convert_fusion.grad_ref = bf16[1536,1152]{1,0:T(8,128)(2,1)} fusion(bf16[1024,1152]{1,0:T(8,128)(2,1)} %copy-done.14, bf16[256,1536]{1,0:T(8,128)(2,1)} %copy-done.65, bf16[512,1536]{1,0:T(8,128)(2,1)} %bitcast.327, bf16[256,1536]{1,0:T(8,128)(2,1)} %copy-done.81), kind=kOutput, calls=%fused_computation | convolution fusion | flops 3635085312 | bytes 9043968 | tf_op jit(solution)/shard_map/dot_general | solution.py:36
  459.4 4.2 collective-permute-done.55
  476.8 14.8 %collective-permute-done.62 = bf16[128,1536]{1,0:T(8,128)(2,1)} collective-permute-done((bf16[128,1536]{1,0:T(8,128)(2,1)S(1)}, bf16[128,1536]{1,0:T(8,128)(2,1)}, u32[]{:S(2)}, u32[]{:S(2)}) %collective-permute-start.62) | collective-permute-done | bytes 393248 | tf_op jit(solution)/shard_map/ppermute | solution.py:463
  498.6 6.1 %all-to-all-start.3 = ((bf16[8,3,48,384]{3,2,1,0:T(8,128)(2,1)}), bf16[8,3,48,384]{3,2,1,0:T(8,128)(2,1)S(1)}, u32[]{:S(2)}, u32[]{:S(2)}) async-start(bf16[8,3,48,384]{3,2,1,0:T(8,128)(2,1)} %bitcast.325), calls=%async_computation.4 | async-start | bytes 1769472 | tf_op jit(solution)/shard_map/all_to_all | solution.py:824
  511.9 15.9 %all-to-all-done.3.refs_0_ = bf16[8,3,48,384]{3,2,1,0:T(8,128)(2,1)S(1)} async-done(((bf16[8,3,48,384]{3,2,1,0:T(8,128)(2,1)}), bf16[8,3,48,384]{3,2,1,0:T(8,128)(2,1)S(1)}, u32[]{:S(2)}, u32[]{:S(2)}) %all-to-all-start.3) | async-done | bytes 884768 | tf_op jit(solution)/shard_map/all_to_all | solution.py:824
  (574 shorter events, 231.9 us)
Async XLA Ops:
  12.4 29.6 %all-to-all-start = ((bf16[8,3,48,384]{3,2,1,0:T(8,128)(2,1)}), bf16[8,3,48,384]{3,2,1,0:T(8,128)(2,1)S(1)}, u32[]{:S(2)}, u32[]{:S(2)}) async-start(bf16[8,3,48,384]{3,2,1,0:T(8,128)(2,1)} %split_in.2), calls=%async_computation | async-start | bytes 1769472 | tf_op jit(solution)/shard_map/all_to_all | solution.py:824
  18.9 65.6 %all-gather.3.cloned.1.call-start = ((), (), s32[]{:S(2)}) async-start(), calls=%async_computation.8 | async-start | bytes 1474560 | tf_op jit(solution)/shard_map/all_gather | solution.py:838
  42.0 27.4 %collective-permute-start = (bf16[24,48,384]{2,1,0:T(8,128)(2,1)S(1)}, bf16[24,48,384]{2,1,0:T(8,128)(2,1)S(1)}, u32[]{:S(2)}, u32[]{:S(2)}) collective-permute-start(bf16[24,48,384]{2,1,0:T(8,128)(2,1)S(1)} %bitcast.313), channel_id=1, source_target_pairs={{0,1},{1,0},{2,3},{3,2},{4,5},{5,4},{6,7},{7,6},{8,9},{9,8},{10,11... | collective-permute-start | bytes 2654216 | tf_op jit(solution)/shard_map/ppermute | solution.py:463
  43.5 25.9 %collective-permute-start.1 = (bf16[24,48,384]{2,1,0:T(8,128)(2,1)S(1)}, bf16[24,48,384]{2,1,0:T(8,128)(2,1)S(1)}, u32[]{:S(2)}, u32[]{:S(2)}) collective-permute-start(bf16[24,48,384]{2,1,0:T(8,128)(2,1)S(1)} %bitcast.314), channel_id=1, source_target_pairs={{0,2},{2,0},{1,3},{3,1},{4,6},{6,4},{5,7},{7,5},{8,10},{10,8},{9,1... | collective-permute-start | bytes 2654216 | tf_op jit(solution)/shard_map/ppermute | solution.py:463
  45.3 19.6 %collective-permute-start.3 = (bf16[128,1536]{1,0:T(8,128)(2,1)S(1)}, bf16[128,1536]{1,0:T(8,128)(2,1)S(1)}, u32[]{:S(2)}, u32[]{:S(2)}) collective-permute-start(bf16[128,1536]{1,0:T(8,128)(2,1)S(1)} %fusion.49), channel_id=1, source_target_pairs={{0,16},{16,0},{1,17},{17,1},{2,18},{18,2},{3,19},{19,3},{4,20},{20... | collective-permute-start | bytes 1179656 | tf_op jit(solution)/shard_map/ppermute | solution.py:463
  45.3 19.9 %collective-permute-start.4 = (bf16[128,1536]{1,0:T(8,128)(2,1)S(1)}, bf16[128,1536]{1,0:T(8,128)(2,1)S(1)}, u32[]{:S(2)}, u32[]{:S(2)}) collective-permute-start(bf16[128,1536]{1,0:T(8,128)(2,1)S(1)} %fusion.49), channel_id=1, source_target_pairs={{0,8},{8,0},{1,9},{9,1},{2,10},{10,2},{3,11},{11,3},{4,12},{12,4},... | collective-permute-start | bytes 1179656 | tf_op jit(solution)/shard_map/ppermute | solution.py:463
  76.1 25.2 %collective-permute-start.11 = (bf16[128,1536]{1,0:T(8,128)(2,1)}, bf16[128,1536]{1,0:T(8,128)(2,1)}, u32[]{:S(2)}, u32[]{:S(2)}) collective-permute-start(bf16[128,1536]{1,0:T(8,128)(2,1)} %bitcast.16), channel_id=1, source_target_pairs={{0,4},{4,0},{1,5},{5,1},{2,6},{6,2},{3,7},{7,3},{8,12},{12,8},{9,1... | collective-permute-start | bytes 1179656 | tf_op jit(solution)/shard_map/ppermute | solution.py:463
  81.2 20.0 %collective-permute-start.12 = (bf16[128,1536]{1,0:T(8,128)(2,1)}, bf16[128,1536]{1,0:T(8,128)(2,1)}, u32[]{:S(2)}, u32[]{:S(2)}) collective-permute-start(bf16[128,1536]{1,0:T(8,128)(2,1)} %bitcast.16), channel_id=1, source_target_pairs={{0,16},{16,0},{1,17},{17,1},{2,18},{18,2},{3,19},{19,3},{4,20},{20... | collective-permute-start | bytes 1179656 | tf_op jit(solution)/shard_map/ppermute | solution.py:463
  81.4 19.9 %collective-permute-start.13 = (bf16[128,1536]{1,0:T(8,128)(2,1)}, bf16[128,1536]{1,0:T(8,128)(2,1)}, u32[]{:S(2)}, u32[]{:S(2)}) collective-permute-start(bf16[128,1536]{1,0:T(8,128)(2,1)} %bitcast.16), channel_id=1, source_target_pairs={{0,8},{8,0},{1,9},{9,1},{2,10},{10,2},{3,11},{11,3},{4,12},{12,4},... | collective-permute-start | bytes 1179656 | tf_op jit(solution)/shard_map/ppermute | solution.py:463
  106.9 23.9 %collective-permute-start.30 = (bf16[2,128,1536]{2,1,0:T(8,128)(2,1)}, bf16[2,128,1536]{2,1,0:T(8,128)(2,1)}, u32[]{:S(2)}, u32[]{:S(2)}) collective-permute-start(bf16[2,128,1536]{2,1,0:T(8,128)(2,1)} %get-tuple-element.279), channel_id=1, source_target_pairs={{0,4},{4,0},{1,5},{5,1},{2,6},{6,2},{3,7},{7,3},{8,12},{12,8},{9,1... | collective-permute-start | bytes 2359304 | tf_op jit(solution)/shard_map/ppermute | solution.py:463
  110.6 35.7 %all-to-all-start.1 = ((bf16[8,3,48,384]{3,2,1,0:T(8,128)(2,1)}), bf16[8,3,48,384]{3,2,1,0:T(8,128)(2,1)S(1)}, u32[]{:S(2)}, u32[]{:S(2)}) async-start(bf16[8,3,48,384]{3,2,1,0:T(8,128)(2,1)} %split_in.3), calls=%async_computation.1 | async-start | bytes 1769472 | tf_op jit(solution)/shard_map/all_to_all | solution.py:824
  114.2 89.8 %all-gather.5.cloned.1.call-start = ((), (), s32[]{:S(2)}) async-start(), calls=%async_computation.9 | async-start | bytes 1474560 | tf_op jit(solution)/shard_map/all_gather | solution.py:838
  114.5 31.1 %collective-permute-start.14 = (bf16[64,1536]{1,0:T(8,128)(2,1)}, bf16[64,1536]{1,0:T(8,128)(2,1)S(1)}, u32[]{:S(2)}, u32[]{:S(2)}) collective-permute-start(bf16[64,1536]{1,0:T(8,128)(2,1)} %slice.391), channel_id=1, source_target_pairs={{0,16},{16,0},{1,17},{17,1},{2,18},{18,2},{3,19},{19,3},{4,20},{20... | collective-permute-start | bytes 589832 | tf_op jit(solution)/shard_map/ppermute | solution.py:463
  117.3 28.9 %collective-permute-start.15 = (bf16[64,1536]{1,0:T(8,128)(2,1)}, bf16[64,1536]{1,0:T(8,128)(2,1)S(1)}, u32[]{:S(2)}, u32[]{:S(2)}) collective-permute-start(bf16[64,1536]{1,0:T(8,128)(2,1)} %slice.392), channel_id=1, source_target_pairs={{0,8},{8,0},{1,9},{9,1},{2,10},{10,2},{3,11},{11,3},{4,12},{12,4},... | collective-permute-start | bytes 589832 | tf_op jit(solution)/shard_map/ppermute | solution.py:463
  153.1 24.4 %collective-permute-start.23 = (bf16[24,48,384]{2,1,0:T(8,128)(2,1)S(1)}, bf16[24,48,384]{2,1,0:T(8,128)(2,1)S(1)}, u32[]{:S(2)}, u32[]{:S(2)}) collective-permute-start(bf16[24,48,384]{2,1,0:T(8,128)(2,1)S(1)} %bitcast.310), channel_id=1, source_target_pairs={{0,1},{1,0},{2,3},{3,2},{4,5},{5,4},{6,7},{7,6},{8,9},{9,8},{10,11... | collective-permute-start | bytes 2654216 | tf_op jit(solution)/shard_map/ppermute | solution.py:463
  154.3 24.1 %collective-permute-start.24 = (bf16[24,48,384]{2,1,0:T(8,128)(2,1)S(1)}, bf16[24,48,384]{2,1,0:T(8,128)(2,1)S(1)}, u32[]{:S(2)}, u32[]{:S(2)}) collective-permute-start(bf16[24,48,384]{2,1,0:T(8,128)(2,1)S(1)} %bitcast.311), channel_id=1, source_target_pairs={{0,2},{2,0},{1,3},{3,1},{4,6},{6,4},{5,7},{7,5},{8,10},{10,8},{9,1... | collective-permute-start | bytes 2654216 | tf_op jit(solution)/shard_map/ppermute | solution.py:463
  155.4 163.1 %reduce-scatter.7.cloned.1.call-start = ((), (), s32[]{:S(2)}) async-start(), calls=%async_computation.10 | async-start | bytes 3538944 | tf_op jit(solution)/shard_map/reduce_scatter | solution.py:929
  175.1 20.3 %collective-permute-start.22 = (bf16[128,1664]{1,0:T(8,128)(2,1)S(1)}, bf16[128,1664]{1,0:T(8,128)(2,1)S(1)}, u32[]{:S(2)}, u32[]{:S(2)}) collective-permute-start(bf16[128,1664]{1,0:T(8,128)(2,1)S(1)} %pad_maximum_fusion.20), channel_id=1, source_target_pairs={{0,16},{16,0},{1,17},{17,1},{2,18},{18,2},{3,19},{19,3},{4,20},{20... | collective-permute-start | bytes 1277960 | tf_op jit(solution)/shard_map/ppermute | solution.py:463
  175.2 20.3 %collective-permute-start.21 = (bf16[128,1664]{1,0:T(8,128)(2,1)S(1)}, bf16[128,1664]{1,0:T(8,128)(2,1)S(1)}, u32[]{:S(2)}, u32[]{:S(2)}) collective-permute-start(bf16[128,1664]{1,0:T(8,128)(2,1)S(1)} %pad_maximum_fusion.19), channel_id=1, source_target_pairs={{0,8},{8,0},{1,9},{9,1},{2,10},{10,2},{3,11},{11,3},{4,12},{12,4},... | collective-permute-start | bytes 1277960 | tf_op jit(solution)/shard_map/ppermute | solution.py:463
  197.1 20.9 %collective-permute-start.26 = (bf16[128,1536]{1,0:T(8,128)(2,1)}, bf16[128,1536]{1,0:T(8,128)(2,1)}, u32[]{:S(2)}, u32[]{:S(2)}) collective-permute-start(bf16[128,1536]{1,0:T(8,128)(2,1)} %multiply_convert_fusion), channel_id=1, source_target_pairs={{0,16},{16,0},{1,17},{17,1},{2,18},{18,2},{3,19},{19,3},{4,20},{20... | collective-permute-start | bytes 1179656 | tf_op jit(solution)/shard_map/ppermute | solution.py:463
  197.4 20.7 %collective-permute-start.27 = (bf16[128,1536]{1,0:T(8,128)(2,1)}, bf16[128,1536]{1,0:T(8,128)(2,1)}, u32[]{:S(2)}, u32[]{:S(2)}) collective-permute-start(bf16[128,1536]{1,0:T(8,128)(2,1)} %multiply_convert_fusion), channel_id=1, source_target_pairs={{0,8},{8,0},{1,9},{9,1},{2,10},{10,2},{3,11},{11,3},{4,12},{12,4},... | collective-permute-start | bytes 1179656 | tf_op jit(solution)/shard_map/ppermute | solution.py:463
  263.5 128.6 %reduce-scatter.13.cloned.1.call-start = ((), (), s32[]{:S(2)}) async-start(), calls=%async_computation.13 | async-start | bytes 4423680
  321.8 19.6 %collective-permute-start.46 = (bf16[128,1536]{1,0:T(8,128)(2,1)}, bf16[128,1536]{1,0:T(8,128)(2,1)S(1)}, u32[]{:S(2)}, u32[]{:S(2)}) collective-permute-start(bf16[128,1536]{1,0:T(8,128)(2,1)} %pad_maximum_fusion.27), channel_id=1, source_target_pairs={{0,16},{16,0},{1,17},{17,1},{2,18},{18,2},{3,19},{19,3},{4,20},{20... | collective-permute-start | bytes 1179656 | tf_op jit(solution)/shard_map/ppermute | solution.py:463
  322.9 19.4 %collective-permute-start.45 = (bf16[128,1536]{1,0:T(8,128)(2,1)}, bf16[128,1536]{1,0:T(8,128)(2,1)}, u32[]{:S(2)}, u32[]{:S(2)}) collective-permute-start(bf16[128,1536]{1,0:T(8,128)(2,1)} %pad_maximum_fusion.26), channel_id=1, source_target_pairs={{0,8},{8,0},{1,9},{9,1},{2,10},{10,2},{3,11},{11,3},{4,12},{12,4},... | collective-permute-start | bytes 1179656 | tf_op jit(solution)/shard_map/ppermute | solution.py:463
  342.4 166.2 %reduce-scatter.11.cloned.1.call-start = ((), (), s32[]{:S(2)}) async-start(), calls=%async_computation.12 | async-start | bytes 1474560 | tf_op jit(solution)/shard_map/reduce_scatter | solution.py:996
  348.1 21.9 %collective-permute-start.48 = (bf16[128,1664]{1,0:T(8,128)(2,1)S(1)}, bf16[128,1664]{1,0:T(8,128)(2,1)S(1)}, u32[]{:S(2)}, u32[]{:S(2)}) collective-permute-start(bf16[128,1664]{1,0:T(8,128)(2,1)S(1)} %pad_maximum_fusion.21), channel_id=1, source_target_pairs={{0,16},{16,0},{1,17},{17,1},{2,18},{18,2},{3,19},{19,3},{4,20},{20... | collective-permute-start | bytes 1277960 | tf_op jit(solution)/shard_map/ppermute | solution.py:463
  348.4 21.8 %collective-permute-start.49 = (bf16[128,1664]{1,0:T(8,128)(2,1)S(1)}, bf16[128,1664]{1,0:T(8,128)(2,1)S(1)}, u32[]{:S(2)}, u32[]{:S(2)}) collective-permute-start(bf16[128,1664]{1,0:T(8,128)(2,1)S(1)} %pad_maximum_fusion.21), channel_id=1, source_target_pairs={{0,8},{8,0},{1,9},{9,1},{2,10},{10,2},{3,11},{11,3},{4,12},{12,4},... | collective-permute-start | bytes 1277960 | tf_op jit(solution)/shard_map/ppermute | solution.py:463
  392.1 27.8 %all-to-all-start.2 = ((bf16[8,3,48,384]{3,2,1,0:T(8,128)(2,1)}), bf16[8,3,48,384]{3,2,1,0:T(8,128)(2,1)S(1)}, u32[]{:S(2)}, u32[]{:S(2)}) async-start(bf16[8,3,48,384]{3,2,1,0:T(8,128)(2,1)} %bitcast.340), calls=%async_computation.3 | async-start | bytes 1769472 | tf_op jit(solution)/shard_map/all_to_all | solution.py:824
  395.8 112.8 %reduce-scatter.9.cloned.1.call-start = ((), (), s32[]{:S(2)}) async-start(), calls=%async_computation.11 | async-start | bytes 1474560 | tf_op jit(solution)/shard_map/reduce_scatter | solution.py:1023
  466.8 26.9 %collective-permute-start.64 = (bf16[24,48,384]{2,1,0:T(8,128)(2,1)}, bf16[24,48,384]{2,1,0:T(8,128)(2,1)}, u32[]{:S(2)}, u32[]{:S(2)}) collective-permute-start(bf16[24,48,384]{2,1,0:T(8,128)(2,1)} %pad_maximum_fusion.7), channel_id=1, source_target_pairs={{0,2},{2,0},{1,3},{3,1},{4,6},{6,4},{5,7},{7,5},{8,10},{10,8},{9,1... | collective-permute-start | bytes 2654216 | tf_op jit(solution)/shard_map/ppermute | solution.py:463
  469.2 26.7 %collective-permute-start.63 = (bf16[24,48,384]{2,1,0:T(8,128)(2,1)}, bf16[24,48,384]{2,1,0:T(8,128)(2,1)}, u32[]{:S(2)}, u32[]{:S(2)}) collective-permute-start(bf16[24,48,384]{2,1,0:T(8,128)(2,1)} %pad_maximum_fusion.6), channel_id=1, source_target_pairs={{0,1},{1,0},{2,3},{3,2},{4,5},{5,4},{6,7},{7,6},{8,9},{9,8},{10,11... | collective-permute-start | bytes 2654216 | tf_op jit(solution)/shard_map/ppermute | solution.py:463
  498.6 29.2 %all-to-all-start.3 = ((bf16[8,3,48,384]{3,2,1,0:T(8,128)(2,1)}), bf16[8,3,48,384]{3,2,1,0:T(8,128)(2,1)S(1)}, u32[]{:S(2)}, u32[]{:S(2)}) async-start(bf16[8,3,48,384]{3,2,1,0:T(8,128)(2,1)} %bitcast.325), calls=%async_computation.4 | async-start | bytes 1769472 | tf_op jit(solution)/shard_map/all_to_all | solution.py:824
  (151 other events, 1116.5 us)
Sparse Core Ops, SparseCore 0:
  21.6 35.1 all-gather.2
  155.6 29.4 all-gather.4
  263.6 39.6 reduce-scatter.6
  342.5 46.5 reduce-scatter.12
  392.4 28.5 reduce-scatter.10
  470.4 34.5 reduce-scatter.8

commit v4 on v3

--- a/solution.py
+++ b/solution.py
@@ -157,10 +157,8 @@
     y = within + carried + skip_ref[0:1, :] * x
     gate = proj[:, :wide].astype(F32)
     gated = (y * (gate * jax.nn.sigmoid(gate))).astype(BF16)
-    if not with_sums:
-        put(gated_ref, core, gated, 0, wide)
-    else:
-        gated_ref[...] = gated
+    put(gated_ref, core, gated, 0, wide)
+    if with_sums:
         gated = gated.astype(F32)
         ones = jnp.ones((8, wide), BF16)
         product = gated * take(refs[0], core).astype(F32)
@@ -178,7 +176,6 @@
     count = length // STRETCH
     whole = lambda shape: pl.BlockSpec(shape, lambda i, at: (0,) * len(shape))
     part = lambda cols: pl.BlockSpec((STRETCH, cols), lambda i, at: (i ^ (at[0] >> 1), 0))
-    plain = pl.BlockSpec((STRETCH, wide), lambda i, at: (i, 0))
     return pl.pallas_call(
         functools.partial(mix_forward_kernel, with_sums=with_sums),
         grid_spec=pltpu.PrefetchScalarGridSpec(
@@ -192,7 +189,7 @@
             ]
             + [part(wide)] * with_sums,
             out_specs=[
-                plain if with_sums else part(wide),
+                part(wide),
                 part(wide),
                 pl.BlockSpec((1, NSTATE, wide), lambda i, at: (i, 0, 0)),
             ]
@@ -291,12 +288,16 @@
         kappa = rho * rho * rho * sums[:, 1:2] / DI
         g_gated = rho * g_gated - gated * kappa
         put(refs[4], core, (gated * rho).astype(BF16), 0, wide)
+        copies = []
     else:
+        copies = [refs[4], refs[5]]
         g_gated = take(pulled_ref, core).astype(F32)
         g_gated = g_gated - gated * take(kappa_ref, core)[:, 0:1].astype(F32)
     dy = g_gated * gate_act
     g_gate = g_gated * y * (gate_sig * (1.0 + gate * (1.0 - gate_sig)))
     put(out_ref, core, g_gate.astype(BF16), 0, wide)
+    for copy_ref in copies[:1]:
+        put(copy_ref, core, g_gate.astype(BF16), 0, wide)
     dy_low = dy.astype(BF16)
     skip_grad_ref[0:1, :] += jnp.sum(x * dy, axis=0, keepdims=True)
 
@@ -354,6 +355,8 @@
     head_grad_ref[1:2, :] -= jnp.sum(step * scaled_decay, axis=0, keepdims=True)
     g_raw = pltpu.roll(g_raw, lax.rem(LANES - turned, LANES), 1)
     put(out_ref, core, g_raw.astype(BF16), wide + chans, wide + chans + LANES)
+    for copy_ref in copies[1:]:
+        put(copy_ref, core, g_raw.astype(BF16), chans, chans + LANES)
 
     d_low = d_scores.astype(BF16)
     ending = (x * (step_wide * to_end)).astype(BF16)
@@ -369,6 +372,8 @@
     for lag in range(CONV - 1):
         g_in = g_in + conv_ref[lag : lag + 1, :] * gext_ref[3 - lag : 3 - lag + rows, :]
     put(out_ref, core, g_in.astype(BF16), wide, wide + chans)
+    for copy_ref in copies[1:]:
+        put(copy_ref, core, g_in.astype(BF16), 0, chans)
     for lag in range(CONV):
         conv_grad_ref[lag : lag + 1, :] += jnp.sum(
             ext_ref[5 + lag : 5 + lag + rows, :] * g_pre, axis=0, keepdims=True
@@ -419,7 +424,7 @@
                 whole((8, LANES)),
                 whole((8, wide)),
             ]
-            + [part(wide)] * as_rows,
+            + ([part(wide)] if as_rows else [part(wide), part(width - wide)]),
             scratch_shapes=[
                 pltpu.VMEM((NSTATE, wide), F32),
                 pltpu.VMEM((STRETCH + 8, wide + BC), F32),
@@ -433,7 +438,8 @@
             jax.ShapeDtypeStruct((8, LANES), F32),
             jax.ShapeDtypeStruct((8, wide), F32),
         ]
-        + [jax.ShapeDtypeStruct((length, wide), BF16)] * as_rows,
+        + [jax.ShapeDtypeStruct((length, wide), BF16)]
+        + [jax.ShapeDtypeStruct((length, width - wide), BF16)] * (not as_rows),
         compiler_params=pltpu.CompilerParams(
             dimension_semantics=("arbitrary",), vmem_limit_bytes=CAP
         ),
@@ -465,6 +471,34 @@
 
 def flip_both(values, names):
     return lax.ppermute(values, names, [(0, 3), (1, 2), (2, 1), (3, 0)])
+
+
+def turn_back(own, near, far, residual, rho, grad, gate_rho, branch):
+    rows, model = own.shape
+
+    def kernel(own_ref, near_ref, far_ref, res_ref, rho_ref, grad_ref, gate_ref, br_ref, *refs):
+        grad_out, sent_out = refs
+        weighed = own_ref[...].astype(F32) + near_ref[...].astype(F32) + far_ref[...].astype(F32)
+        res, rho, gate = res_ref[...], rho_ref[...], gate_ref[...]
+        mean = jnp.sum(weighed * res, axis=1, keepdims=True) / model
+        total = grad_ref[...].astype(F32) + rho * weighed - res * (rho * rho * rho * mean)
+        grad_out[...] = total
+        pulled = total * gate
+        kappa = gate * gate * jnp.sum(pulled * br_ref[...], axis=1, keepdims=True) / DI
+        sent_out[:, :model] = pulled.astype(BF16)
+        sent_out[:, model:] = jnp.broadcast_to(kappa, (rows, LANES)).astype(BF16)
+
+    return pl.pallas_call(
+        kernel,
+        in_specs=all_vmem(8),
+        out_specs=all_vmem(2),
+        out_shape=[
+            jax.ShapeDtypeStruct((rows, model), F32),
+            jax.ShapeDtypeStruct((rows, model + LANES), BF16),
+        ],
+        compiler_params=pltpu.CompilerParams(vmem_limit_bytes=CAP),
+        name="turn_back",
+    )(own, near, far, residual, rho, grad, gate_rho, branch)
 
 
 class Axes:
@@ -591,54 +625,84 @@
 def cut_in(axes, place, grad, spare, depth, wide, relative):
     copies, team = 2 ** len(axes.copies), 2 ** len(axes.team)
     parts = grad.shape[1] // wide
-    extra, room = spare.shape[1:]
+    pairs_at = [(r, k) for r in range(copies) for k in range(team)]
+    if spare is not None:
+        extra, room = spare.shape[1:]
     if depth % 16:
-        flat = grad.reshape(copies * team, depth, -1).at[:, :extra, -room:].set(spare)
-        at = [axes.at(place[2], r, k, relative) for r in range(copies) for k in range(team)]
-        flat = jnp.take(flat, jnp.stack(at), axis=0)
-        flat = [
-            flat[:, :, columns_of(part, wide) : columns_of(part, wide) + wide]
-            for part in range(parts)
-        ]
-        return jnp.stack(flat, axis=1).reshape(copies, team * parts, depth, wide)
-
-    def kernel(place_ref, grad_ref, spare_ref, out_ref):
-        for r in range(copies):
-            for k in range(team):
-                spot = axes.at(place_ref[2], r, k, relative)
-                rows = pl.ds(pl.multiple_of(spot * depth, 16), depth)
-                for part in range(parts):
-                    base = columns_of(part, wide)
-                    out_ref[r, parts * k + part] = grad_ref[rows, base : base + wide]
-                out_ref[r, parts * k + parts - 1, 0:extra, wide - room :] = spare_ref[spot]
-
+        flat = grad.reshape(copies * team, depth, -1)
+        if spare is not None:
+            flat = flat.at[:, :extra, -room:].set(spare)
+        at = jnp.stack([axes.at(place[2], r, k, relative) for r, k in pairs_at])
+        flat = jnp.take(flat, at, axis=0).reshape(copies, team, depth, parts, wide)
+        flat = flat.transpose(0, 1, 3, 2, 4).reshape(copies, team * parts, depth, wide)
+        return [flat[r] for r in range(copies)]
+
+    def kernel(place_ref, grad_ref, *refs):
+        out_refs = refs[-copies:]
+        for r, k in pairs_at:
+            spot = axes.at(place_ref[2], r, k, relative)
+            rows = pl.ds(pl.multiple_of(spot * depth, 16), depth)
+            for part in range(parts):
+                out_refs[r][parts * k + part] = grad_ref[rows, part * wide : (part + 1) * wide]
+            if spare is not None:
+                out_refs[r][parts * k + parts - 1, 0:extra, wide - room :] = refs[0][spot]
+
+    given = [] if spare is None else [spare]
     return pl.pallas_call(
         kernel,
-        in_specs=[SMEM] + all_vmem(2),
-        out_specs=pl.BlockSpec(memory_space=pltpu.VMEM),
-        out_shape=jax.ShapeDtypeStruct((copies, team * parts, depth, wide), BF16),
+        in_specs=[SMEM] + all_vmem(1 + len(given)),
+        out_specs=all_vmem(copies),
+        out_shape=[jax.ShapeDtypeStruct((team * parts, depth, wide), BF16)] * copies,
         compiler_params=pltpu.CompilerParams(vmem_limit_bytes=CAP),
         name="cut_in",
-    )(place, grad, spare)
+    )(place, grad, *given)
+
+
+def join_out(axes, place, blocks, grad):
+    copies = len(blocks)
+    count, depth, wide = blocks[0].shape
+    each, model = grad.shape[0] // copies, grad.shape[1]
+    more = (each // depth) * (model // wide)
+
+    def kernel(place_ref, grad_ref, *refs):
+        block_refs, out_refs = refs[:copies], refs[copies:]
+        for r in range(copies):
+            out_refs[r][0:count] = block_refs[r][...]
+            copy = (place_ref[2] & axes.bits(axes.copies, -1)) ^ axes.bits(axes.copies, r)
+            for at in range(more):
+                row, column = at // (model // wide), at % (model // wide)
+                first = copy * each + row * depth
+                out_refs[r][count + at] = grad_ref[
+                    pl.ds(pl.multiple_of(first, 16), depth), column * wide : (column + 1) * wide
+                ]
+
+    return pl.pallas_call(
+        kernel,
+        in_specs=[SMEM] + all_vmem(1 + copies),
+        out_specs=all_vmem(copies),
+        out_shape=[jax.ShapeDtypeStruct((count + more, depth, wide), BF16)] * copies,
+        compiler_params=pltpu.CompilerParams(vmem_limit_bytes=CAP),
+        name="join_out",
+    )(place, grad, *blocks)
 
 
 def finish_in(axes, grads, weight, gain):
     layers, depth, columns = weight.shape
     team = 2 ** len(axes.team)
     wide = DI // team
-    parts = grads[0].shape[1]
-    room = parts * wide - 2 * wide - (columns - 2 * DI)
+    parts = grads[0][1].shape[1]
+    room = (parts - 1) * wide - (columns - 2 * DI)
 
     def kernel(weight_ref, gain_ref, *refs):
         grad_ref, sum_ref, spare_ref = refs[-3:]
         for layer in range(layers):
-            blocks_ref = refs[layer]
+            gate_ref, rest_ref = refs[2 * layer : 2 * layer + 2]
             scale = gain_ref[layer].astype(F32)
             tails = []
-            for part in range(2, parts):
-                tail = blocks_ref[0, part].astype(F32)
+            for part in range(1, parts):
+                tail = rest_ref[0, part].astype(F32)
                 for k in range(1, team):
-                    tail = tail + blocks_ref[k, part].astype(F32)
+                    tail = tail + rest_ref[k, part].astype(F32)
                 tails.append(tail)
             tail = jnp.concatenate(tails, axis=1)
             spare_ref[layer] = tail[:, columns - 2 * DI :]
@@ -646,20 +710,18 @@
             grad_ref[layer, :, 2 * DI :] = tail * scale
             total = jnp.sum(tail * weight_ref[layer, :, 2 * DI :].astype(F32), 1, keepdims=True)
             for k in range(team):
-                for part in range(2):
-                    values = blocks_ref[k, part].astype(F32)
-                    base = (1 - part) * DI + k * wide
-                    grad_ref[layer, :, base : base + wide] = values * scale
+                for base, values in ((0, gate_ref[k, 0]), (DI, rest_ref[k, 0])):
+                    values = values.astype(F32)
+                    spot = slice(base + k * wide, base + (k + 1) * wide)
+                    grad_ref[layer, :, spot] = values * scale
                     total = total + jnp.sum(
-                        values * weight_ref[layer, :, base : base + wide].astype(F32),
-                        1,
-                        keepdims=True,
+                        values * weight_ref[layer, :, spot].astype(F32), 1, keepdims=True
                     )
             sum_ref[layer] = jnp.broadcast_to(total, (depth, LANES))
 
     grads, sums, spares = pl.pallas_call(
         kernel,
-        in_specs=all_vmem(2 + layers),
+        in_specs=all_vmem(2 + 2 * layers),
         out_specs=all_vmem(3),
         out_shape=[
             jax.ShapeDtypeStruct((layers, depth, columns), F32),
@@ -668,7 +730,7 @@
         ],
         compiler_params=pltpu.CompilerParams(vmem_limit_bytes=CAP),
         name="finish_in",
-    )(weight, gain[..., None], *grads)
+    )(weight, gain[..., None], *[part for pair in grads for part in pair])
     return grads, sums[:, :, 0], spares
 
 
@@ -688,25 +750,34 @@
     return flip(one[:half], slow), flip(two[half:], fast)
 
 
+def copies_whole_corner(axes, parts):
+    return (flip(parts[1], axes.copies[0]),)
+
+
 def copies_lists(parts, corner):
     count = parts[0].shape[0]
-    half = count // 2
+    each = count // len(corner)
     lists = [[(array, at) for at in range(count)] for array in parts]
-    return lists + [[(corner[at // half], at % half) for at in range(count)]]
+    return lists + [[(corner[at // each], at % each) for at in range(count)]]
 
 
 def sum_corner(axes, pieces):
     slow, fast = axes.copies
-    half = pieces.shape[1] // 2
-    return flip(pieces[3, :half], slow), flip(pieces[3, half:], fast)
+    half = pieces[3].shape[0] // 2
+    return flip(pieces[3][:half], slow), flip(pieces[3][half:], fast)
 
 
 def sum_sides(axes, pieces, corner):
     slow, fast = axes.copies
-    half = pieces.shape[1] // 2
-    to_fast = jnp.concatenate([add_low(pieces[1, :half], corner[0]), pieces[1, half:]], axis=0)
-    to_slow = jnp.concatenate([pieces[2, :half], add_low(pieces[2, half:], corner[1])], axis=0)
+    half = pieces[0].shape[0] // 2
+    to_fast = jnp.concatenate([add_low(pieces[1][:half], corner[0]), pieces[1][half:]], axis=0)
+    to_slow = jnp.concatenate([pieces[2][:half], add_low(pieces[2][half:], corner[1])], axis=0)
     return flip(to_fast, fast), flip(to_slow, slow)
+
+
+def sum_direct(axes, pieces):
+    slow, fast = axes.copies
+    return flip(pieces[1], fast), flip(pieces[2], slow), flip_both(pieces[3], axes.copies)
 
 
 def gather_start(axes, rows):
@@ -719,12 +790,10 @@
 def gather_corner(axes, parts):
     if len(axes.links) != 2:
         return parts, []
-    far, near = axes.links
     rows, other, from_far, from_near = parts
-    half = rows.shape[0] // 2
     sides = jnp.stack([from_near, from_far])
     sides = jnp.stack([sides, flip(sides, "c")], axis=1).reshape(-1, rows.shape[1])
-    corner = flip(from_near[:half], far), flip(from_far[half:], near)
+    corner = (flip(from_far, axes.links[1]),)
     return corner, [jnp.concatenate([rows, other], axis=0), sides]
 
 
@@ -735,25 +804,22 @@
             whole = jnp.concatenate([whole, flip(whole, name)], axis=0)
         whole = jnp.stack([whole, flip(whole, "c")], axis=1)
         return whole.reshape(-1, corner[0].shape[1])
-    last = jnp.concatenate(corner, axis=0)
-    return jnp.concatenate([last, flip(last, "c")], axis=0)
-
-
-def core_sum(rows_of, first, last, rows):
-    both = rows_of(first, last).reshape(-1, 2, rows, rows_of.columns)
+    return jnp.concatenate([corner[0], flip(corner[0], "c")], axis=0)
+
+
+def core_sum(values, rows):
+    both = values.reshape(-1, 2, rows, values.shape[-1])
     return add_low(both[:, 0], flip(both[:, 1], "c"))
 
 
 def scatter_corner(axes, rows_of, rows):
     team = 2 ** len(axes.team)
     if len(axes.links) != 2:
-        return (core_sum(rows_of, 0, team * rows, rows),)
-    far, near = axes.links
-    corner = core_sum(rows_of, 6 * rows, 8 * rows, rows)[0]
-    half = rows // 2
-    hops = flip(corner[:half], far), flip(corner[half:], near)
-    sides = core_sum(rows_of, 2 * rows, 6 * rows, rows)
-    return hops, sides, core_sum(rows_of, 0, 2 * rows, rows)[0]
+        return (core_sum(rows_of(0, team * rows, ()), rows),)
+    corner = core_sum(rows_of(6 * rows, 8 * rows, ()), rows)[0]
+    hop = flip(corner, axes.links[1])
+    sides = core_sum(rows_of(2 * rows, 6 * rows, corner), rows)
+    return hop, sides, core_sum(rows_of(0, 2 * rows, corner), rows)[0]
 
 
 def scatter_sides(axes, parts):
@@ -764,11 +830,8 @@
             whole = add_low(whole[:half], flip(whole[half:], name))
         return (whole[0],)
     far, near = axes.links
-    hops, sides, own = parts
-    half = own.shape[0] // 2
-    to_near = jnp.concatenate([add_low(sides[0, :half], hops[0]), sides[0, half:]], axis=0)
-    to_far = jnp.concatenate([sides[1, :half], add_low(sides[1, half:], hops[1])], axis=0)
-    return own, flip(to_near, near), flip(to_far, far)
+    hop, sides, own = parts
+    return own, flip(sides[0], near), flip(add_low(sides[1], hop), far)
 
 
 def add_all(parts):
@@ -776,14 +839,6 @@
     for part in parts[1:]:
         total = total + part.astype(F32)
     return total
-
-
-class Rows:
-    def __init__(self, make, columns):
-        self.make, self.columns = make, columns
-
-    def __call__(self, first, last):
-        return self.make(first, last)
 
 
 def local(
@@ -880,17 +935,17 @@
     blocks = in_blocks(1, last)
     gated_0, y_0, enter_0 = mix_forward(place, proj_0, conv[0], head[0], skip[0])
     cot_hops, cot = gather_corner(axes, cot)
-    gated_0, blocks, cot_hops = together(gated_0, blocks, cot_hops)
+    (gated_0, y_0, enter_0), blocks, cot_hops = together((gated_0, y_0, enter_0), blocks, cot_hops)
     cot = cot + [gather_end(axes, cot_hops)]
     weight_out_1 = out_rows(1, gated_0)
 
-    def branch_rows(begin, end):
-        cut = gated_0[begin:end]
+    def branch_rows(begin, end, others):
+        cut = after(gated_0, others)[begin:end]
         squares = jnp.sum(jnp.square(cut.astype(F32)), axis=1, keepdims=True)
         squares = jnp.broadcast_to(squares, (end - begin, LANES))
         return jnp.concatenate([mm(cut, weight_out_0), squares], axis=1).astype(BF16)
 
-    got = together(*scatter_corner(axes, Rows(branch_rows, model + LANES), rows))
+    got = together(*scatter_corner(axes, branch_rows, rows))
     got = scatter_sides(axes, got)
     if paired:
         got, copied = together(got, copies_start(axes, blocks))
@@ -903,7 +958,9 @@
     gathered = gather_start(axes, (residual_1 * rho_1).astype(BF16))
     g_scaled = jnp.concatenate([mm_nt(piece, weight_out_1).astype(BF16) for piece in cot], axis=0)
     if paired:
-        gathered, corner, g_scaled = together(gathered, copies_corner(axes, copied), g_scaled)
+        gathered, corner, g_scaled = together(
+            gathered, copies_whole_corner(axes, copied), g_scaled
+        )
         weight_in_1 = join_in(axes, place, copies_lists(copied, corner), True)[0]
     else:
         weight_in_1 = in_columns(blocks)[0]
@@ -924,12 +981,16 @@
     else:
         for name in axes.links:
             sums = sums + flip(sums, name)
-    branch_1 = mm(gated_1, weight_out_1).astype(BF16)
-    sums, branch_1 = together(sums, branch_1)
-    branch_1 = lax.psum_scatter(branch_1, axes.team, scatter_dimension=0, tiled=True)
-    g_proj, g_conv, g_head, g_skip, scaled_1 = mix_backward(
+
+    def last_rows(begin, end, others):
+        return mm(after(gated_1, others)[begin:end], weight_out_1).astype(BF16)
+
+    sums, branch_1 = together(sums, scatter_corner(axes, last_rows, rows))
+    branch_1 = scatter_sides(axes, branch_1)
+    outs = mix_backward(
         place, proj_1, y_1, g_scaled, sums, enter_1, conv[1], head[1], skip[1], True
     )
+    (g_proj, g_conv, g_head, g_skip, scaled_1), branch_1 = together(outs, branch_1)
     got_1 = jnp.concatenate(after(cot, g_proj), axis=0)
     normed = jnp.concatenate(after(pieces_1, g_proj), axis=0)
 
@@ -959,69 +1020,83 @@
         more = -spare.shape[1] % 16 if depth % 16 == 0 else 0
         return jnp.pad(spare, ((0, 0), (0, more), (0, 0))).astype(BF16)
 
-    def in_gradient(normed, g_proj, g_conv, g_head, g_skip, quick):
+    def in_gradient(normed, g_proj, beside, quick):
+        spare = None if beside is None else spare_rows(*beside)
         g_in = mm_tn(normed, g_proj).astype(BF16)
-        spare = spare_rows(g_conv, g_head, g_skip)
         return cut_in(axes, place, g_in, spare, depth, wide, quick)
 
     def copies_scatter(values):
-        return lax.psum_scatter(values, axes.copies, scatter_dimension=0)
+        return lax.psum_scatter(jnp.stack(values), axes.copies, scatter_dimension=0)
 
     def owned(summed):
-        return team_swap(summed.reshape(team, parts, depth, wide))
+        return team_swap(summed.reshape(team, -1, depth, wide))
 
     def weighed_rows(g_proj, weight_in):
-        make = lambda begin, end: mm_nt(g_proj[begin:end], weight_in).astype(BF16)
-        return Rows(make, model)
-
-    weighed = scatter_corner(axes, weighed_rows(g_proj, weight_in_1), rows)
-    weighed, branch_1 = together(weighed, branch_1)
+        def make(begin, end, others):
+            return mm_nt(after(g_proj, others)[begin:end], weight_in).astype(BF16)
+
+        return make
+
+    weighed = together(*scatter_corner(axes, weighed_rows(g_proj, weight_in_1), rows))
     weighed = scatter_sides(axes, weighed)
-    blocks = in_gradient(normed, after(g_proj, weighed[0]), g_conv, g_head, g_skip, False)
+    g_late = after(g_proj, weighed[0])
+    blocks = in_gradient(normed, g_late, (g_conv, g_head, g_skip), False)
     weighed, blocks = together(weighed, blocks)
     summed = copies_scatter(blocks)
     squares = lax.dynamic_slice_in_dim(sums, me * rows, rows, 1)[0][:, None]
-    out = (residual_1 + lax.rsqrt(squares / DI + eps) * branch_1.astype(F32)).astype(BF16)
-    weighed = add_all(weighed)
-    mean = jnp.mean(weighed * residual_1, axis=1, keepdims=True)
-    grad = cotangent[0].astype(F32)
-    grad = grad + rho_1 * weighed - residual_1 * (rho_1 * rho_1 * rho_1 * mean)
-
-    pulled = grad * gate_rho_0
-    kappa = gate_rho_0 * gate_rho_0 * jnp.sum(pulled * branch_0, axis=1, keepdims=True) / DI
-    sent = jnp.concatenate([pulled, jnp.broadcast_to(kappa, (rows, LANES))], axis=1)
-    gathered = gather_start(axes, sent.astype(BF16))
+    out = (residual_1 + lax.rsqrt(squares / DI + eps) * add_all(branch_1)).astype(BF16)
+    if len(weighed) == 1:
+        weighed = weighed + (jnp.zeros_like(weighed[0]),) * 2
+
+    grad, sent = turn_back(
+        *weighed, residual_1, rho_1, cotangent[0], gate_rho_0, branch_0
+    )
+    gathered = gather_start(axes, sent)
     g_out = mm_tn(scaled_1, got_1).astype(BF16)
     gathered, g_out = together(gathered, g_out)
     g_out_1 = lax.psum_scatter(g_out, axes.copies, scatter_dimension=0, tiled=True)
     hops, pieces = gather_corner(axes, gathered)
     g_scaled = [mm_nt(piece[:, :model], weight_out_0).astype(BF16) for piece in pieces]
-    hops, g_scaled = together(hops, g_scaled)
+    normed = jnp.concatenate(after(pieces_0, gathered), axis=0)
+    hops, g_scaled, normed = together(hops, g_scaled, normed)
     last = gather_end(axes, hops)
     pieces = pieces + [last]
     g_scaled = g_scaled + [mm_nt(last[:, :model], weight_out_0).astype(BF16)]
     g_scaled = jnp.concatenate(g_scaled, axis=0)
     kappa = jnp.concatenate([piece[:, model:] for piece in pieces], axis=0)
-    g_proj, g_conv, g_head, g_skip = mix_backward(
-        place, proj_0, y_0, g_scaled, after(kappa, summed), enter_0, conv[0], head[0], skip[0], False
+    kappa = after(kappa, summed)
+    outs = mix_backward(
+        place, proj_0, y_0, g_scaled, kappa, enter_0, conv[0], head[0], skip[0], False
     )
-    g_proj, owned_1 = together(g_proj, owned(summed))
-    normed = jnp.concatenate(after(pieces_0, g_proj), axis=0)
+    outs, owned_1 = together(outs, owned(summed))
+    g_proj, g_conv, g_head, g_skip, g_gate, g_rest = outs
+    owned_1 = owned_1[:, :1], owned_1[:, 1:]
     got = jnp.concatenate([piece[:, :model] for piece in after(pieces, g_proj)], axis=0)
-    blocks = in_gradient(normed, g_proj, g_conv, g_head, g_skip, paired)
-    weighed = scatter_corner(axes, weighed_rows(after(g_proj, blocks), weight_in_0), rows)
+    beside = g_conv, g_head, g_skip
     g_out = mm_tn(gated_0, got).astype(BF16)
     if paired:
-        corner = sum_corner(axes, blocks)
-        weighed, corner, g_out = together(weighed, corner, g_out)
+        gates = in_gradient(normed, g_gate, None, True)
+        gates = join_out(axes, place, gates, g_out)
+        g_proj = after(g_proj, gates)
+    weighed = scatter_corner(axes, weighed_rows(g_proj, weight_in_0), rows)
+    if paired:
+        weighed, gate_parts = together(weighed, sum_direct(axes, gates))
         weighed = scatter_sides(axes, weighed)
-        weighed, sides = together(weighed, sum_sides(axes, blocks, corner))
-        summed = add_low(blocks[0], *sides)
+        rests = in_gradient(normed, after(g_rest, gate_parts), beside, True)
+        corner = sum_corner(axes, rests)
+        weighed, corner = together(weighed, corner)
+        gates = add_low(gates[0], *gate_parts)
+        g_out_0 = gates[team:].reshape(-1, model // wide, depth, wide)
+        g_out_0 = g_out_0.transpose(0, 2, 1, 3).reshape(-1, model)
+        gates = owned(gates[:team])
+        sides, gates = together(sum_sides(axes, rests, corner), gates)
+        rests = owned(add_low(rests[0], *sides))
     else:
         weighed = scatter_sides(axes, weighed)
-        summed = copies_scatter(blocks)
-    g_out_0 = lax.psum_scatter(g_out, axes.copies, scatter_dimension=0, tiled=True)
-    owned_0 = owned(summed)
+        gates = owned(copies_scatter(in_gradient(normed, g_gate, None, False)))
+        rests = owned(copies_scatter(in_gradient(normed, g_rest, beside, False)))
+        g_out_0 = lax.psum_scatter(g_out, axes.copies, scatter_dimension=0, tiled=True)
+    owned_0 = gates, rests
     weighed = add_all(weighed)
     mean = jnp.mean(weighed * residual_0, axis=1, keepdims=True)
     grad = grad + rho_0 * weighed - residual_0 * (rho_0 * rho_0 * rho_0 * mean)

time: 548 us -> 533 us (0.973)
  waiting for transfers between devices: 182 us -> 194 us
  local copies, waits for them, and re-layouts: 58.3 us -> 46.4 us
  Pallas kernels: 83.2 us -> 77 us
    all_to_all x4 -> x5, waiting for transfers between devices: 37.2 us -> 47.3 us  [team_swap(): return lax.all_to_all(blocks, axes.team, split_axis=0, concat_axis=0)]
    ppermute x64, waiting for transfers between devices: 145 us -> 136 us  [flip(): return lax.ppermute(values, axis, [(0, 1), (1, 0)])]
    ppermute x1 -> x2, waiting for transfers between devices: 0.01 us -> 8.63 us  [flip_both(): return lax.ppermute(values, names, [(0, 3), (1, 2), (2, 1), (3, 0)])]
    dot_general x12, matrix products: 17.7 us -> 26 us  [mm_nt(): lax.dot_general(left, right, (((1,), (1,)), ((), ())), preferred_element_...]
    ppermute x64, starting transfers between devices: 56.5 us -> 48.2 us  [flip(): return lax.ppermute(values, axis, [(0, 1), (1, 0)])]
    pallas_call x2, Pallas kernels: 50.8 us -> 43.2 us  [mix_backward(): pl.pallas_call(functools.partial(mix_backward_kernel, as_rows=as_rows), g...]
    squeeze x3 -> x8, other arithmetic: 2.19 us -> 8 us  [the longest x4 4.01 us: scatter_corner(): corner = core_sum(rows_of(6 * rows, 8 * rows, ()), rows)[0]]
    dot_general x4 -> x5, matrix products: 21.5 us -> 17.6 us  [mm_tn(): lax.dot_general(left, right, (((0,), (0,)), ((), ())), preferred_element_...]
  transfers between devices with their start and end apart: 75 -> 75, of which waited for: 36 -> 32; matrix products, arithmetic and copies ran while one was open for 24% -> 23% of each run, Pallas kernels for 13% -> 12%
where the time goes in v4:
time: 533 us; the launch traced here: 526 us
  waiting for transfers between devices  194 us (36%)
  Pallas kernels  77 us (14%)
  starting transfers between devices  74.6 us (14%)
  matrix products  66.8 us (13%)
  other arithmetic  50.8 us (10%)
  local copies, waits for them, and re-layouts  46.4 us (9%)
  between operations  16.2 us (3%)
    ppermute x64, waiting for transfers between devices, flip(): return lax.ppermute(values, axis, [(0, 1), (1, 0)])  136 us
    ppermute x64, starting transfers between devices, flip(): return lax.ppermute(values, axis, [(0, 1), (1, 0)])  48.2 us
    all_to_all x5, waiting for transfers between devices, team_swap(): return lax.all_to_all(blocks, axes.team, split_axis=0, concat_axis=0)  47.3 us
    pallas_call x2, Pallas kernels, mix_backward(): pl.pallas_call(functools.partial(mix_backward_kernel, as_rows=as_rows), g...  43.2 us
    unnamed x223, local copies, waits for them, and re-layouts  28.3 us
    dot_general x12, matrix products, mm_nt(): lax.dot_general(left, right, (((1,), (1,)), ((), ())), preferred_element_...  26 us
    dot_general x12, matrix products, mm(): return jnp.dot(left, right, preferred_element_type=F32)  23.2 us
    all_to_all x5, starting transfers between devices, team_swap(): return lax.all_to_all(blocks, axes.team, split_axis=0, concat_axis=0)  22.5 us
  transfers between devices with their start and end apart: 75, of which 32 were waited for; matrix products, arithmetic and copies ran while one was open for 23% of the time, Pallas kernels for 12%

profile of v4, /device:TPU:0, one launch (start us, length us, event | category | flops | bytes accessed | tf_op | source)
XLA Modules:
  0.0 525.9 jit_solution(6670686102140341603)
XLA Ops:
  11.9 6.5 %all-to-all-start = ((bf16[8,3,48,384]{3,2,1,0:T(8,128)(2,1)}), bf16[8,3,48,384]{3,2,1,0:T(8,128)(2,1)S(1)}, u32[]{:S(2)}, u32[]{:S(2)}) async-start(bf16[8,3,48,384]{3,2,1,0:T(8,128)(2,1)} %split_in.2), calls=%async_computation | async-start | bytes 1769472 | tf_op jit(solution)/shard_map/all_to_all | solution.py:879
  20.4 21.0 %all-to-all-done = bf16[8,3,48,384]{3,2,1,0:T(8,128)(2,1)S(1)} async-done(((bf16[8,3,48,384]{3,2,1,0:T(8,128)(2,1)}), bf16[8,3,48,384]{3,2,1,0:T(8,128)(2,1)S(1)}, u32[]{:S(2)}, u32[]{:S(2)}) %all-to-all-start) | async-done | bytes 884768 | tf_op jit(solution)/shard_map/all_to_all | solution.py:879
  46.8 17.8 %collective-permute-done.3 = bf16[128,1536]{1,0:T(8,128)(2,1)S(1)} collective-permute-done((bf16[128,1536]{1,0:T(8,128)(2,1)}, bf16[128,1536]{1,0:T(8,128)(2,1)S(1)}, u32[]{:S(2)}, u32[]{:S(2)}) %collective-permute-start.3) | collective-permute-done | bytes 393248 | tf_op jit(solution)/shard_map/ppermute | solution.py:469
  64.9 4.0 collective-permute-done.refs_1_
  78.3 8.5 %collective-permute-done.7 = bf16[128,1536]{1,0:T(8,128)(2,1)S(1)} collective-permute-done((bf16[128,1536]{1,0:T(8,128)(2,1)S(1)}, bf16[128,1536]{1,0:T(8,128)(2,1)S(1)}, u32[]{:S(2)}, u32[]{:S(2)}) %collective-permute-start.7) | collective-permute-done | bytes 393248 | tf_op jit(solution)/shard_map/ppermute | solution.py:469
  92.0 4.4 convolution_convert_fusion.12
  107.9 3.6 all-to-all-start.1
  115.3 7.2 %mix_forward.2 = (bf16[1024,384]{1,0:T(8,128)(2,1)S(1)}, bf16[1024,384]{1,0:T(8,128)(2,1)S(1)}, f32[4,128,384]{2,1,0:T(8,128)S(1)}) custom-call(s32[3]{0:T(128)S(1)} %pad_add_fusion.place_ref, bf16[1024,1152]{1,0:T(8,128)(2,1)S(1)} %pad_maximum_fusion.2.proj_ref.before_ref, f32[8,640]{1,0:T(8,128)S(1)} %get-tuple-element.352.conv_ref, ...), custom_call_target="tpu_custom_call" | custom-call | flops 7077888000 | bytes 6144000 | tf_op jit(solution)/shard_map/mix_forward/pallas_call | solution.py:179
  124.3 10.2 %all-to-all-done.1 = bf16[8,3,48,384]{3,2,1,0:T(8,128)(2,1)S(1)} async-done(((bf16[8,3,48,384]{3,2,1,0:T(8,128)(2,1)}), bf16[8,3,48,384]{3,2,1,0:T(8,128)(2,1)S(1)}, u32[]{:S(2)}, u32[]{:S(2)}) %all-to-all-start.1) | async-done | bytes 884768 | tf_op jit(solution)/shard_map/all_to_all | solution.py:879
  152.1 9.6 %collective-permute-done.15 = bf16[128,1664]{1,0:T(8,128)(2,1)S(1)} collective-permute-done((bf16[128,1664]{1,0:T(8,128)(2,1)}, bf16[128,1664]{1,0:T(8,128)(2,1)S(1)}, u32[]{:S(2)}, u32[]{:S(2)}) %collective-permute-start.15) | collective-permute-done | bytes 426016 | tf_op jit(solution)/shard_map/ppermute | solution.py:469
  166.3 17.0 %collective-permute-done.19 = bf16[128,1664]{1,0:T(8,128)(2,1)S(1)} collective-permute-done((bf16[128,1664]{1,0:T(8,128)(2,1)S(1)}, bf16[128,1664]{1,0:T(8,128)(2,1)S(1)}, u32[]{:S(2)}, u32[]{:S(2)}) %collective-permute-start.19) | collective-permute-done | bytes 426016 | tf_op jit(solution)/shard_map/ppermute | solution.py:469
  193.4 11.7 %collective-permute-done.23 = bf16[128,1536]{1,0:T(8,128)(2,1)} collective-permute-done((bf16[128,1536]{1,0:T(8,128)(2,1)}, bf16[128,1536]{1,0:T(8,128)(2,1)}, u32[]{:S(2)}, u32[]{:S(2)}) %collective-permute-start.23) | collective-permute-done | bytes 393248 | tf_op jit(solution)/shard_map/ppermute | solution.py:469
  210.5 3.7 join_in.3
  227.9 8.6 %mix_forward.3 = (bf16[1024,384]{1,0:T(8,128)(2,1)S(1)}, bf16[1024,384]{1,0:T(8,128)(2,1)S(1)}, f32[4,128,384]{2,1,0:T(8,128)S(1)}, f32[8,1024]{1,0:T(8,128)S(1)}) custom-call(s32[3]{0:T(128)S(1)} %pad_add_fusion.place_ref, bf16[1024,1152]{1,0:T(8,128)(2,1)S(1)} %pad_maximum_fusion.3.proj_ref.before_ref, f32[8,640]{1,0:T(8,128)S(1)} %get-tuple-element.351.conv_ref, ...), custom_call_target="tpu_custom_call" | custom-call | flops 7077888000 | bytes 6144000 | tf_op jit(solution)/shard_map/mix_forward/pallas_call | solution.py:179
  253.6 6.9 %collective-permute-done.36 = bf16[128,1536]{1,0:T(8,128)(2,1)S(1)} collective-permute-done((bf16[128,1536]{1,0:T(8,128)(2,1)}, bf16[128,1536]{1,0:T(8,128)(2,1)S(1)}, u32[]{:S(2)}, u32[]{:S(2)}) %collective-permute-start.36) | collective-permute-done | bytes 393248 | tf_op jit(solution)/shard_map/ppermute | solution.py:469
  263.4 22.3 %mix_backward.2 = (bf16[1024,1152]{1,0:T(8,128)(2,1)S(1)}, f32[8,640]{1,0:T(8,128)S(1)}, f32[8,128]{1,0:T(8,128)S(1)}, f32[8,384]{1,0:T(8,128)S(1)}, bf16[1024,384]{1,0:T(8,128)(2,1)S(1)}) custom-call(s32[3]{0:T(128)S(1)} %pad_add_fusion.place_ref, bf16[1024,1152]{1,0:T(8,128)(2,1)} %copy-done.4, bf16[1024,1152]{1,0:T(8,128)(2,1)} %copy-done.4, ...), custom_call_target="tpu_custom_call" | custom-call | flops 15728640000 | bytes 9216000 | tf_op jit(solution)/shard_map/mix_backward/pallas_call | solution.py:405
  295.1 3.5 convolution_convert_fusion.19
  304.4 9.1 %collective-permute-done.42 = bf16[128,1536]{1,0:T(8,128)(2,1)S(1)} collective-permute-done((bf16[128,1536]{1,0:T(8,128)(2,1)S(1)}, bf16[128,1536]{1,0:T(8,128)(2,1)S(1)}, u32[]{:S(2)}, u32[]{:S(2)}) %collective-permute-start.42) | collective-permute-done | bytes 393248 | tf_op jit(solution)/shard_map/ppermute | solution.py:469
  316.1 5.8 %convolution_convert_fusion.grad_ref = bf16[1536,1152]{1,0:T(8,128)(2,1)} fusion(bf16[1024,1152]{1,0:T(8,128)(2,1)S(1)} %copy-done.18, bf16[256,1536]{1,0:T(8,128)(2,1)S(1)} %copy-done.90, bf16[512,1536]{1,0:T(8,128)(2,1)S(1)} %bitcast.350, bf16[256,1536]{1,0:T(8,128)(2,1)S(1)} %copy-done.92), kind=kOutput, calls=%fused_computation | convolution fusion | flops 3635085312 | bytes 9043968 | tf_op jit(solution)/shard_map/dot_general | solution.py:36
  324.2 9.1 %collective-permute-done.46.far_ref = bf16[128,1536]{1,0:T(8,128)(2,1)S(1)} collective-permute-done((bf16[128,1536]{1,0:T(8,128)(2,1)S(1)}, bf16[128,1536]{1,0:T(8,128)(2,1)S(1)}, u32[]{:S(2)}, u32[]{:S(2)}) %collective-permute-start.46) | collective-permute-done | bytes 393248 | tf_op jit(solution)/shard_map/ppermute | solution.py:469
  343.9 3.6 fusion.20
  347.5 16.3 %collective-permute-done.48 = bf16[128,1664]{1,0:T(8,128)(2,1)} collective-permute-done((bf16[128,1664]{1,0:T(8,128)(2,1)}, bf16[128,1664]{1,0:T(8,128)(2,1)}, u32[]{:S(2)}, u32[]{:S(2)}) %collective-permute-start.48) | collective-permute-done | bytes 426016 | tf_op jit(solution)/shard_map/ppermute | solution.py:469
  382.2 4.6 all-to-all-start.2
  388.2 20.8 %mix_backward.3 = (bf16[1024,1152]{1,0:T(8,128)(2,1)}, f32[8,640]{1,0:T(8,128)S(1)}, f32[8,128]{1,0:T(8,128)S(1)}, f32[8,384]{1,0:T(8,128)S(1)}, bf16[1024,384]{...) custom-call(s32[3]{0:T(128)S(1)} %pad_add_fusion.place_ref, bf16[1024,1152]{1,0:T(8,128)(2,1)} %copy-done.3, ...), custom_call_target="tpu_custom_call" | custom-call | flops 15728640000 | bytes 9216000 | tf_op jit(solution)/shard_map/mix_backward/pallas_call | solution.py:405
  410.2 3.9 convolution_convert_fusion.8.grad_ref
  440.2 8.6 %collective-permute-done.59 = bf16[16,48,384]{2,1,0:T(8,128)(2,1)} collective-permute-done((bf16[16,48,384]{2,1,0:T(8,128)(2,1)S(1)}, bf16[16,48,384]{2,1,0:T(8,128)(2,1)}, u32[]{:S(2)}, u32[]{:S(2)}) %collective-permute-start.59) | collective-permute-done | bytes 589856 | tf_op jit(solution)/shard_map/ppermute | solution.py:473
  460.8 3.8 collective-permute-done.62
  465.6 6.5 %collective-permute-done.61 = bf16[128,1536]{1,0:T(8,128)(2,1)S(1)} collective-permute-done((bf16[128,1536]{1,0:T(8,128)(2,1)S(1)}, bf16[128,1536]{1,0:T(8,128)(2,1)S(1)}, u32[]{:S(2)}, u32[]{:S(2)}) %collective-permute-start.61) | collective-permute-done | bytes 393248 | tf_op jit(solution)/shard_map/ppermute | solution.py:469
  477.1 4.2 all-to-all-start.3
  486.5 5.3 %all-to-all-done.3.refs_0_ = bf16[8,1,48,384]{3,2,1,0:T(8,128)(2,1)S(1)} async-done(((bf16[8,1,48,384]{3,2,1,0:T(8,128)(2,1)}), bf16[8,1,48,384]{3,2,1,0:T(8,128)(2,1)S(1)}, u32[]{:S(2)}, u32[]{:S(2)}) %all-to-all-start.3) | async-done | bytes 294944 | tf_op jit(solution)/shard_map/all_to_all | solution.py:879
  494.1 3.7 all-to-all-start.4
  503.7 10.7 %all-to-all-done.4.refs_1_ = bf16[8,2,48,384]{3,2,1,0:T(8,128)(2,1)S(1)} async-done(((bf16[8,2,48,384]{3,2,1,0:T(8,128)(2,1)}), bf16[8,2,48,384]{3,2,1,0:T(8,128)(2,1)S(1)}, u32[]{:S(2)}, u32[]{:S(2)}) %all-to-all-start.4) | async-done | bytes 589856 | tf_op jit(solution)/shard_map/all_to_all | solution.py:879
  (566 shorter events, 227.3 us)
Async XLA Ops:
  11.9 29.6 %all-to-all-start = ((bf16[8,3,48,384]{3,2,1,0:T(8,128)(2,1)}), bf16[8,3,48,384]{3,2,1,0:T(8,128)(2,1)S(1)}, u32[]{:S(2)}, u32[]{:S(2)}) async-start(bf16[8,3,48,384]{3,2,1,0:T(8,128)(2,1)} %split_in.2), calls=%async_computation | async-start | bytes 1769472 | tf_op jit(solution)/shard_map/all_to_all | solution.py:879
  18.4 69.1 %all-gather.3.cloned.1.call-start = ((), (), s32[]{:S(2)}) async-start(), calls=%async_computation.7 | async-start | bytes 1474560 | tf_op jit(solution)/shard_map/all_gather | solution.py:893
  41.5 27.4 %collective-permute-start = (bf16[24,48,384]{2,1,0:T(8,128)(2,1)S(1)}, bf16[24,48,384]{2,1,0:T(8,128)(2,1)S(1)}, u32[]{:S(2)}, u32[]{:S(2)}) collective-permute-start(bf16[24,48,384]{2,1,0:T(8,128)(2,1)S(1)} %bitcast.317), channel_id=1, source_target_pairs={{0,1},{1,0},{2,3},{3,2},{4,5},{5,4},{6,7},{7,6},{8,9},{9,8},{10,11... | collective-permute-start | bytes 2654216 | tf_op jit(solution)/shard_map/ppermute | solution.py:469
  43.0 25.9 %collective-permute-start.1 = (bf16[24,48,384]{2,1,0:T(8,128)(2,1)S(1)}, bf16[24,48,384]{2,1,0:T(8,128)(2,1)S(1)}, u32[]{:S(2)}, u32[]{:S(2)}) collective-permute-start(bf16[24,48,384]{2,1,0:T(8,128)(2,1)S(1)} %bitcast.318), channel_id=1, source_target_pairs={{0,2},{2,0},{1,3},{3,1},{4,6},{6,4},{5,7},{7,5},{8,10},{10,8},{9,1... | collective-permute-start | bytes 2654216 | tf_op jit(solution)/shard_map/ppermute | solution.py:469
  44.8 19.8 %collective-permute-start.3 = (bf16[128,1536]{1,0:T(8,128)(2,1)}, bf16[128,1536]{1,0:T(8,128)(2,1)S(1)}, u32[]{:S(2)}, u32[]{:S(2)}) collective-permute-start(bf16[128,1536]{1,0:T(8,128)(2,1)} %fusion.42), channel_id=1, source_target_pairs={{0,16},{16,0},{1,17},{17,1},{2,18},{18,2},{3,19},{19,3},{4,20},{20... | collective-permute-start | bytes 1179656 | tf_op jit(solution)/shard_map/ppermute | solution.py:469
  44.9 20.1 %collective-permute-start.4 = (bf16[128,1536]{1,0:T(8,128)(2,1)}, bf16[128,1536]{1,0:T(8,128)(2,1)S(1)}, u32[]{:S(2)}, u32[]{:S(2)}) collective-permute-start(bf16[128,1536]{1,0:T(8,128)(2,1)} %fusion.42), channel_id=1, source_target_pairs={{0,8},{8,0},{1,9},{9,1},{2,10},{10,2},{3,11},{11,3},{4,12},{12,4},... | collective-permute-start | bytes 1179656 | tf_op jit(solution)/shard_map/ppermute | solution.py:469
  69.2 33.8 %collective-permute-start.10 = (bf16[128,1536]{1,0:T(8,128)(2,1)S(1)}, bf16[128,1536]{1,0:T(8,128)(2,1)}, u32[]{:S(2)}, u32[]{:S(2)}) collective-permute-start(bf16[128,1536]{1,0:T(8,128)(2,1)S(1)} %bitcast.320), channel_id=1, source_target_pairs={{0,4},{4,0},{1,5},{5,1},{2,6},{6,2},{3,7},{7,3},{8,12},{12,8},{9,1... | collective-permute-start | bytes 1179656 | tf_op jit(solution)/shard_map/ppermute | solution.py:469
  69.2 33.8 %collective-permute-start.11 = (bf16[128,1536]{1,0:T(8,128)(2,1)S(1)}, bf16[128,1536]{1,0:T(8,128)(2,1)}, u32[]{:S(2)}, u32[]{:S(2)}) collective-permute-start(bf16[128,1536]{1,0:T(8,128)(2,1)S(1)} %bitcast.321), channel_id=1, source_target_pairs={{0,16},{16,0},{1,17},{17,1},{2,18},{18,2},{3,19},{19,3},{4,20},{20... | collective-permute-start | bytes 1179656 | tf_op jit(solution)/shard_map/ppermute | solution.py:469
  103.0 21.3 %collective-permute-start.13 = (bf16[128,1536]{1,0:T(8,128)(2,1)}, bf16[128,1536]{1,0:T(8,128)(2,1)}, u32[]{:S(2)}, u32[]{:S(2)}) collective-permute-start(bf16[128,1536]{1,0:T(8,128)(2,1)} %collective-permute-done.11), channel_id=1, source_target_pairs={{0,8},{8,0},{1,9},{9,1},{2,10},{10,2},{3,11},{11,3},{4,12},{12,4},... | collective-permute-start | bytes 1179656 | tf_op jit(solution)/shard_map/ppermute | solution.py:469
  106.7 31.0 %collective-permute-start.26 = (bf16[2,128,1536]{2,1,0:T(8,128)(2,1)}, bf16[2,128,1536]{2,1,0:T(8,128)(2,1)}, u32[]{:S(2)}, u32[]{:S(2)}) collective-permute-start(bf16[2,128,1536]{2,1,0:T(8,128)(2,1)} %get-tuple-element.339), channel_id=1, source_target_pairs={{0,4},{4,0},{1,5},{5,1},{2,6},{6,2},{3,7},{7,3},{8,12},{12,8},{9,1... | collective-permute-start | bytes 2359304 | tf_op jit(solution)/shard_map/ppermute | solution.py:469
  107.9 26.6 %all-to-all-start.1 = ((bf16[8,3,48,384]{3,2,1,0:T(8,128)(2,1)}), bf16[8,3,48,384]{3,2,1,0:T(8,128)(2,1)S(1)}, u32[]{:S(2)}, u32[]{:S(2)}) async-start(bf16[8,3,48,384]{3,2,1,0:T(8,128)(2,1)} %split_in.3), calls=%async_computation.1 | async-start | bytes 1769472 | tf_op jit(solution)/shard_map/all_to_all | solution.py:879
  111.5 76.6 %all-gather.5.cloned.1.call-start = ((), (), s32[]{:S(2)}) async-start(), calls=%async_computation.8 | async-start | bytes 1474560 | tf_op jit(solution)/shard_map/all_gather | solution.py:893
  140.6 25.3 %collective-permute-start.20 = (bf16[24,48,384]{2,1,0:T(8,128)(2,1)S(1)}, bf16[24,48,384]{2,1,0:T(8,128)(2,1)}, u32[]{:S(2)}, u32[]{:S(2)}) collective-permute-start(bf16[24,48,384]{2,1,0:T(8,128)(2,1)S(1)} %bitcast.314), channel_id=1, source_target_pairs={{0,1},{1,0},{2,3},{3,2},{4,5},{5,4},{6,7},{7,6},{8,9},{9,8},{10,11... | collective-permute-start | bytes 2654216 | tf_op jit(solution)/shard_map/ppermute | solution.py:469
  141.4 24.9 %collective-permute-start.21 = (bf16[24,48,384]{2,1,0:T(8,128)(2,1)S(1)}, bf16[24,48,384]{2,1,0:T(8,128)(2,1)S(1)}, u32[]{:S(2)}, u32[]{:S(2)}) collective-permute-start(bf16[24,48,384]{2,1,0:T(8,128)(2,1)S(1)} %bitcast.315), channel_id=1, source_target_pairs={{0,2},{2,0},{1,3},{3,1},{4,6},{6,4},{5,7},{7,5},{8,10},{10,8},{9,1... | collective-permute-start | bytes 2654216 | tf_op jit(solution)/shard_map/ppermute | solution.py:469
  148.8 233.4 %reduce-scatter.7.cloned.1.call-start = ((), (), s32[]{:S(2)}) async-start(), calls=%async_computation.10 | async-start | bytes 4423680
  161.8 21.5 %collective-permute-start.19 = (bf16[128,1664]{1,0:T(8,128)(2,1)S(1)}, bf16[128,1664]{1,0:T(8,128)(2,1)S(1)}, u32[]{:S(2)}, u32[]{:S(2)}) collective-permute-start(bf16[128,1664]{1,0:T(8,128)(2,1)S(1)} %fusion.38), channel_id=1, source_target_pairs={{0,16},{16,0},{1,17},{17,1},{2,18},{18,2},{3,19},{19,3},{4,20},{20... | collective-permute-start | bytes 1277960 | tf_op jit(solution)/shard_map/ppermute | solution.py:469
  162.1 21.2 %collective-permute-start.18 = (bf16[128,1664]{1,0:T(8,128)(2,1)S(1)}, bf16[128,1664]{1,0:T(8,128)(2,1)S(1)}, u32[]{:S(2)}, u32[]{:S(2)}) collective-permute-start(bf16[128,1664]{1,0:T(8,128)(2,1)S(1)} %slice_bitcast_fusion.6), channel_id=1, source_target_pairs={{0,8},{8,0},{1,9},{9,1},{2,10},{10,2},{3,11},{11,3},{4,12},{12,4},... | collective-permute-start | bytes 1277960 | tf_op jit(solution)/shard_map/ppermute | solution.py:469
  184.8 20.3 %collective-permute-start.23 = (bf16[128,1536]{1,0:T(8,128)(2,1)}, bf16[128,1536]{1,0:T(8,128)(2,1)}, u32[]{:S(2)}, u32[]{:S(2)}) collective-permute-start(bf16[128,1536]{1,0:T(8,128)(2,1)} %multiply_convert_fusion), channel_id=1, source_target_pairs={{0,16},{16,0},{1,17},{17,1},{2,18},{18,2},{3,19},{19,3},{4,20},{20... | collective-permute-start | bytes 1179656 | tf_op jit(solution)/shard_map/ppermute | solution.py:469
  185.4 20.0 %collective-permute-start.24 = (bf16[128,1536]{1,0:T(8,128)(2,1)}, bf16[128,1536]{1,0:T(8,128)(2,1)}, u32[]{:S(2)}, u32[]{:S(2)}) collective-permute-start(bf16[128,1536]{1,0:T(8,128)(2,1)} %multiply_convert_fusion), channel_id=1, source_target_pairs={{0,8},{8,0},{1,9},{9,1},{2,10},{10,2},{3,11},{11,3},{4,12},{12,4},... | collective-permute-start | bytes 1179656 | tf_op jit(solution)/shard_map/ppermute | solution.py:469
  187.0 21.8 %collective-permute-start.25 = (bf16[24,48,384]{2,1,0:T(8,128)(2,1)}, bf16[24,48,384]{2,1,0:T(8,128)(2,1)}, u32[]{:S(2)}, u32[]{:S(2)}) collective-permute-start(bf16[24,48,384]{2,1,0:T(8,128)(2,1)} %collective-permute-done.20.refs_1_), channel_id=1, source_target_pairs={{0,2},{2,0},{1,3},{3,1},{4,6},{6,4},{5,7},{7,5},{8,10},{10,8},{9,1... | collective-permute-start | bytes 2654216 | tf_op jit(solution)/shard_map/ppermute | solution.py:469
  260.7 26.4 %collective-permute-start.40 = (bf16[128,1536]{1,0:T(8,128)(2,1)S(1)}, bf16[128,1536]{1,0:T(8,128)(2,1)S(1)}, u32[]{:S(2)}, u32[]{:S(2)}) collective-permute-start(bf16[128,1536]{1,0:T(8,128)(2,1)S(1)} %fusion.54), channel_id=1, source_target_pairs={{0,16},{16,0},{1,17},{17,1},{2,18},{18,2},{3,19},{19,3},{4,20},{20... | collective-permute-start | bytes 1179656 | tf_op jit(solution)/shard_map/ppermute | solution.py:469
  262.2 25.7 %collective-permute-start.39 = (bf16[128,1536]{1,0:T(8,128)(2,1)S(1)}, bf16[128,1536]{1,0:T(8,128)(2,1)S(1)}, u32[]{:S(2)}, u32[]{:S(2)}) collective-permute-start(bf16[128,1536]{1,0:T(8,128)(2,1)S(1)} %slice_bitcast_fusion.21), channel_id=1, source_target_pairs={{0,8},{8,0},{1,9},{9,1},{2,10},{10,2},{3,11},{11,3},{4,12},{12,4},... | collective-permute-start | bytes 1179656 | tf_op jit(solution)/shard_map/ppermute | solution.py:469
  313.6 19.7 %collective-permute-start.46 = (bf16[128,1536]{1,0:T(8,128)(2,1)S(1)}, bf16[128,1536]{1,0:T(8,128)(2,1)S(1)}, u32[]{:S(2)}, u32[]{:S(2)}) collective-permute-start(bf16[128,1536]{1,0:T(8,128)(2,1)S(1)} %fusion.51), channel_id=1, source_target_pairs={{0,16},{16,0},{1,17},{17,1},{2,18},{18,2},{3,19},{19,3},{4,20},{20... | collective-permute-start | bytes 1179656 | tf_op jit(solution)/shard_map/ppermute | solution.py:469
  336.2 161.6 %reduce-scatter.5.cloned.1.call-start = ((), (), s32[]{:S(2)}) async-start(), calls=%async_computation.9 | async-start | bytes 1474560 | tf_op jit(solution)/shard_map/reduce_scatter | solution.py:1057
  341.5 22.2 %collective-permute-start.48 = (bf16[128,1664]{1,0:T(8,128)(2,1)}, bf16[128,1664]{1,0:T(8,128)(2,1)}, u32[]{:S(2)}, u32[]{:S(2)}) collective-permute-start(bf16[128,1664]{1,0:T(8,128)(2,1)} %get-tuple-element.265), channel_id=1, source_target_pairs={{0,16},{16,0},{1,17},{17,1},{2,18},{18,2},{3,19},{19,3},{4,20},{20... | collective-permute-start | bytes 1277960 | tf_op jit(solution)/shard_map/ppermute | solution.py:469
  342.4 21.4 %collective-permute-start.49 = (bf16[128,1664]{1,0:T(8,128)(2,1)}, bf16[128,1664]{1,0:T(8,128)(2,1)S(1)}, u32[]{:S(2)}, u32[]{:S(2)}) collective-permute-start(bf16[128,1664]{1,0:T(8,128)(2,1)} %get-tuple-element.265), channel_id=1, source_target_pairs={{0,8},{8,0},{1,9},{9,1},{2,10},{10,2},{3,11},{11,3},{4,12},{12,4},... | collective-permute-start | bytes 1277960 | tf_op jit(solution)/shard_map/ppermute | solution.py:469
  382.2 28.0 %all-to-all-start.2 = ((bf16[8,3,48,384]{3,2,1,0:T(8,128)(2,1)}), bf16[8,3,48,384]{3,2,1,0:T(8,128)(2,1)}, u32[]{:S(2)}, u32[]{:S(2)}) async-start(bf16[8,3,48,384]{3,2,1,0:T(8,128)(2,1)} %bitcast.356), calls=%async_computation.2 | async-start | bytes 1769472 | tf_op jit(solution)/shard_map/all_to_all | solution.py:879
  419.2 20.9 %collective-permute-start.57 = (bf16[16,48,384]{2,1,0:T(8,128)(2,1)}, bf16[16,48,384]{2,1,0:T(8,128)(2,1)}, u32[]{:S(2)}, u32[]{:S(2)}) collective-permute-start(bf16[16,48,384]{2,1,0:T(8,128)(2,1)} %get-tuple-element.296), channel_id=1, source_target_pairs={{0,1},{1,0},{2,3},{3,2},{4,5},{5,4},{6,7},{7,6},{8,9},{9,8},{10,11... | collective-permute-start | bytes 1769480 | tf_op jit(solution)/shard_map/ppermute | solution.py:469
  420.6 19.6 %collective-permute-start.58 = (bf16[16,48,384]{2,1,0:T(8,128)(2,1)S(1)}, bf16[16,48,384]{2,1,0:T(8,128)(2,1)}, u32[]{:S(2)}, u32[]{:S(2)}) collective-permute-start(bf16[16,48,384]{2,1,0:T(8,128)(2,1)S(1)} %get-tuple-element.297), channel_id=1, source_target_pairs={{0,2},{2,0},{1,3},{3,1},{4,6},{6,4},{5,7},{7,5},{8,10},{10,8},{9,1... | collective-permute-start | bytes 1769480 | tf_op jit(solution)/shard_map/ppermute | solution.py:469
  421.3 27.6 %collective-permute-start.59 = (bf16[16,48,384]{2,1,0:T(8,128)(2,1)S(1)}, bf16[16,48,384]{2,1,0:T(8,128)(2,1)}, u32[]{:S(2)}, u32[]{:S(2)}) collective-permute-start(bf16[16,48,384]{2,1,0:T(8,128)(2,1)S(1)} %get-tuple-element.298), channel_id=1, source_target_pairs={{0,3},{1,2},{2,1},{3,0},{4,7},{5,6},{6,5},{7,4},{8,11},{9,10},{10,... | collective-permute-start | bytes 1769480 | tf_op jit(solution)/shard_map/ppermute | solution.py:473
  452.0 20.2 %collective-permute-start.61 = (bf16[128,1536]{1,0:T(8,128)(2,1)S(1)}, bf16[128,1536]{1,0:T(8,128)(2,1)S(1)}, u32[]{:S(2)}, u32[]{:S(2)}) collective-permute-start(bf16[128,1536]{1,0:T(8,128)(2,1)S(1)} %fusion.48), channel_id=1, source_target_pairs={{0,16},{16,0},{1,17},{17,1},{2,18},{18,2},{3,19},{19,3},{4,20},{20... | collective-permute-start | bytes 1179656 | tf_op jit(solution)/shard_map/ppermute | solution.py:469
  494.1 20.4 %all-to-all-start.4 = ((bf16[8,2,48,384]{3,2,1,0:T(8,128)(2,1)}), bf16[8,2,48,384]{3,2,1,0:T(8,128)(2,1)S(1)}, u32[]{:S(2)}, u32[]{:S(2)}) async-start(bf16[8,2,48,384]{3,2,1,0:T(8,128)(2,1)} %bitcast.346), calls=%async_computation.4 | async-start | bytes 1179648 | tf_op jit(solution)/shard_map/all_to_all | solution.py:879
  (151 other events, 1152.6 us)
Sparse Core Ops, SparseCore 0:
  21.1 35.1 all-gather.2
  149.0 29.1 all-gather.4
  336.4 45.8 reduce-scatter.6
  385.6 28.5 reduce-scatter.4

commit v5 on v4

--- a/solution.py
+++ b/solution.py
@@ -57,23 +57,47 @@
     return jnp.where(lane < 32, total, 0.0)
 
 
+def sum_rows(values, ones):
+    high = values.astype(BF16).astype(F32)
+    left = values - high
+    middle = left.astype(BF16).astype(F32)
+    parts = jnp.concatenate([high, middle, left - middle], axis=0)
+    total = mm_low(parts, ones)
+    return total[0:8] + total[8:16] + total[16:24]
+
+
+def as_columns(*rows):
+    stacked = jnp.concatenate(rows, axis=0)
+    rest = jnp.zeros((LANES - stacked.shape[0], stacked.shape[1]), F32)
+    return jnp.transpose(jnp.concatenate([stacked, rest], axis=0))
+
+
+def logistic(values):
+    return 0.5 * jnp.tanh(0.5 * values) + 0.5
+
+
 def iota(shape, dim):
     return lax.broadcasted_iota(jnp.int32, shape, dim)
 
 
-def head_spread(width):
-    return (iota((LANES, width), 0) == iota((LANES, width), 1) // HD).astype(F32)
-
-
-def head_fold(width):
-    return (iota((width, LANES), 0) // HD == iota((width, LANES), 1)).astype(F32)
+def head_spread(width, first):
+    return (iota((LANES, width), 0) == iota((LANES, width), 1) // HD + first).astype(BF16)
+
+
+def head_fold(heads, width):
+    return iota((heads, width), 0) == iota((heads, width), 1) // HD
 
 
 def own_steps(raw, turned):
     return pltpu.roll(raw.astype(F32), turned, 1)
 
 
-def steps_of(raw, head_rows):
+def steps_of(raw, head_ref):
+    shifted = jnp.transpose(raw)[0:8] + head_ref[:, 0:1]
+    return shifted, jnp.maximum(shifted, 0.0) + jnp.log1p(jnp.exp(-jnp.abs(shifted)))
+
+
+def steps_beside(raw, head_rows):
     shifted = raw + head_rows[0:1]
     step = jnp.maximum(shifted, 0.0) + jnp.log1p(jnp.exp(-jnp.abs(shifted)))
     return shifted, step
@@ -122,17 +146,17 @@
     b_low = act[:, wide : wide + NSTATE].astype(BF16)
     c_low = act[:, wide + NSTATE :].astype(BF16)
 
-    _, step = steps_of(own_steps(proj[:, wide + chans :], turned), head_ref)
+    _, step = steps_beside(own_steps(proj[:, wide + chans :], turned), head_ref)
     decay = -step * head_ref[1:2, :]
     lower = iota((rows, rows), 0) >= iota((rows, rows), 1)
     cum = mm_thirds(lower.astype(F32), decay)
     cum_t = jnp.transpose(cum)
-    spread = head_spread(wide)
+    spread = head_spread(wide, 0)
     total = cum[rows - 1 : rows, :]
     step_wide = mm_low(step, spread)
     grown = mm_low(jnp.exp(cum), spread)
     ending_wide = mm_low(step * jnp.exp(total - cum), spread)
-    kept = mm_exact(jnp.broadcast_to(jnp.exp(total), (8, LANES)), spread)[0:1, :]
+    kept = mm_exact(jnp.broadcast_to(jnp.exp(total), (8, LANES)), spread.astype(F32))[0:1, :]
 
     scores = mm_nt(c_low, b_low)
     weighted = x * step_wide
@@ -157,8 +181,10 @@
     y = within + carried + skip_ref[0:1, :] * x
     gate = proj[:, :wide].astype(F32)
     gated = (y * (gate * jax.nn.sigmoid(gate))).astype(BF16)
-    put(gated_ref, core, gated, 0, wide)
-    if with_sums:
+    if not with_sums:
+        put(gated_ref, core, gated, 0, wide)
+    else:
+        gated_ref[...] = gated
         gated = gated.astype(F32)
         ones = jnp.ones((8, wide), BF16)
         product = gated * take(refs[0], core).astype(F32)
@@ -176,6 +202,7 @@
     count = length // STRETCH
     whole = lambda shape: pl.BlockSpec(shape, lambda i, at: (0,) * len(shape))
     part = lambda cols: pl.BlockSpec((STRETCH, cols), lambda i, at: (i ^ (at[0] >> 1), 0))
+    plain = pl.BlockSpec((STRETCH, wide), lambda i, at: (i, 0))
     return pl.pallas_call(
         functools.partial(mix_forward_kernel, with_sums=with_sums),
         grid_spec=pltpu.PrefetchScalarGridSpec(
@@ -189,7 +216,7 @@
             ]
             + [part(wide)] * with_sums,
             out_specs=[
-                part(wide),
+                plain if with_sums else part(wide),
                 part(wide),
                 pl.BlockSpec((1, NSTATE, wide), lambda i, at: (i, 0, 0)),
             ]
@@ -253,7 +280,7 @@
     pre = conv_ref[CONV : CONV + 1, :] + conv_ref[0:1, :] * ext_ref[5 : 5 + rows, :]
     for lag in range(1, CONV):
         pre = pre + conv_ref[lag : lag + 1, :] * ext_ref[5 + lag : 5 + lag + rows, :]
-    sig = jax.nn.sigmoid(pre)
+    sig = logistic(pre)
     act = pre * sig
     slope = sig * (1.0 + pre * (1.0 - sig))
     x = act[:, :wide]
@@ -262,23 +289,24 @@
     c_low = act[:, wide + NSTATE :].astype(BF16)
 
     shifted, step = steps_of(own_steps(proj[:, wide + chans :], turned), head_ref)
-    rate = head_ref[1:2, :]
+    rate = head_ref[:, 1:2]
     decay = -step * rate
     lower = iota((rows, rows), 0) >= iota((rows, rows), 1)
     upper = iota((rows, rows), 0) <= iota((rows, rows), 1)
-    cum = mm_thirds(lower.astype(F32), decay)
-    cum_t = jnp.transpose(cum)
-    spread = head_spread(wide)
-    fold = head_fold(wide)
-    total = cum[rows - 1 : rows, :]
-    step_wide = mm_low(step, spread)
-    grown = mm_low(jnp.exp(cum), spread)
-    to_end = mm_low(jnp.exp(total - cum), spread)
-    kept = mm_exact(jnp.broadcast_to(jnp.exp(total), (8, LANES)), spread)[0:1, :]
+    cum_t = sum_rows(decay, upper)
+    total = cum_t[:, rows - 1 : rows]
+    cum = as_columns(cum_t, step, jnp.exp(cum_t), jnp.exp(total - cum_t))
+    cum_low = cum.astype(BF16)
+    step_wide = mm(cum_low, head_spread(wide, 8))
+    grown = mm(cum_low, head_spread(wide, 16))
+    to_end = mm(cum_low, head_spread(wide, 24))
+    fold = head_fold(8, wide)
+    fold_low = head_fold(16, wide).astype(BF16)
+    kept = jnp.sum(jnp.where(fold, jnp.exp(total), 0.0), axis=0, keepdims=True)
 
     gate = proj[:, :wide].astype(F32)
     y = take(y_ref, core).astype(F32)
-    gate_sig = jax.nn.sigmoid(gate)
+    gate_sig = logistic(gate)
     gate_act = gate * gate_sig
     gated = y * gate_act
     if as_rows:
@@ -316,7 +344,7 @@
             fade = jnp.where(upper, jnp.exp(gap), 0.0)
             own = jnp.where(side == head - start // HD, both_x, jnp.zeros_like(both_x))
             faded = fade * mm_nt(own, both_dy)
-            stepped = faded * step[:, head : head + 1]
+            stepped = faded * cum[:, 8 + head : 9 + head]
             d_scores = d_scores + stepped
             parts.append(mm((scores_t * fade).astype(BF16), both_dy))
             column = jnp.where(
@@ -337,23 +365,20 @@
     g_x = step_wide * (inner + outer) + wide_ref[0:1, :] * dy
     dy_grown = dy * grown
     dy_grown_low = dy_grown.astype(BF16)
-    carried_sum = mm_low(dy_grown * mm(c_low, enter_low), fold)
-    outer_sum = mm_low(x * outer, fold)
-    state_sum = mm_exact(
-        jnp.broadcast_to(jnp.sum(enter * dstate, axis=0, keepdims=True), (8, wide)), fold
-    )[0:1, :]
+    carried_sum = mm_nt(fold_low, (dy_grown * mm(c_low, enter_low)).astype(BF16))[0:8]
+    outer_sum = mm_nt(fold_low, (x * outer).astype(BF16))[0:8]
+    state_sum = jnp.sum(enter * dstate, axis=0, keepdims=True)
+    state_sum = jnp.sum(jnp.where(fold, state_sum, 0.0), axis=1, keepdims=True)
+    column = jnp.transpose(column)[0:8]
     step_outer = step * outer_sum
-    g_cum = jnp.transpose(rows_ref[...]) + carried_sum - step * column - step_outer
-    g_total = (
-        jnp.sum(step_outer, axis=0, keepdims=True)
-        + jnp.exp(total) * state_sum
-    )
-    g_decay = mm_thirds(upper.astype(F32), g_cum) + g_total
+    g_cum = rows_ref[0:8, :] + carried_sum - step * column - step_outer
+    g_total = jnp.sum(step_outer, axis=1, keepdims=True) + jnp.exp(total) * state_sum
+    g_decay = sum_rows(g_cum, lower) + g_total
     scaled_decay = rate * g_decay
     g_raw = (column + outer_sum - scaled_decay) * jax.nn.sigmoid(shifted)
-    head_grad_ref[0:1, :] += jnp.sum(g_raw, axis=0, keepdims=True)
-    head_grad_ref[1:2, :] -= jnp.sum(step * scaled_decay, axis=0, keepdims=True)
-    g_raw = pltpu.roll(g_raw, lax.rem(LANES - turned, LANES), 1)
+    head_grad_ref[:, 0:1] += jnp.sum(g_raw, axis=1, keepdims=True)
+    head_grad_ref[:, 1:2] -= jnp.sum(step * scaled_decay, axis=1, keepdims=True)
+    g_raw = pltpu.roll(as_columns(g_raw), lax.rem(LANES - turned, LANES), 1)
     put(out_ref, core, g_raw.astype(BF16), wide + chans, wide + chans + LANES)
     for copy_ref in copies[1:]:
         put(copy_ref, core, g_raw.astype(BF16), chans, chans + LANES)
@@ -368,16 +393,15 @@
     gext_ref[0:rows, wide : wide + NSTATE] = g_b * slope[:, wide : wide + NSTATE]
     gext_ref[0:rows, wide + NSTATE :] = g_c * slope[:, wide + NSTATE :]
     g_pre = gext_ref[0:rows, :]
-    g_in = conv_ref[CONV - 1 : CONV, :] * g_pre
-    for lag in range(CONV - 1):
-        g_in = g_in + conv_ref[lag : lag + 1, :] * gext_ref[3 - lag : 3 - lag + rows, :]
+    current = ext_ref[8 : 8 + rows, :]
+    g_in = jnp.zeros_like(g_pre)
+    for lag in range(CONV):
+        moved = gext_ref[3 - lag : 3 - lag + rows, :]
+        g_in = g_in + conv_ref[lag : lag + 1, :] * moved
+        conv_grad_ref[lag : lag + 1, :] += jnp.sum(current * moved, axis=0, keepdims=True)
     put(out_ref, core, g_in.astype(BF16), wide, wide + chans)
     for copy_ref in copies[1:]:
         put(copy_ref, core, g_in.astype(BF16), 0, chans)
-    for lag in range(CONV):
-        conv_grad_ref[lag : lag + 1, :] += jnp.sum(
-            ext_ref[5 + lag : 5 + lag + rows, :] * g_pre, axis=0, keepdims=True
-        )
     conv_grad_ref[CONV : CONV + 1, :] += jnp.sum(g_pre, axis=0, keepdims=True)
     gext_ref[rows : rows + 8, :] = gext_ref[0:8, :]
 
@@ -429,7 +453,7 @@
                 pltpu.VMEM((NSTATE, wide), F32),
                 pltpu.VMEM((STRETCH + 8, wide + BC), F32),
                 pltpu.VMEM((STRETCH + 8, wide + BC), F32),
-                pltpu.VMEM((LANES, STRETCH), F32),
+                pltpu.VMEM((8, STRETCH), F32),
             ],
         ),
         out_shape=[
@@ -791,10 +815,8 @@
     if len(axes.links) != 2:
         return parts, []
     rows, other, from_far, from_near = parts
-    sides = jnp.stack([from_near, from_far])
-    sides = jnp.stack([sides, flip(sides, "c")], axis=1).reshape(-1, rows.shape[1])
-    corner = (flip(from_far, axes.links[1]),)
-    return corner, [jnp.concatenate([rows, other], axis=0), sides]
+    most = [rows, other, from_near, flip(from_near, "c"), from_far, flip(from_far, "c")]
+    return (flip(from_far, axes.links[1]),), [jnp.concatenate(most, axis=0)]
 
 
 def gather_end(axes, corner):
@@ -930,10 +952,11 @@
     head = jnp.stack([dt_bias, a_log, skip_gain], axis=1)
     skip = jnp.pad(jnp.repeat(head[:, 2:], HD, axis=2), ((0, 0), (0, 7), (0, 0)))
     head = jnp.stack([head[:, 0], jnp.exp(head[:, 1])], axis=1)
-    head = jnp.pad(head, ((0, 0), (0, 6), (0, LANES - heads)))
+    head_rows = jnp.pad(head, ((0, 0), (0, 6), (0, LANES - heads)))
+    head = jnp.pad(head.transpose(0, 2, 1), ((0, 0), (0, 8 - heads), (0, LANES - 2)))
 
     blocks = in_blocks(1, last)
-    gated_0, y_0, enter_0 = mix_forward(place, proj_0, conv[0], head[0], skip[0])
+    gated_0, y_0, enter_0 = mix_forward(place, proj_0, conv[0], head_rows[0], skip[0])
     cot_hops, cot = gather_corner(axes, cot)
     (gated_0, y_0, enter_0), blocks, cot_hops = together((gated_0, y_0, enter_0), blocks, cot_hops)
     cot = cot + [gather_end(axes, cot_hops)]
@@ -971,7 +994,7 @@
     pieces_1 = pieces_1 + [last]
     proj_1 = jnp.concatenate(proj_1 + [mm(last, weight_in_1).astype(BF16)], axis=0)
     gated_1, y_1, enter_1, sums = mix_forward(
-        place, proj_1, conv[1], head[1], skip[1], g_scaled
+        place, proj_1, conv[1], head_rows[1], skip[1], g_scaled
     )
 
     sums = sums + flip(sums, "c")
@@ -982,15 +1005,13 @@
         for name in axes.links:
             sums = sums + flip(sums, name)
 
-    def last_rows(begin, end, others):
-        return mm(after(gated_1, others)[begin:end], weight_out_1).astype(BF16)
-
-    sums, branch_1 = together(sums, scatter_corner(axes, last_rows, rows))
-    branch_1 = scatter_sides(axes, branch_1)
+    branch_1 = mm(gated_1, weight_out_1).astype(BF16)
+    sums, branch_1 = together(sums, branch_1)
+    branch_1 = lax.psum_scatter(branch_1, axes.team, scatter_dimension=0, tiled=True)
     outs = mix_backward(
         place, proj_1, y_1, g_scaled, sums, enter_1, conv[1], head[1], skip[1], True
     )
-    (g_proj, g_conv, g_head, g_skip, scaled_1), branch_1 = together(outs, branch_1)
+    g_proj, g_conv, g_head, g_skip, scaled_1 = outs
     got_1 = jnp.concatenate(after(cot, g_proj), axis=0)
     normed = jnp.concatenate(after(pieces_1, g_proj), axis=0)
 
@@ -1010,7 +1031,7 @@
             for at, end in cuts
         ]
         g_head = jnp.stack(
-            [g_head[0, :heads], g_head[1, :heads], jnp.sum(g_skip[0].reshape(heads, HD), 1)]
+            [g_head[:heads, 0], g_head[:heads, 1], jnp.sum(g_skip[0].reshape(heads, HD), 1)]
         )
         g_head = jnp.pad(g_head, ((0, 0), (0, room - heads)))
         sharers = team * copies // team
@@ -1037,14 +1058,15 @@
 
         return make
 
-    weighed = together(*scatter_corner(axes, weighed_rows(g_proj, weight_in_1), rows))
+    weighed = scatter_corner(axes, weighed_rows(g_proj, weight_in_1), rows)
+    weighed, branch_1 = together(weighed, branch_1)
     weighed = scatter_sides(axes, weighed)
     g_late = after(g_proj, weighed[0])
     blocks = in_gradient(normed, g_late, (g_conv, g_head, g_skip), False)
     weighed, blocks = together(weighed, blocks)
     summed = copies_scatter(blocks)
     squares = lax.dynamic_slice_in_dim(sums, me * rows, rows, 1)[0][:, None]
-    out = (residual_1 + lax.rsqrt(squares / DI + eps) * add_all(branch_1)).astype(BF16)
+    out = (residual_1 + lax.rsqrt(squares / DI + eps) * branch_1.astype(F32)).astype(BF16)
     if len(weighed) == 1:
         weighed = weighed + (jnp.zeros_like(weighed[0]),) * 2
 

time: 533 us -> 524 us (0.983)
  waiting for transfers between devices: 194 us -> 172 us
  local copies, waits for them, and re-layouts: 46.4 us -> 65.8 us
    unnamed x223 -> x229, local copies, waits for them, and re-layouts: 28.3 us -> 43.9 us
    another operation x14 -> x6, other arithmetic: 9.61 us -> 0.26 us  [the longest x8 9.36 us: gather_corner(): jnp.stack([sides, flip(sides, 'c')], axis=1).reshape(-1, rows.shape[1])]
    ppermute x2, waiting for transfers between devices: 8.63 us -> 0.01 us  [flip_both(): return lax.ppermute(values, names, [(0, 3), (1, 2), (2, 1), (3, 0)])]
    all_to_all x5, waiting for transfers between devices: 47.3 us -> 40 us  [team_swap(): return lax.all_to_all(blocks, axes.team, split_axis=0, concat_axis=0)]
    ppermute x64 -> x62, starting transfers between devices: 48.2 us -> 44.2 us  [flip(): return lax.ppermute(values, axis, [(0, 1), (1, 0)])]
    ppermute x64 -> x62, waiting for transfers between devices: 136 us -> 132 us  [flip(): return lax.ppermute(values, axis, [(0, 1), (1, 0)])]
    dot_general x12 -> x10, matrix products: 26 us -> 22.7 us  [mm_nt(): lax.dot_general(left, right, (((1,), (1,)), ((), ())), preferred_element_...]
    dot_general x12 -> x8, matrix products: 23.2 us -> 24.6 us  [mm(): return jnp.dot(left, right, preferred_element_type=F32)]
  transfers between devices with their start and end apart: 75 -> 74, of which waited for: 32 -> 30; matrix products, arithmetic and copies ran while one was open for 23% -> 28% of each run, Pallas kernels for 12% -> 12%
where the time goes in v5:
time: 524 us; the launch traced here: 516 us
  waiting for transfers between devices  172 us (33%)
  starting transfers between devices  75.1 us (14%)
  Pallas kernels  72.8 us (14%)
  matrix products  68.7 us (13%)
  local copies, waits for them, and re-layouts  65.8 us (13%)
  other arithmetic  45.8 us (9%)
  between operations  15.9 us (3%)
    ppermute x62, waiting for transfers between devices, flip(): return lax.ppermute(values, axis, [(0, 1), (1, 0)])  132 us
    ppermute x62, starting transfers between devices, flip(): return lax.ppermute(values, axis, [(0, 1), (1, 0)])  44.2 us
    unnamed x229, local copies, waits for them, and re-layouts  43.9 us
    all_to_all x5, waiting for transfers between devices, team_swap(): return lax.all_to_all(blocks, axes.team, split_axis=0, concat_axis=0)  40 us
    pallas_call x2, Pallas kernels, mix_backward(): pl.pallas_call(functools.partial(mix_backward_kernel, as_rows=as_rows), g...  38.7 us
    all_to_all x5, starting transfers between devices, team_swap(): return lax.all_to_all(blocks, axes.team, split_axis=0, concat_axis=0)  26.4 us
    dot_general x8, matrix products, mm(): return jnp.dot(left, right, preferred_element_type=F32)  24.6 us
    dot_general x10, matrix products, mm_nt(): lax.dot_general(left, right, (((1,), (1,)), ((), ())), preferred_element_...  22.7 us
  transfers between devices with their start and end apart: 74, of which 30 were waited for; matrix products, arithmetic and copies ran while one was open for 28% of the time, Pallas kernels for 12%

profile of v5, /device:TPU:0, one launch (start us, length us, event | category | flops | bytes accessed | tf_op | source)
XLA Modules:
  0.0 516.1 jit_solution(9932893361083304945)
XLA Ops:
  12.4 6.5 %all-to-all-start = ((bf16[8,3,48,384]{3,2,1,0:T(8,128)(2,1)}), bf16[8,3,48,384]{3,2,1,0:T(8,128)(2,1)S(1)}, u32[]{:S(2)}, u32[]{:S(2)}) async-start(bf16[8,3,48,384]{3,2,1,0:T(8,128)(2,1)} %split_in.2), calls=%async_computation | async-start | bytes 1769472 | tf_op jit(solution)/shard_map/all_to_all | solution.py:901
  20.5 21.4 %all-to-all-done = bf16[8,3,48,384]{3,2,1,0:T(8,128)(2,1)S(1)} async-done(((bf16[8,3,48,384]{3,2,1,0:T(8,128)(2,1)}), bf16[8,3,48,384]{3,2,1,0:T(8,128)(2,1)S(1)}, u32[]{:S(2)}, u32[]{:S(2)}) %all-to-all-start) | async-done | bytes 884768 | tf_op jit(solution)/shard_map/all_to_all | solution.py:901
  49.0 17.0 %collective-permute-done.3 = bf16[128,1536]{1,0:T(8,128)(2,1)} collective-permute-done((bf16[128,1536]{1,0:T(8,128)(2,1)}, bf16[128,1536]{1,0:T(8,128)(2,1)}, u32[]{:S(2)}, u32[]{:S(2)}) %collective-permute-start.3) | collective-permute-done | bytes 393248 | tf_op jit(solution)/shard_map/ppermute | solution.py:493
  90.0 7.3 %convolution_convert_fusion.4 = bf16[768,1152]{1,0:T(8,128)(2,1)} fusion(bf16[768,1536]{1,0:T(8,128)(2,1)} %copy-done.49, bf16[1536,1152]{1,0:T(8,128)(2,1)} %get-tuple-element.167), kind=kOutput, calls=%fused_computation.5 | convolution fusion | flops 2718793728 | bytes 7667712 | tf_op jit(solution)/shard_map/dot_general | solution.py:28
  103.5 5.1 all-to-all-start.1
  110.9 7.0 %mix_forward.2 = (bf16[1024,384]{1,0:T(8,128)(2,1)S(1)}, bf16[1024,384]{1,0:T(8,128)(2,1)S(1)}, f32[4,128,384]{2,1,0:T(8,128)S(1)}) custom-call(s32[3]{0:T(128)S(1)} %pad_add_fusion.place_ref, bf16[1024,1152]{1,0:T(8,128)(2,1)S(1)} %pad_maximum_fusion.2.proj_ref.before_ref, f32[8,640]{1,0:T(8,128)S(1)} %get-tuple-element.316.conv_ref, ...), custom_call_target="tpu_custom_call" | custom-call | flops 7077888000 | bytes 6144000 | tf_op jit(solution)/shard_map/mix_forward/pallas_call | solution.py:206
  122.8 8.9 %all-to-all-done.1 = bf16[8,3,48,384]{3,2,1,0:T(8,128)(2,1)S(1)} async-done(((bf16[8,3,48,384]{3,2,1,0:T(8,128)(2,1)}), bf16[8,3,48,384]{3,2,1,0:T(8,128)(2,1)S(1)}, u32[]{:S(2)}, u32[]{:S(2)}) %all-to-all-start.1) | async-done | bytes 884768 | tf_op jit(solution)/shard_map/all_to_all | solution.py:901
  149.0 9.6 %collective-permute-done.16 = bf16[128,1664]{1,0:T(8,128)(2,1)S(1)} collective-permute-done((bf16[128,1664]{1,0:T(8,128)(2,1)}, bf16[128,1664]{1,0:T(8,128)(2,1)S(1)}, u32[]{:S(2)}, u32[]{:S(2)}) %collective-permute-start.16) | collective-permute-done | bytes 426016 | tf_op jit(solution)/shard_map/ppermute | solution.py:493
  164.3 15.9 %collective-permute-done.20 = bf16[128,1664]{1,0:T(8,128)(2,1)S(1)} collective-permute-done((bf16[128,1664]{1,0:T(8,128)(2,1)S(1)}, bf16[128,1664]{1,0:T(8,128)(2,1)S(1)}, u32[]{:S(2)}, u32[]{:S(2)}) %collective-permute-start.20) | collective-permute-done | bytes 426016 | tf_op jit(solution)/shard_map/ppermute | solution.py:493
  192.2 13.0 %collective-permute-done.24 = bf16[128,1536]{1,0:T(8,128)(2,1)} collective-permute-done((bf16[128,1536]{1,0:T(8,128)(2,1)}, bf16[128,1536]{1,0:T(8,128)(2,1)}, u32[]{:S(2)}, u32[]{:S(2)}) %collective-permute-start.24) | collective-permute-done | bytes 393248 | tf_op jit(solution)/shard_map/ppermute | solution.py:493
  207.0 4.0 join_in.3
  214.4 4.3 convolution_convert_fusion.3
  220.8 3.5 convolution_convert_fusion.9
  225.5 8.5 %mix_forward.3 = (bf16[1024,384]{1,0:T(8,128)(2,1)S(1)}, bf16[1024,384]{1,0:T(8,128)(2,1)S(1)}, f32[4,128,384]{2,1,0:T(8,128)S(1)}, f32[8,1024]{1,0:T(8,128)S(1)}) custom-call(s32[3]{0:T(128)S(1)} %pad_add_fusion.place_ref, bf16[1024,1152]{1,0:T(8,128)(2,1)S(1)} %pad_maximum_fusion.3.proj_ref.before_ref, f32[8,640]{1,0:T(8,128)S(1)} %get-tuple-element.315.conv_ref, ...), custom_call_target="tpu_custom_call" | custom-call | flops 7077888000 | bytes 6144000 | tf_op jit(solution)/shard_map/mix_forward/pallas_call | solution.py:206
  242.4 5.0 convolution_convert_fusion.1
  250.1 19.5 %mix_backward.2 = (bf16[1024,1152]{1,0:T(8,128)(2,1)S(1)}, f32[8,640]{1,0:T(8,128)S(1)}, f32[8,128]{1,0:T(8,128)S(1)}, f32[8,384]{1,0:T(8,128)S(1)}, bf16[1024,384]{1,0:T(8,128)(2,1)S(1)}) custom-call(s32[3]{0:T(128)S(1)} %pad_add_fusion.place_ref, bf16[1024,1152]{1,0:T(8,128)(2,1)} %copy-done.6, bf16[1024,1152]{1,0:T(8,128)(2,1)} %copy-done.6, ...), custom_call_target="tpu_custom_call" | custom-call | flops 15728640000 | bytes 9216000 | tf_op jit(solution)/shard_map/mix_backward/pallas_call | solution.py:429
  274.9 3.6 convolution_convert_fusion.15
  283.8 9.5 %collective-permute-done.39 = bf16[128,1536]{1,0:T(8,128)(2,1)} collective-permute-done((bf16[128,1536]{1,0:T(8,128)(2,1)S(1)}, bf16[128,1536]{1,0:T(8,128)(2,1)}, u32[]{:S(2)}, u32[]{:S(2)}) %collective-permute-start.39) | collective-permute-done | bytes 393248 | tf_op jit(solution)/shard_map/ppermute | solution.py:493
  297.0 8.7 %convolution_convert_fusion.grad_ref = bf16[1536,1152]{1,0:T(8,128)(2,1)} fusion(bf16[1024,1152]{1,0:T(8,128)(2,1)} %copy-done.24, bf16[256,1536]{1,0:T(8,128)(2,1)} %copy-done.72, bf16[768,1536]{1,0:T(8,128)(2,1)} %copy-done.77), kind=kOutput, calls=%fused_computation | convolution fusion | flops 3631939584 | bytes 9043968 | tf_op jit(solution)/shard_map/dot_general | solution.py:36
  308.2 6.3 %collective-permute-done.43.far_ref = bf16[128,1536]{1,0:T(8,128)(2,1)S(1)} collective-permute-done((bf16[128,1536]{1,0:T(8,128)(2,1)S(1)}, bf16[128,1536]{1,0:T(8,128)(2,1)S(1)}, u32[]{:S(2)}, u32[]{:S(2)}) %collective-permute-start.43) | collective-permute-done | bytes 393248 | tf_op jit(solution)/shard_map/ppermute | solution.py:493
  327.1 4.2 fusion.14
  331.3 15.3 %collective-permute-done.45 = bf16[128,1664]{1,0:T(8,128)(2,1)} collective-permute-done((bf16[128,1664]{1,0:T(8,128)(2,1)}, bf16[128,1664]{1,0:T(8,128)(2,1)}, u32[]{:S(2)}, u32[]{:S(2)}) %collective-permute-start.45) | collective-permute-done | bytes 426016 | tf_op jit(solution)/shard_map/ppermute | solution.py:493
  355.1 4.2 collective-permute-done.47
  365.7 4.4 all-to-all-start.2
  372.5 19.2 %mix_backward.3 = (bf16[1024,1152]{1,0:T(8,128)(2,1)}, f32[8,640]{1,0:T(8,128)S(1)}, f32[8,128]{1,0:T(8,128)S(1)}, f32[8,384]{1,0:T(8,128)S(1)}, bf16[1024,384]{...) custom-call(s32[3]{0:T(128)S(1)} %pad_add_fusion.place_ref, bf16[1024,1152]{1,0:T(8,128)(2,1)} %copy-done.5, ...), custom_call_target="tpu_custom_call" | custom-call | flops 15728640000 | bytes 9216000 | tf_op jit(solution)/shard_map/mix_backward/pallas_call | solution.py:429
  393.2 3.9 convolution_convert_fusion.8.grad_ref
  411.3 3.5 convolution_convert_fusion.13
  422.0 9.4 %collective-permute-done.56 = bf16[16,48,384]{2,1,0:T(8,128)(2,1)} collective-permute-done((bf16[16,48,384]{2,1,0:T(8,128)(2,1)}, bf16[16,48,384]{2,1,0:T(8,128)(2,1)}, u32[]{:S(2)}, u32[]{:S(2)}) %collective-permute-start.56) | collective-permute-done | bytes 589856 | tf_op jit(solution)/shard_map/ppermute | solution.py:493
  450.2 11.3 %collective-permute-done.59 = bf16[128,1536]{1,0:T(8,128)(2,1)} collective-permute-done((bf16[128,1536]{1,0:T(8,128)(2,1)}, bf16[128,1536]{1,0:T(8,128)(2,1)}, u32[]{:S(2)}, u32[]{:S(2)}) %collective-permute-start.59) | collective-permute-done | bytes 393248 | tf_op jit(solution)/shard_map/ppermute | solution.py:493
  472.1 3.9 collective-permute-done.63
  481.0 7.1 %all-to-all-start.4 = ((bf16[8,2,48,384]{3,2,1,0:T(8,128)(2,1)}), bf16[8,2,48,384]{3,2,1,0:T(8,128)(2,1)S(1)}, u32[]{:S(2)}, u32[]{:S(2)}) async-start(bf16[8,2,48,384]{3,2,1,0:T(8,128)(2,1)} %bitcast.273), calls=%async_computation.5 | async-start | bytes 1179648 | tf_op jit(solution)/shard_map/all_to_all | solution.py:901
  495.4 9.4 %all-to-all-done.4.refs_1_ = bf16[8,2,48,384]{3,2,1,0:T(8,128)(2,1)S(1)} async-done(((bf16[8,2,48,384]{3,2,1,0:T(8,128)(2,1)}), bf16[8,2,48,384]{3,2,1,0:T(8,128)(2,1)S(1)}, u32[]{:S(2)}, u32[]{:S(2)}) %all-to-all-start.4) | async-done | bytes 589856 | tf_op jit(solution)/shard_map/all_to_all | solution.py:901
  (549 shorter events, 220.1 us)
Async XLA Ops:
  12.4 29.5 %all-to-all-start = ((bf16[8,3,48,384]{3,2,1,0:T(8,128)(2,1)}), bf16[8,3,48,384]{3,2,1,0:T(8,128)(2,1)S(1)}, u32[]{:S(2)}, u32[]{:S(2)}) async-start(bf16[8,3,48,384]{3,2,1,0:T(8,128)(2,1)} %split_in.2), calls=%async_computation | async-start | bytes 1769472 | tf_op jit(solution)/shard_map/all_to_all | solution.py:901
  18.9 63.5 %all-gather.3.cloned.1.call-start = ((), (), s32[]{:S(2)}) async-start(), calls=%async_computation.8 | async-start | bytes 1474560 | tf_op jit(solution)/shard_map/all_gather | solution.py:915
  42.0 24.4 %collective-permute-start = (bf16[24,48,384]{2,1,0:T(8,128)(2,1)S(1)}, bf16[24,48,384]{2,1,0:T(8,128)(2,1)S(1)}, u32[]{:S(2)}, u32[]{:S(2)}) collective-permute-start(bf16[24,48,384]{2,1,0:T(8,128)(2,1)S(1)} %bitcast.252), channel_id=1, source_target_pairs={{0,1},{1,0},{2,3},{3,2},{4,5},{5,4},{6,7},{7,6},{8,9},{9,8},{10,11... | collective-permute-start | bytes 2654216 | tf_op jit(solution)/shard_map/ppermute | solution.py:493
  43.5 25.7 %collective-permute-start.1 = (bf16[24,48,384]{2,1,0:T(8,128)(2,1)S(1)}, bf16[24,48,384]{2,1,0:T(8,128)(2,1)S(1)}, u32[]{:S(2)}, u32[]{:S(2)}) collective-permute-start(bf16[24,48,384]{2,1,0:T(8,128)(2,1)S(1)} %bitcast.253), channel_id=1, source_target_pairs={{0,2},{2,0},{1,3},{3,1},{4,6},{6,4},{5,7},{7,5},{8,10},{10,8},{9,1... | collective-permute-start | bytes 2654216 | tf_op jit(solution)/shard_map/ppermute | solution.py:493
  46.1 19.9 %collective-permute-start.3 = (bf16[128,1536]{1,0:T(8,128)(2,1)}, bf16[128,1536]{1,0:T(8,128)(2,1)}, u32[]{:S(2)}, u32[]{:S(2)}) collective-permute-start(bf16[128,1536]{1,0:T(8,128)(2,1)} %fusion.35), channel_id=1, source_target_pairs={{0,16},{16,0},{1,17},{17,1},{2,18},{18,2},{3,19},{19,3},{4,20},{20... | collective-permute-start | bytes 1179656 | tf_op jit(solution)/shard_map/ppermute | solution.py:493
  46.2 20.2 %collective-permute-start.4 = (bf16[128,1536]{1,0:T(8,128)(2,1)}, bf16[128,1536]{1,0:T(8,128)(2,1)}, u32[]{:S(2)}, u32[]{:S(2)}) collective-permute-start(bf16[128,1536]{1,0:T(8,128)(2,1)} %fusion.35), channel_id=1, source_target_pairs={{0,8},{8,0},{1,9},{9,1},{2,10},{10,2},{3,11},{11,3},{4,12},{12,4},... | collective-permute-start | bytes 1179656 | tf_op jit(solution)/shard_map/ppermute | solution.py:493
  76.6 21.9 %collective-permute-start.11 = (bf16[128,1536]{1,0:T(8,128)(2,1)S(1)}, bf16[128,1536]{1,0:T(8,128)(2,1)}, u32[]{:S(2)}, u32[]{:S(2)}) collective-permute-start(bf16[128,1536]{1,0:T(8,128)(2,1)S(1)} %bitcast.258), channel_id=1, source_target_pairs={{0,4},{4,0},{1,5},{5,1},{2,6},{6,2},{3,7},{7,3},{8,12},{12,8},{9,1... | collective-permute-start | bytes 1179656 | tf_op jit(solution)/shard_map/ppermute | solution.py:493
  78.1 20.8 %collective-permute-start.12 = (bf16[128,1536]{1,0:T(8,128)(2,1)S(1)}, bf16[128,1536]{1,0:T(8,128)(2,1)}, u32[]{:S(2)}, u32[]{:S(2)}) collective-permute-start(bf16[128,1536]{1,0:T(8,128)(2,1)S(1)} %bitcast.259), channel_id=1, source_target_pairs={{0,16},{16,0},{1,17},{17,1},{2,18},{18,2},{3,19},{19,3},{4,20},{20... | collective-permute-start | bytes 1179656 | tf_op jit(solution)/shard_map/ppermute | solution.py:493
  98.8 37.0 %collective-permute-start.28 = (bf16[128,1536]{1,0:T(8,128)(2,1)}, bf16[128,1536]{1,0:T(8,128)(2,1)}, u32[]{:S(2)}, u32[]{:S(2)}) collective-permute-start(bf16[128,1536]{1,0:T(8,128)(2,1)} %collective-permute-done.12), channel_id=1, source_target_pairs={{0,4},{4,0},{1,5},{5,1},{2,6},{6,2},{3,7},{7,3},{8,12},{12,8},{9,1... | collective-permute-start | bytes 1179656 | tf_op jit(solution)/shard_map/ppermute | solution.py:493
  99.1 23.7 %collective-permute-start.14 = (bf16[128,1536]{1,0:T(8,128)(2,1)}, bf16[128,1536]{1,0:T(8,128)(2,1)}, u32[]{:S(2)}, u32[]{:S(2)}) collective-permute-start(bf16[128,1536]{1,0:T(8,128)(2,1)} %collective-permute-done.12), channel_id=1, source_target_pairs={{0,8},{8,0},{1,9},{9,1},{2,10},{10,2},{3,11},{11,3},{4,12},{12,4},... | collective-permute-start | bytes 1179656 | tf_op jit(solution)/shard_map/ppermute | solution.py:493
  103.5 28.1 %all-to-all-start.1 = ((bf16[8,3,48,384]{3,2,1,0:T(8,128)(2,1)}), bf16[8,3,48,384]{3,2,1,0:T(8,128)(2,1)S(1)}, u32[]{:S(2)}, u32[]{:S(2)}) async-start(bf16[8,3,48,384]{3,2,1,0:T(8,128)(2,1)} %split_in.3), calls=%async_computation.1 | async-start | bytes 1769472 | tf_op jit(solution)/shard_map/all_to_all | solution.py:901
  108.6 78.5 %all-gather.5.cloned.1.call-start = ((), (), s32[]{:S(2)}) async-start(), calls=%async_computation.9 | async-start | bytes 1474560 | tf_op jit(solution)/shard_map/all_gather | solution.py:915
  137.6 25.3 %collective-permute-start.21 = (bf16[24,48,384]{2,1,0:T(8,128)(2,1)S(1)}, bf16[24,48,384]{2,1,0:T(8,128)(2,1)}, u32[]{:S(2)}, u32[]{:S(2)}) collective-permute-start(bf16[24,48,384]{2,1,0:T(8,128)(2,1)S(1)} %bitcast.255), channel_id=1, source_target_pairs={{0,1},{1,0},{2,3},{3,2},{4,5},{5,4},{6,7},{7,6},{8,9},{9,8},{10,11... | collective-permute-start | bytes 2654216 | tf_op jit(solution)/shard_map/ppermute | solution.py:493
  139.4 24.9 %collective-permute-start.22 = (bf16[24,48,384]{2,1,0:T(8,128)(2,1)S(1)}, bf16[24,48,384]{2,1,0:T(8,128)(2,1)}, u32[]{:S(2)}, u32[]{:S(2)}) collective-permute-start(bf16[24,48,384]{2,1,0:T(8,128)(2,1)S(1)} %bitcast.256), channel_id=1, source_target_pairs={{0,2},{2,0},{1,3},{3,1},{4,6},{6,4},{5,7},{7,5},{8,10},{10,8},{9,1... | collective-permute-start | bytes 2654216 | tf_op jit(solution)/shard_map/ppermute | solution.py:493
  145.8 147.5 %reduce-scatter.6.cloned.1.call-start = ((), (), s32[]{:S(2)}) async-start(), calls=%async_computation.10 | async-start | bytes 3538944 | tf_op jit(solution)/shard_map/reduce_scatter | solution.py:1010
  158.7 21.5 %collective-permute-start.20 = (bf16[128,1664]{1,0:T(8,128)(2,1)S(1)}, bf16[128,1664]{1,0:T(8,128)(2,1)S(1)}, u32[]{:S(2)}, u32[]{:S(2)}) collective-permute-start(bf16[128,1664]{1,0:T(8,128)(2,1)S(1)} %fusion.31), channel_id=1, source_target_pairs={{0,16},{16,0},{1,17},{17,1},{2,18},{18,2},{3,19},{19,3},{4,20},{20... | collective-permute-start | bytes 1277960 | tf_op jit(solution)/shard_map/ppermute | solution.py:493
  158.9 21.3 %collective-permute-start.19 = (bf16[128,1664]{1,0:T(8,128)(2,1)S(1)}, bf16[128,1664]{1,0:T(8,128)(2,1)S(1)}, u32[]{:S(2)}, u32[]{:S(2)}) collective-permute-start(bf16[128,1664]{1,0:T(8,128)(2,1)S(1)} %slice_bitcast_fusion.4), channel_id=1, source_target_pairs={{0,8},{8,0},{1,9},{9,1},{2,10},{10,2},{3,11},{11,3},{4,12},{12,4},... | collective-permute-start | bytes 1277960 | tf_op jit(solution)/shard_map/ppermute | solution.py:493
  180.2 25.1 %collective-permute-start.26 = (bf16[24,48,384]{2,1,0:T(8,128)(2,1)}, bf16[24,48,384]{2,1,0:T(8,128)(2,1)}, u32[]{:S(2)}, u32[]{:S(2)}) collective-permute-start(bf16[24,48,384]{2,1,0:T(8,128)(2,1)} %collective-permute-done.21.refs_1_), channel_id=1, source_target_pairs={{0,2},{2,0},{1,3},{3,1},{4,6},{6,4},{5,7},{7,5},{8,10},{10,8},{9,1... | collective-permute-start | bytes 2654216 | tf_op jit(solution)/shard_map/ppermute | solution.py:493
  184.8 20.3 %collective-permute-start.24 = (bf16[128,1536]{1,0:T(8,128)(2,1)}, bf16[128,1536]{1,0:T(8,128)(2,1)}, u32[]{:S(2)}, u32[]{:S(2)}) collective-permute-start(bf16[128,1536]{1,0:T(8,128)(2,1)} %multiply_convert_fusion), channel_id=1, source_target_pairs={{0,16},{16,0},{1,17},{17,1},{2,18},{18,2},{3,19},{19,3},{4,20},{20... | collective-permute-start | bytes 1179656 | tf_op jit(solution)/shard_map/ppermute | solution.py:493
  185.4 20.0 %collective-permute-start.25 = (bf16[128,1536]{1,0:T(8,128)(2,1)}, bf16[128,1536]{1,0:T(8,128)(2,1)}, u32[]{:S(2)}, u32[]{:S(2)}) collective-permute-start(bf16[128,1536]{1,0:T(8,128)(2,1)} %multiply_convert_fusion), channel_id=1, source_target_pairs={{0,8},{8,0},{1,9},{9,1},{2,10},{10,2},{3,11},{11,3},{4,12},{12,4},... | collective-permute-start | bytes 1179656 | tf_op jit(solution)/shard_map/ppermute | solution.py:493
  247.4 118.3 %reduce-scatter.10.cloned.1.call-start = ((), (), s32[]{:S(2)}) async-start(), calls=%async_computation.12 | async-start | bytes 4423680
  294.4 20.0 %collective-permute-start.43 = (bf16[128,1536]{1,0:T(8,128)(2,1)S(1)}, bf16[128,1536]{1,0:T(8,128)(2,1)S(1)}, u32[]{:S(2)}, u32[]{:S(2)}) collective-permute-start(bf16[128,1536]{1,0:T(8,128)(2,1)S(1)} %fusion.43), channel_id=1, source_target_pairs={{0,16},{16,0},{1,17},{17,1},{2,18},{18,2},{3,19},{19,3},{4,20},{20... | collective-permute-start | bytes 1179656 | tf_op jit(solution)/shard_map/ppermute | solution.py:493
  318.0 170.0 %reduce-scatter.8.cloned.1.call-start = ((), (), s32[]{:S(2)}) async-start(), calls=%async_computation.11 | async-start | bytes 1474560 | tf_op jit(solution)/shard_map/reduce_scatter | solution.py:1079
  324.5 22.1 %collective-permute-start.45 = (bf16[128,1664]{1,0:T(8,128)(2,1)}, bf16[128,1664]{1,0:T(8,128)(2,1)}, u32[]{:S(2)}, u32[]{:S(2)}) collective-permute-start(bf16[128,1664]{1,0:T(8,128)(2,1)} %get-tuple-element.236), channel_id=1, source_target_pairs={{0,16},{16,0},{1,17},{17,1},{2,18},{18,2},{3,19},{19,3},{4,20},{20... | collective-permute-start | bytes 1277960 | tf_op jit(solution)/shard_map/ppermute | solution.py:493
  324.5 22.3 %collective-permute-start.46 = (bf16[128,1664]{1,0:T(8,128)(2,1)}, bf16[128,1664]{1,0:T(8,128)(2,1)}, u32[]{:S(2)}, u32[]{:S(2)}) collective-permute-start(bf16[128,1664]{1,0:T(8,128)(2,1)} %get-tuple-element.236), channel_id=1, source_target_pairs={{0,8},{8,0},{1,9},{9,1},{2,10},{10,2},{3,11},{11,3},{4,12},{12,4},... | collective-permute-start | bytes 1277960 | tf_op jit(solution)/shard_map/ppermute | solution.py:493
  365.7 27.4 %all-to-all-start.2 = ((bf16[8,3,48,384]{3,2,1,0:T(8,128)(2,1)}), bf16[8,3,48,384]{3,2,1,0:T(8,128)(2,1)}, u32[]{:S(2)}, u32[]{:S(2)}) async-start(bf16[8,3,48,384]{3,2,1,0:T(8,128)(2,1)} %bitcast.279), calls=%async_computation.3 | async-start | bytes 1769472 | tf_op jit(solution)/shard_map/all_to_all | solution.py:901
  402.4 19.7 %collective-permute-start.55 = (bf16[16,48,384]{2,1,0:T(8,128)(2,1)}, bf16[16,48,384]{2,1,0:T(8,128)(2,1)}, u32[]{:S(2)}, u32[]{:S(2)}) collective-permute-start(bf16[16,48,384]{2,1,0:T(8,128)(2,1)} %get-tuple-element.264), channel_id=1, source_target_pairs={{0,1},{1,0},{2,3},{3,2},{4,5},{5,4},{6,7},{7,6},{8,9},{9,8},{10,11... | collective-permute-start | bytes 1769480 | tf_op jit(solution)/shard_map/ppermute | solution.py:493
  403.3 28.1 %collective-permute-start.56 = (bf16[16,48,384]{2,1,0:T(8,128)(2,1)}, bf16[16,48,384]{2,1,0:T(8,128)(2,1)}, u32[]{:S(2)}, u32[]{:S(2)}) collective-permute-start(bf16[16,48,384]{2,1,0:T(8,128)(2,1)} %get-tuple-element.265), channel_id=1, source_target_pairs={{0,2},{2,0},{1,3},{3,1},{4,6},{6,4},{5,7},{7,5},{8,10},{10,8},{9,1... | collective-permute-start | bytes 1769480 | tf_op jit(solution)/shard_map/ppermute | solution.py:493
  404.7 26.7 %collective-permute-start.57 = (bf16[16,48,384]{2,1,0:T(8,128)(2,1)S(1)}, bf16[16,48,384]{2,1,0:T(8,128)(2,1)}, u32[]{:S(2)}, u32[]{:S(2)}) collective-permute-start(bf16[16,48,384]{2,1,0:T(8,128)(2,1)S(1)} %get-tuple-element.266), channel_id=1, source_target_pairs={{0,3},{1,2},{2,1},{3,0},{4,7},{5,6},{6,5},{7,4},{8,11},{9,10},{10,... | collective-permute-start | bytes 1769480 | tf_op jit(solution)/shard_map/ppermute | solution.py:497
  440.1 21.4 %collective-permute-start.59 = (bf16[128,1536]{1,0:T(8,128)(2,1)}, bf16[128,1536]{1,0:T(8,128)(2,1)}, u32[]{:S(2)}, u32[]{:S(2)}) collective-permute-start(bf16[128,1536]{1,0:T(8,128)(2,1)} %fusion.40), channel_id=1, source_target_pairs={{0,16},{16,0},{1,17},{17,1},{2,18},{18,2},{3,19},{19,3},{4,20},{20... | collective-permute-start | bytes 1179656 | tf_op jit(solution)/shard_map/ppermute | solution.py:493
  446.7 25.5 %all-to-all-start.3 = ((bf16[8,1,48,384]{3,2,1,0:T(8,128)(2,1)}), bf16[8,1,48,384]{3,2,1,0:T(8,128)(2,1)S(1)}, u32[]{:S(2)}, u32[]{:S(2)}) async-start(bf16[8,1,48,384]{3,2,1,0:T(8,128)(2,1)} %get-tuple-element.309), calls=%async_computation.4 | async-start | bytes 589824 | tf_op jit(solution)/shard_map/all_to_all | solution.py:901
  481.0 23.8 %all-to-all-start.4 = ((bf16[8,2,48,384]{3,2,1,0:T(8,128)(2,1)}), bf16[8,2,48,384]{3,2,1,0:T(8,128)(2,1)S(1)}, u32[]{:S(2)}, u32[]{:S(2)}) async-start(bf16[8,2,48,384]{3,2,1,0:T(8,128)(2,1)} %bitcast.273), calls=%async_computation.5 | async-start | bytes 1179648 | tf_op jit(solution)/shard_map/all_to_all | solution.py:901
  (145 other events, 1244.8 us)
Sparse Core Ops, SparseCore 0:
  46.0 28.1 all-gather.2
  145.9 28.8 all-gather.4
  247.5 38.0 reduce-scatter.5
  318.1 46.4 reduce-scatter.9
  367.9 28.5 reduce-scatter.7

commit v6 on v5

--- a/solution.py
+++ b/solution.py
@@ -831,7 +831,7 @@
 
 def core_sum(values, rows):
     both = values.reshape(-1, 2, rows, values.shape[-1])
-    return add_low(both[:, 0], flip(both[:, 1], "c"))
+    return both[:, 0] + flip(both[:, 1].astype(BF16), "c").astype(F32)
 
 
 def scatter_corner(axes, rows_of, rows):
@@ -839,7 +839,7 @@
     if len(axes.links) != 2:
         return (core_sum(rows_of(0, team * rows, ()), rows),)
     corner = core_sum(rows_of(6 * rows, 8 * rows, ()), rows)[0]
-    hop = flip(corner, axes.links[1])
+    hop = flip(corner.astype(BF16), axes.links[1])
     sides = core_sum(rows_of(2 * rows, 6 * rows, corner), rows)
     return hop, sides, core_sum(rows_of(0, 2 * rows, corner), rows)[0]
 
@@ -853,7 +853,7 @@
         return (whole[0],)
     far, near = axes.links
     hop, sides, own = parts
-    return own, flip(sides[0], near), flip(add_low(sides[1], hop), far)
+    return own, flip(sides[0].astype(BF16), near), flip(add_low(sides[1], hop), far)
 
 
 def add_all(parts):
@@ -955,7 +955,7 @@
     head_rows = jnp.pad(head, ((0, 0), (0, 6), (0, LANES - heads)))
     head = jnp.pad(head.transpose(0, 2, 1), ((0, 0), (0, 8 - heads), (0, LANES - 2)))
 
-    blocks = in_blocks(1, last)
+    blocks = in_blocks(1, hops)
     gated_0, y_0, enter_0 = mix_forward(place, proj_0, conv[0], head_rows[0], skip[0])
     cot_hops, cot = gather_corner(axes, cot)
     (gated_0, y_0, enter_0), blocks, cot_hops = together((gated_0, y_0, enter_0), blocks, cot_hops)
@@ -966,7 +966,7 @@
         cut = after(gated_0, others)[begin:end]
         squares = jnp.sum(jnp.square(cut.astype(F32)), axis=1, keepdims=True)
         squares = jnp.broadcast_to(squares, (end - begin, LANES))
-        return jnp.concatenate([mm(cut, weight_out_0), squares], axis=1).astype(BF16)
+        return jnp.concatenate([mm(cut, weight_out_0), squares], axis=1)
 
     got = together(*scatter_corner(axes, branch_rows, rows))
     got = scatter_sides(axes, got)
@@ -1041,6 +1041,12 @@
         more = -spare.shape[1] % 16 if depth % 16 == 0 else 0
         return jnp.pad(spare, ((0, 0), (0, more), (0, 0))).astype(BF16)
 
+    def head_sums(g_head, g_skip):
+        skips = jnp.sum(g_skip[0].reshape(heads, HD), 1)
+        return jnp.stack([g_head[:heads, 0], g_head[:heads, 1], skips])
+
+    head_1 = head_sums(g_head, g_skip)
+
     def in_gradient(normed, g_proj, beside, quick):
         spare = None if beside is None else spare_rows(*beside)
         g_in = mm_tn(normed, g_proj).astype(BF16)
@@ -1054,7 +1060,7 @@
 
     def weighed_rows(g_proj, weight_in):
         def make(begin, end, others):
-            return mm_nt(after(g_proj, others)[begin:end], weight_in).astype(BF16)
+            return mm_nt(after(g_proj, others)[begin:end], weight_in)
 
         return make
 
@@ -1095,6 +1101,7 @@
     owned_1 = owned_1[:, :1], owned_1[:, 1:]
     got = jnp.concatenate([piece[:, :model] for piece in after(pieces, g_proj)], axis=0)
     beside = g_conv, g_head, g_skip
+    head_grad = lax.psum(jnp.stack([head_sums(g_head, g_skip), head_1]), axes.copies)
     g_out = mm_tn(gated_0, got).astype(BF16)
     if paired:
         gates = in_gradient(normed, g_gate, None, True)
@@ -1106,12 +1113,11 @@
         weighed = scatter_sides(axes, weighed)
         rests = in_gradient(normed, after(g_rest, gate_parts), beside, True)
         corner = sum_corner(axes, rests)
-        weighed, corner = together(weighed, corner)
         gates = add_low(gates[0], *gate_parts)
         g_out_0 = gates[team:].reshape(-1, model // wide, depth, wide)
         g_out_0 = g_out_0.transpose(0, 2, 1, 3).reshape(-1, model)
         gates = owned(gates[:team])
-        sides, gates = together(sum_sides(axes, rests, corner), gates)
+        sides = sum_sides(axes, rests, corner)
         rests = owned(add_low(rests[0], *sides))
     else:
         weighed = scatter_sides(axes, weighed)
@@ -1132,7 +1138,6 @@
         spare[:, at * taps : (at + 1) * taps, : end - start] for at, (start, end) in enumerate(cuts)
     ]
     conv_grad = jnp.concatenate(conv_grad, axis=2)
-    head_grad = spare[:, len(cuts) * taps : len(cuts) * taps + 3, :heads]
     return (
         out[None],
         grad[None],

time: 524 us -> 511 us (0.975)
  waiting for transfers between devices: 172 us -> 149 us
  blocking collectives: 0 us -> 10.3 us
    ppermute x62, waiting for transfers between devices: 132 us -> 115 us  [flip(): return lax.ppermute(values, axis, [(0, 1), (1, 0)])]
    psum x0 -> x1, blocking collectives: none -> 10.3 us  [local(): lax.psum(jnp.stack([head_sums(g_head, g_skip), head_1]), axes.copies)]
    convert_element_type x0 -> x12, local copies, waits for them, and re-layouts: none -> 7.44 us  [the longest x9 5.42 us: core_sum(): return both[:, 0] + flip(both[:, 1].astype(BF16), 'c').astype(F32)]
    all_to_all x5, waiting for transfers between devices: 40 us -> 32.6 us  [team_swap(): return lax.all_to_all(blocks, axes.team, split_axis=0, concat_axis=0)]
    add x0 -> x3, other arithmetic: none -> 6.33 us  [core_sum(): return both[:, 0] + flip(both[:, 1].astype(BF16), 'c').astype(F32)]
    unnamed x229 -> x205, local copies, waits for them, and re-layouts: 43.9 us -> 45.7 us
  transfers between devices with their start and end apart: 74 -> 74, of which waited for: 30 -> 26; matrix products, arithmetic and copies ran while one was open for 28% -> 28% of each run, Pallas kernels for 12% -> 12%
where the time goes in v6:
time: 511 us; the launch traced here: 505 us
  waiting for transfers between devices  149 us (29%)
  starting transfers between devices  74.6 us (15%)
  Pallas kernels  72.4 us (14%)
  local copies, waits for them, and re-layouts  69.3 us (14%)
  matrix products  66.5 us (13%)
  other arithmetic  47.1 us (9%)
  between operations  15.8 us (3%)
  blocking collectives  10.3 us (2%)
    ppermute x62, waiting for transfers between devices, flip(): return lax.ppermute(values, axis, [(0, 1), (1, 0)])  115 us
    unnamed x205, local copies, waits for them, and re-layouts  45.7 us
    ppermute x62, starting transfers between devices, flip(): return lax.ppermute(values, axis, [(0, 1), (1, 0)])  45.3 us
    pallas_call x2, Pallas kernels, mix_backward(): pl.pallas_call(functools.partial(mix_backward_kernel, as_rows=as_rows), g...  38.8 us
    all_to_all x5, waiting for transfers between devices, team_swap(): return lax.all_to_all(blocks, axes.team, split_axis=0, concat_axis=0)  32.6 us
    all_to_all x5, starting transfers between devices, team_swap(): return lax.all_to_all(blocks, axes.team, split_axis=0, concat_axis=0)  24.9 us
    dot_general x8, matrix products, mm(): return jnp.dot(left, right, preferred_element_type=F32)  23.4 us
    dot_general x10, matrix products, mm_nt(): lax.dot_general(left, right, (((1,), (1,)), ((), ())), preferred_element_...  22 us
  transfers between devices with their start and end apart: 74, of which 26 were waited for; matrix products, arithmetic and copies ran while one was open for 28% of the time, Pallas kernels for 12%

profile of v6, /device:TPU:0, one launch (start us, length us, event | category | flops | bytes accessed | tf_op | source)
XLA Modules:
  0.0 505.1 jit_solution(7934016410850494396)
XLA Ops:
  11.9 6.5 %all-to-all-start = ((bf16[8,3,48,384]{3,2,1,0:T(8,128)(2,1)}), bf16[8,3,48,384]{3,2,1,0:T(8,128)(2,1)S(1)}, u32[]{:S(2)}, u32[]{:S(2)}) async-start(bf16[8,3,48,384]{3,2,1,0:T(8,128)(2,1)} %split_in.2), calls=%async_computation | async-start | bytes 1769472 | tf_op jit(solution)/shard_map/all_to_all | solution.py:901
  19.5 21.9 %all-to-all-done = bf16[8,3,48,384]{3,2,1,0:T(8,128)(2,1)S(1)} async-done(((bf16[8,3,48,384]{3,2,1,0:T(8,128)(2,1)}), bf16[8,3,48,384]{3,2,1,0:T(8,128)(2,1)S(1)}, u32[]{:S(2)}, u32[]{:S(2)}) %all-to-all-start) | async-done | bytes 884768 | tf_op jit(solution)/shard_map/all_to_all | solution.py:901
  49.4 17.0 %collective-permute-done.3 = bf16[128,1536]{1,0:T(8,128)(2,1)} collective-permute-done((bf16[128,1536]{1,0:T(8,128)(2,1)}, bf16[128,1536]{1,0:T(8,128)(2,1)}, u32[]{:S(2)}, u32[]{:S(2)}) %collective-permute-start.3) | collective-permute-done | bytes 393248 | tf_op jit(solution)/shard_map/ppermute | solution.py:493
  80.0 3.7 collective-permute-done.7.refs_3_
  90.2 4.7 all-to-all-start.1
  95.5 6.1 %convolution_convert_fusion.4 = bf16[768,1152]{1,0:T(8,128)(2,1)S(1)} fusion(bf16[768,1536]{1,0:T(8,128)(2,1)} %copy-done.45, bf16[1536,1152]{1,0:T(8,128)(2,1)} %get-tuple-element.159), kind=kOutput, calls=%fused_computation.6 | convolution fusion | flops 2718793728 | bytes 7667712 | tf_op jit(solution)/shard_map/dot_general | solution.py:28
  106.5 7.0 %mix_forward.2 = (bf16[1024,384]{1,0:T(8,128)(2,1)S(1)}, bf16[1024,384]{1,0:T(8,128)(2,1)S(1)}, f32[4,128,384]{2,1,0:T(8,128)S(1)}) custom-call(s32[3]{0:T(128)S(1)} %pad_add_fusion.place_ref, bf16[1024,1152]{1,0:T(8,128)(2,1)S(1)} %pad_maximum_fusion.3.proj_ref.before_ref, f32[8,640]{1,0:T(8,128)S(1)} %get-tuple-element.297.conv_ref, ...), custom_call_target="tpu_custom_call" | custom-call | flops 7077888000 | bytes 6144000 | tf_op jit(solution)/shard_map/mix_forward/pallas_call | solution.py:206
  117.3 3.6 collective-permute-done.14
  142.6 8.9 %collective-permute-done.16 = bf16[128,1664]{1,0:T(8,128)(2,1)S(1)} collective-permute-done((bf16[128,1664]{1,0:T(8,128)(2,1)}, bf16[128,1664]{1,0:T(8,128)(2,1)S(1)}, u32[]{:S(2)}, u32[]{:S(2)}) %collective-permute-start.16) | collective-permute-done | bytes 426016 | tf_op jit(solution)/shard_map/ppermute | solution.py:493
  155.9 17.2 %collective-permute-done.20 = bf16[128,1664]{1,0:T(8,128)(2,1)S(1)} collective-permute-done((bf16[128,1664]{1,0:T(8,128)(2,1)S(1)}, bf16[128,1664]{1,0:T(8,128)(2,1)S(1)}, u32[]{:S(2)}, u32[]{:S(2)}) %collective-permute-start.20) | collective-permute-done | bytes 426016 | tf_op jit(solution)/shard_map/ppermute | solution.py:493
  184.9 13.1 %collective-permute-done.24 = bf16[128,1536]{1,0:T(8,128)(2,1)} collective-permute-done((bf16[128,1536]{1,0:T(8,128)(2,1)}, bf16[128,1536]{1,0:T(8,128)(2,1)}, u32[]{:S(2)}, u32[]{:S(2)}) %collective-permute-start.24) | collective-permute-done | bytes 393248 | tf_op jit(solution)/shard_map/ppermute | solution.py:493
  199.7 3.7 join_in.3
  206.7 4.3 convolution_convert_fusion.3
  213.0 3.5 convolution_convert_fusion.6
  217.7 8.5 %mix_forward.3 = (bf16[1024,384]{1,0:T(8,128)(2,1)S(1)}, bf16[1024,384]{1,0:T(8,128)(2,1)S(1)}, f32[4,128,384]{2,1,0:T(8,128)S(1)}, f32[8,1024]{1,0:T(8,128)S(1)}) custom-call(s32[3]{0:T(128)S(1)} %pad_add_fusion.place_ref, bf16[1024,1152]{1,0:T(8,128)(2,1)S(1)} %pad_maximum_fusion.4.proj_ref.before_ref, f32[8,640]{1,0:T(8,128)S(1)} %get-tuple-element.296.conv_ref, ...), custom_call_target="tpu_custom_call" | custom-call | flops 7077888000 | bytes 6144000 | tf_op jit(solution)/shard_map/mix_forward/pallas_call | solution.py:206
  234.5 4.9 convolution_convert_fusion.1
  241.8 19.6 %mix_backward.2 = (bf16[1024,1152]{1,0:T(8,128)(2,1)S(1)}, f32[8,640]{1,0:T(8,128)S(1)}, f32[8,128]{1,0:T(8,128)S(1)}, f32[8,384]{1,0:T(8,128)S(1)}, bf16[1024,384]{1,0:T(8,128)(2,1)S(1)}) custom-call(s32[3]{0:T(128)S(1)} %pad_add_fusion.place_ref, bf16[1024,1152]{1,0:T(8,128)(2,1)} %copy-done.4, bf16[1024,1152]{1,0:T(8,128)(2,1)} %copy-done.4, ...), custom_call_target="tpu_custom_call" | custom-call | flops 15728640000 | bytes 9216000 | tf_op jit(solution)/shard_map/mix_backward/pallas_call | solution.py:429
  265.8 3.6 fusion.62
  275.9 9.5 %collective-permute-done.39 = bf16[128,1536]{1,0:T(8,128)(2,1)} collective-permute-done((bf16[128,1536]{1,0:T(8,128)(2,1)S(1)}, bf16[128,1536]{1,0:T(8,128)(2,1)}, u32[]{:S(2)}, u32[]{:S(2)}) %collective-permute-start.39) | collective-permute-done | bytes 393248 | tf_op jit(solution)/shard_map/ppermute | solution.py:493
  290.6 8.7 %convolution_convert_fusion.grad_ref = bf16[1536,1152]{1,0:T(8,128)(2,1)} fusion(bf16[1024,1152]{1,0:T(8,128)(2,1)} %copy-done.20, bf16[256,1536]{1,0:T(8,128)(2,1)} %copy-done.71, bf16[768,1536]{1,0:T(8,128)(2,1)} %copy-done.72), kind=kOutput, calls=%fused_computation | convolution fusion | flops 3631939584 | bytes 9043968 | tf_op jit(solution)/shard_map/dot_general | solution.py:36
  301.7 6.5 %collective-permute-done.43.far_ref = bf16[128,1536]{1,0:T(8,128)(2,1)S(1)} collective-permute-done((bf16[128,1536]{1,0:T(8,128)(2,1)S(1)}, bf16[128,1536]{1,0:T(8,128)(2,1)S(1)}, u32[]{:S(2)}, u32[]{:S(2)}) %collective-permute-start.43) | collective-permute-done | bytes 393248 | tf_op jit(solution)/shard_map/ppermute | solution.py:493
  320.5 4.2 fusion.14
  324.7 15.2 %collective-permute-done.45 = bf16[128,1664]{1,0:T(8,128)(2,1)S(1)} collective-permute-done((bf16[128,1664]{1,0:T(8,128)(2,1)}, bf16[128,1664]{1,0:T(8,128)(2,1)S(1)}, u32[]{:S(2)}, u32[]{:S(2)}) %collective-permute-start.45) | collective-permute-done | bytes 426016 | tf_op jit(solution)/shard_map/ppermute | solution.py:493
  358.9 4.6 all-to-all-start.2
  364.7 19.2 %mix_backward.3 = (bf16[1024,1152]{1,0:T(8,128)(2,1)}, f32[8,640]{1,0:T(8,128)S(1)}, f32[8,128]{1,0:T(8,128)S(1)}, f32[8,384]{1,0:T(8,128)S(1)}, bf16[1024,384]{...) custom-call(s32[3]{0:T(128)S(1)} %pad_add_fusion.place_ref, bf16[1024,1152]{1,0:T(8,128)(2,1)} %copy-done.3, ...), custom_call_target="tpu_custom_call" | custom-call | flops 15728640000 | bytes 9216000 | tf_op jit(solution)/shard_map/mix_backward/pallas_call | solution.py:429
  386.7 3.9 convolution_convert_fusion.5.grad_ref
  406.4 3.5 fusion.60
  417.2 10.3 %psum.7 = f32[2,3,6]{2,1,0:T(4,128)S(1)} all-reduce(f32[2,3,6]{2,1,0:T(4,128)S(1)} %pad_maximum_fusion.17), channel_id=1, replica_groups=mesh['a'=2,'b0'=2,'c'=2,'p0'=2,'q'=2] {'p0','q'}, use_global_device_ids=true, to_apply=%region_10.11 | all-reduce | flops 36 | bytes 288 | tf_op jit(solution)/shard_map/psum | solution.py:1104
  446.9 4.3 all-to-all-start.3
  463.6 5.6 %collective-permute-done.61 = bf16[16,48,384]{2,1,0:T(8,128)(2,1)S(1)} collective-permute-done((bf16[16,48,384]{2,1,0:T(8,128)(2,1)S(1)}, bf16[16,48,384]{2,1,0:T(8,128)(2,1)S(1)}, u32[]{:S(2)}, u32[]{:S(2)}) %collective-permute-start.61) | collective-permute-done | bytes 589856 | tf_op jit(solution)/shard_map/ppermute | solution.py:493
  472.7 4.9 all-to-all-start.4
  485.3 9.1 %all-to-all-done.4.refs_1_ = bf16[8,2,48,384]{3,2,1,0:T(8,128)(2,1)S(1)} async-done(((bf16[8,2,48,384]{3,2,1,0:T(8,128)(2,1)}), bf16[8,2,48,384]{3,2,1,0:T(8,128)(2,1)S(1)}, u32[]{:S(2)}, u32[]{:S(2)}) %all-to-all-start.4) | async-done | bytes 589856 | tf_op jit(solution)/shard_map/all_to_all | solution.py:901
  (532 shorter events, 222.0 us)
Async XLA Ops:
  11.9 29.5 %all-to-all-start = ((bf16[8,3,48,384]{3,2,1,0:T(8,128)(2,1)}), bf16[8,3,48,384]{3,2,1,0:T(8,128)(2,1)S(1)}, u32[]{:S(2)}, u32[]{:S(2)}) async-start(bf16[8,3,48,384]{3,2,1,0:T(8,128)(2,1)} %split_in.2), calls=%async_computation | async-start | bytes 1769472 | tf_op jit(solution)/shard_map/all_to_all | solution.py:901
  18.4 61.7 %all-gather.3.cloned.1.call-start = ((), (), s32[]{:S(2)}) async-start(), calls=%async_computation.8 | async-start | bytes 1474560 | tf_op jit(solution)/shard_map/all_gather | solution.py:915
  41.5 25.3 %collective-permute-start = (bf16[24,48,384]{2,1,0:T(8,128)(2,1)S(1)}, bf16[24,48,384]{2,1,0:T(8,128)(2,1)S(1)}, u32[]{:S(2)}, u32[]{:S(2)}) collective-permute-start(bf16[24,48,384]{2,1,0:T(8,128)(2,1)S(1)} %bitcast.250), channel_id=1, source_target_pairs={{0,1},{1,0},{2,3},{3,2},{4,5},{5,4},{6,7},{7,6},{8,9},{9,8},{10,11... | collective-permute-start | bytes 2654216 | tf_op jit(solution)/shard_map/ppermute | solution.py:493
  42.9 24.1 %collective-permute-start.1 = (bf16[24,48,384]{2,1,0:T(8,128)(2,1)S(1)}, bf16[24,48,384]{2,1,0:T(8,128)(2,1)S(1)}, u32[]{:S(2)}, u32[]{:S(2)}) collective-permute-start(bf16[24,48,384]{2,1,0:T(8,128)(2,1)S(1)} %bitcast.251), channel_id=1, source_target_pairs={{0,2},{2,0},{1,3},{3,1},{4,6},{6,4},{5,7},{7,5},{8,10},{10,8},{9,1... | collective-permute-start | bytes 2654216 | tf_op jit(solution)/shard_map/ppermute | solution.py:493
  46.6 20.2 %collective-permute-start.4 = (bf16[128,1536]{1,0:T(8,128)(2,1)}, bf16[128,1536]{1,0:T(8,128)(2,1)}, u32[]{:S(2)}, u32[]{:S(2)}) collective-permute-start(bf16[128,1536]{1,0:T(8,128)(2,1)} %fusion.37), channel_id=1, source_target_pairs={{0,8},{8,0},{1,9},{9,1},{2,10},{10,2},{3,11},{11,3},{4,12},{12,4},... | collective-permute-start | bytes 1179656 | tf_op jit(solution)/shard_map/ppermute | solution.py:493
  74.2 28.5 %collective-permute-start.11 = (bf16[128,1536]{1,0:T(8,128)(2,1)S(1)}, bf16[128,1536]{1,0:T(8,128)(2,1)}, u32[]{:S(2)}, u32[]{:S(2)}) collective-permute-start(bf16[128,1536]{1,0:T(8,128)(2,1)S(1)} %bitcast.253), channel_id=1, source_target_pairs={{0,4},{4,0},{1,5},{5,1},{2,6},{6,2},{3,7},{7,3},{8,12},{12,8},{9,1... | collective-permute-start | bytes 1179656 | tf_op jit(solution)/shard_map/ppermute | solution.py:493
  75.7 27.0 %collective-permute-start.12 = (bf16[128,1536]{1,0:T(8,128)(2,1)S(1)}, bf16[128,1536]{1,0:T(8,128)(2,1)}, u32[]{:S(2)}, u32[]{:S(2)}) collective-permute-start(bf16[128,1536]{1,0:T(8,128)(2,1)S(1)} %bitcast.254), channel_id=1, source_target_pairs={{0,16},{16,0},{1,17},{17,1},{2,18},{18,2},{3,19},{19,3},{4,20},{20... | collective-permute-start | bytes 1179656 | tf_op jit(solution)/shard_map/ppermute | solution.py:493
  80.0 22.8 %collective-permute-start.13 = (bf16[128,1536]{1,0:T(8,128)(2,1)S(1)}, bf16[128,1536]{1,0:T(8,128)(2,1)}, u32[]{:S(2)}, u32[]{:S(2)}) collective-permute-start(bf16[128,1536]{1,0:T(8,128)(2,1)S(1)} %bitcast.255), channel_id=1, source_target_pairs={{0,8},{8,0},{1,9},{9,1},{2,10},{10,2},{3,11},{11,3},{4,12},{12,4},... | collective-permute-start | bytes 1179656 | tf_op jit(solution)/shard_map/ppermute | solution.py:493
  90.2 30.7 %all-to-all-start.1 = ((bf16[8,3,48,384]{3,2,1,0:T(8,128)(2,1)}), bf16[8,3,48,384]{3,2,1,0:T(8,128)(2,1)S(1)}, u32[]{:S(2)}, u32[]{:S(2)}) async-start(bf16[8,3,48,384]{3,2,1,0:T(8,128)(2,1)} %split_in.3), calls=%async_computation.1 | async-start | bytes 1769472 | tf_op jit(solution)/shard_map/all_to_all | solution.py:901
  94.9 84.9 %all-gather.5.cloned.1.call-start = ((), (), s32[]{:S(2)}) async-start(), calls=%async_computation.9 | async-start | bytes 1474560 | tf_op jit(solution)/shard_map/all_gather | solution.py:915
  102.7 22.4 %collective-permute-start.28 = (bf16[128,1536]{1,0:T(8,128)(2,1)}, bf16[128,1536]{1,0:T(8,128)(2,1)S(1)}, u32[]{:S(2)}, u32[]{:S(2)}) collective-permute-start(bf16[128,1536]{1,0:T(8,128)(2,1)} %collective-permute-done.12), channel_id=1, source_target_pairs={{0,4},{4,0},{1,5},{5,1},{2,6},{6,2},{3,7},{7,3},{8,12},{12,8},{9,1... | collective-permute-start | bytes 1179656 | tf_op jit(solution)/shard_map/ppermute | solution.py:493
  125.9 30.0 %collective-permute-start.21 = (bf16[24,48,384]{2,1,0:T(8,128)(2,1)S(1)}, bf16[24,48,384]{2,1,0:T(8,128)(2,1)}, u32[]{:S(2)}, u32[]{:S(2)}) collective-permute-start(bf16[24,48,384]{2,1,0:T(8,128)(2,1)S(1)} %bitcast.247), channel_id=1, source_target_pairs={{0,1},{1,0},{2,3},{3,2},{4,5},{5,4},{6,7},{7,6},{8,9},{9,8},{10,11... | collective-permute-start | bytes 2654216 | tf_op jit(solution)/shard_map/ppermute | solution.py:493
  127.4 28.5 %collective-permute-start.22 = (bf16[24,48,384]{2,1,0:T(8,128)(2,1)S(1)}, bf16[24,48,384]{2,1,0:T(8,128)(2,1)S(1)}, u32[]{:S(2)}, u32[]{:S(2)}) collective-permute-start(bf16[24,48,384]{2,1,0:T(8,128)(2,1)S(1)} %bitcast.248), channel_id=1, source_target_pairs={{0,2},{2,0},{1,3},{3,1},{4,6},{6,4},{5,7},{7,5},{8,10},{10,8},{9,1... | collective-permute-start | bytes 2654216 | tf_op jit(solution)/shard_map/ppermute | solution.py:493
  138.8 146.6 %reduce-scatter.6.cloned.1.call-start = ((), (), s32[]{:S(2)}) async-start(), calls=%async_computation.10 | async-start | bytes 3538944 | tf_op jit(solution)/shard_map/reduce_scatter | solution.py:1010
  151.7 21.5 %collective-permute-start.20 = (bf16[128,1664]{1,0:T(8,128)(2,1)S(1)}, bf16[128,1664]{1,0:T(8,128)(2,1)S(1)}, u32[]{:S(2)}, u32[]{:S(2)}) collective-permute-start(bf16[128,1664]{1,0:T(8,128)(2,1)S(1)} %fusion.35), channel_id=1, source_target_pairs={{0,16},{16,0},{1,17},{17,1},{2,18},{18,2},{3,19},{19,3},{4,20},{20... | collective-permute-start | bytes 1277960 | tf_op jit(solution)/shard_map/ppermute | solution.py:493
  154.2 20.2 %collective-permute-start.19 = (bf16[128,1664]{1,0:T(8,128)(2,1)S(1)}, bf16[128,1664]{1,0:T(8,128)(2,1)S(1)}, u32[]{:S(2)}, u32[]{:S(2)}) collective-permute-start(bf16[128,1664]{1,0:T(8,128)(2,1)S(1)} %fusion.66), channel_id=1, source_target_pairs={{0,8},{8,0},{1,9},{9,1},{2,10},{10,2},{3,11},{11,3},{4,12},{12,4},... | collective-permute-start | bytes 1277960 | tf_op jit(solution)/shard_map/ppermute | solution.py:493
  174.4 23.7 %collective-permute-start.26 = (bf16[24,48,384]{2,1,0:T(8,128)(2,1)}, bf16[24,48,384]{2,1,0:T(8,128)(2,1)}, u32[]{:S(2)}, u32[]{:S(2)}) collective-permute-start(bf16[24,48,384]{2,1,0:T(8,128)(2,1)} %collective-permute-done.21.refs_1_), channel_id=1, source_target_pairs={{0,2},{2,0},{1,3},{3,1},{4,6},{6,4},{5,7},{7,5},{8,10},{10,8},{9,1... | collective-permute-start | bytes 2654216 | tf_op jit(solution)/shard_map/ppermute | solution.py:493
  176.9 21.2 %collective-permute-start.24 = (bf16[128,1536]{1,0:T(8,128)(2,1)}, bf16[128,1536]{1,0:T(8,128)(2,1)}, u32[]{:S(2)}, u32[]{:S(2)}) collective-permute-start(bf16[128,1536]{1,0:T(8,128)(2,1)} %multiply_convert_fusion), channel_id=1, source_target_pairs={{0,16},{16,0},{1,17},{17,1},{2,18},{18,2},{3,19},{19,3},{4,20},{20... | collective-permute-start | bytes 1179656 | tf_op jit(solution)/shard_map/ppermute | solution.py:493
  177.2 20.9 %collective-permute-start.25 = (bf16[128,1536]{1,0:T(8,128)(2,1)}, bf16[128,1536]{1,0:T(8,128)(2,1)}, u32[]{:S(2)}, u32[]{:S(2)}) collective-permute-start(bf16[128,1536]{1,0:T(8,128)(2,1)} %multiply_convert_fusion), channel_id=1, source_target_pairs={{0,8},{8,0},{1,9},{9,1},{2,10},{10,2},{3,11},{11,3},{4,12},{12,4},... | collective-permute-start | bytes 1179656 | tf_op jit(solution)/shard_map/ppermute | solution.py:493
  239.5 119.4 %reduce-scatter.10.cloned.1.call-start = ((), (), s32[]{:S(2)}) async-start(), calls=%async_computation.12 | async-start | bytes 4423680
  287.9 20.3 %collective-permute-start.43 = (bf16[128,1536]{1,0:T(8,128)(2,1)S(1)}, bf16[128,1536]{1,0:T(8,128)(2,1)S(1)}, u32[]{:S(2)}, u32[]{:S(2)}) collective-permute-start(bf16[128,1536]{1,0:T(8,128)(2,1)S(1)} %fusion.53), channel_id=1, source_target_pairs={{0,16},{16,0},{1,17},{17,1},{2,18},{18,2},{3,19},{19,3},{4,20},{20... | collective-permute-start | bytes 1179656 | tf_op jit(solution)/shard_map/ppermute | solution.py:493
  311.8 165.9 %reduce-scatter.8.cloned.1.call-start = ((), (), s32[]{:S(2)}) async-start(), calls=%async_computation.11 | async-start | bytes 1474560 | tf_op jit(solution)/shard_map/reduce_scatter | solution.py:1085
  317.9 21.9 %collective-permute-start.45 = (bf16[128,1664]{1,0:T(8,128)(2,1)}, bf16[128,1664]{1,0:T(8,128)(2,1)S(1)}, u32[]{:S(2)}, u32[]{:S(2)}) collective-permute-start(bf16[128,1664]{1,0:T(8,128)(2,1)} %get-tuple-element.228), channel_id=1, source_target_pairs={{0,16},{16,0},{1,17},{17,1},{2,18},{18,2},{3,19},{19,3},{4,20},{20... | collective-permute-start | bytes 1277960 | tf_op jit(solution)/shard_map/ppermute | solution.py:493
  317.9 22.2 %collective-permute-start.46 = (bf16[128,1664]{1,0:T(8,128)(2,1)}, bf16[128,1664]{1,0:T(8,128)(2,1)}, u32[]{:S(2)}, u32[]{:S(2)}) collective-permute-start(bf16[128,1664]{1,0:T(8,128)(2,1)} %get-tuple-element.228), channel_id=1, source_target_pairs={{0,8},{8,0},{1,9},{9,1},{2,10},{10,2},{3,11},{11,3},{4,12},{12,4},... | collective-permute-start | bytes 1277960 | tf_op jit(solution)/shard_map/ppermute | solution.py:493
  358.9 27.8 %all-to-all-start.2 = ((bf16[8,3,48,384]{3,2,1,0:T(8,128)(2,1)}), bf16[8,3,48,384]{3,2,1,0:T(8,128)(2,1)}, u32[]{:S(2)}, u32[]{:S(2)}) async-start(bf16[8,3,48,384]{3,2,1,0:T(8,128)(2,1)} %bitcast.271), calls=%async_computation.3 | async-start | bytes 1769472 | tf_op jit(solution)/shard_map/all_to_all | solution.py:901
  395.4 39.1 %collective-permute-start.55 = (bf16[16,48,384]{2,1,0:T(8,128)(2,1)}, bf16[16,48,384]{2,1,0:T(8,128)(2,1)S(1)}, u32[]{:S(2)}, u32[]{:S(2)}) collective-permute-start(bf16[16,48,384]{2,1,0:T(8,128)(2,1)} %get-tuple-element.256), channel_id=1, source_target_pairs={{0,1},{1,0},{2,3},{3,2},{4,5},{5,4},{6,7},{7,6},{8,9},{9,8},{10,11... | collective-permute-start | bytes 1769480 | tf_op jit(solution)/shard_map/ppermute | solution.py:493
  396.8 37.7 %collective-permute-start.56 = (bf16[16,48,384]{2,1,0:T(8,128)(2,1)S(1)}, bf16[16,48,384]{2,1,0:T(8,128)(2,1)}, u32[]{:S(2)}, u32[]{:S(2)}) collective-permute-start(bf16[16,48,384]{2,1,0:T(8,128)(2,1)S(1)} %get-tuple-element.257), channel_id=1, source_target_pairs={{0,2},{2,0},{1,3},{3,1},{4,6},{6,4},{5,7},{7,5},{8,10},{10,8},{9,1... | collective-permute-start | bytes 1769480 | tf_op jit(solution)/shard_map/ppermute | solution.py:493
  397.4 37.1 %collective-permute-start.57 = (bf16[16,48,384]{2,1,0:T(8,128)(2,1)S(1)}, bf16[16,48,384]{2,1,0:T(8,128)(2,1)}, u32[]{:S(2)}, u32[]{:S(2)}) collective-permute-start(bf16[16,48,384]{2,1,0:T(8,128)(2,1)S(1)} %get-tuple-element.258), channel_id=1, source_target_pairs={{0,3},{1,2},{2,1},{3,0},{4,7},{5,6},{6,5},{7,4},{8,11},{9,10},{10,... | collective-permute-start | bytes 1769480 | tf_op jit(solution)/shard_map/ppermute | solution.py:497
  446.9 25.9 %all-to-all-start.3 = ((bf16[8,1,48,384]{3,2,1,0:T(8,128)(2,1)}), bf16[8,1,48,384]{3,2,1,0:T(8,128)(2,1)S(1)}, u32[]{:S(2)}, u32[]{:S(2)}) async-start(bf16[8,1,48,384]{3,2,1,0:T(8,128)(2,1)} %get-tuple-element.293), calls=%async_computation.4 | async-start | bytes 589824 | tf_op jit(solution)/shard_map/all_to_all | solution.py:901
  458.4 22.3 %collective-permute-start.58 = (bf16[128,1536]{1,0:T(8,128)(2,1)}, bf16[128,1536]{1,0:T(8,128)(2,1)}, u32[]{:S(2)}, u32[]{:S(2)}) collective-permute-start(bf16[128,1536]{1,0:T(8,128)(2,1)} %fusion.73), channel_id=1, source_target_pairs={{0,8},{8,0},{1,9},{9,1},{2,10},{10,2},{3,11},{11,3},{4,12},{12,4},... | collective-permute-start | bytes 1179656 | tf_op jit(solution)/shard_map/ppermute | solution.py:493
  461.2 20.0 %collective-permute-start.59 = (bf16[128,1536]{1,0:T(8,128)(2,1)}, bf16[128,1536]{1,0:T(8,128)(2,1)}, u32[]{:S(2)}, u32[]{:S(2)}) collective-permute-start(bf16[128,1536]{1,0:T(8,128)(2,1)} %fusion.52), channel_id=1, source_target_pairs={{0,16},{16,0},{1,17},{17,1},{2,18},{18,2},{3,19},{19,3},{4,20},{20... | collective-permute-start | bytes 1179656 | tf_op jit(solution)/shard_map/ppermute | solution.py:493
  472.7 21.6 %all-to-all-start.4 = ((bf16[8,2,48,384]{3,2,1,0:T(8,128)(2,1)}), bf16[8,2,48,384]{3,2,1,0:T(8,128)(2,1)S(1)}, u32[]{:S(2)}, u32[]{:S(2)}) async-start(bf16[8,2,48,384]{3,2,1,0:T(8,128)(2,1)} %bitcast.86), calls=%async_computation.5 | async-start | bytes 1179648 | tf_op jit(solution)/shard_map/all_to_all | solution.py:901
  (133 other events, 1087.1 us)
Sparse Core Ops, SparseCore 0:
  46.4 30.6 all-gather.2
  138.9 27.4 all-gather.4
  239.6 40.2 reduce-scatter.5
  311.9 46.9 reduce-scatter.9
  362.2 28.5 reduce-scatter.7
